TPU v7x, 512 devices: a whole 4x8x8 slice. The times are simulated.
512 devices in a mesh: section: 16 (over x, y_hi, core), dp: 32 (over z, y_lo).
Axes of the slice: x: 4, y: 8 (y_hi: 2, y_lo: 4; y = y_hi * 4 + y_lo), z: 8, core: 2. Of those that a mesh axis runs over, the one named last changes fastest.
Arguments:
- acts: bfloat16 [16, 4096, 3584], P('section', 'dp'), may hold values from -6 to 6
- norm_gain: float32 [16, 3584], P('section'), may hold values from 0.1 to 1.9
- proj: bfloat16 [16, 3584, 512], P('section', 'dp'), may hold values from -0.25 to 0.25
- out_grad: bfloat16 [16, 4096, 512], P('section', 'dp'), may hold values from -6 to 6
- owner_slot: int32 [16, 7], P('section'), may hold values from 0 to 31, as said below
- left_root: bfloat16 [16, 32, 512, 512], P('section', 'dp'), as said below
- right_root: bfloat16 [16, 32, 512, 512], P('section', 'dp'), as said below
Outputs:
- section_grad: bfloat16 [16, 4096, 3584], P('section', 'dp')
- left_gram: bfloat16 [16, 32, 512, 512], P('section', 'dp')
- right_gram: bfloat16 [16, 32, 512, 512], P('section', 'dp')
- precond: bfloat16 [16, 32, 512, 512], P('section', 'dp')
Inputs may be any that keep to these rules, and one draw needn't show every extreme that they name: `owner_slot`: in each layer the 7 values are distinct; place k belongs to index k // 1 of dp; no index of dp receives more than 1 block. `left_root`: Symmetric. `right_root`: Symmetric.
All inputs are finite; a program needn't handle non-finite values.
Results may differ from a plain program's by a relative error of at most 0.034.
Values may be sent and summed in bfloat16 or wider, within the bound.
No kernel may reach another device: no remote copies, remote signals or barrier semaphores. Data moves between devices by JAX's collectives and lax.ppermute only.
A program may use at most 128 MiB of HBM per device.

v0:
```python
import jax
import jax.numpy as jnp
from jax import lax
from jax.sharding import PartitionSpec as P

norm_eps = 1e-06


def entering(value, axis, join, neutral):
    count = lax.axis_size(axis)
    place = lax.axis_index(axis)
    ahead = count - 1 - place
    gathered = lax.all_gather(value.astype(jnp.bfloat16), axis)
    state = jnp.zeros_like(value) + jnp.asarray(neutral, value.dtype)

    def one(step, state):
        source = count - 1 - step
        return join(state, lax.dynamic_index_in_dim(gathered, source, 0, False).astype(value.dtype))

    return lax.fori_loop(0, ahead, one, state)


def add_later(earlier, later):
    return earlier + later


def body(acts, norm_gain, proj, out_grad, owner_slot, left_root, right_root):
    rows_here = acts.shape[1]
    width = acts.shape[2]
    keys_width = out_grad.shape[2]
    block = left_root.shape[2]
    places = left_root.shape[1]
    groups = lax.axis_size("dp")
    scale = (rows_here * groups) ** (-0.5)
    stream = acts[0].astype(jnp.float32)
    gain = norm_gain[0]
    radius = jnp.sqrt(jnp.mean(stream * stream, axis=1, keepdims=True) + norm_eps)
    unit = stream / radius
    normed = (unit * gain).astype(jnp.bfloat16)
    upstream = out_grad[0]
    shard_rows = proj[0]
    back = lax.dot_general(
        upstream,
        lax.all_gather(shard_rows, "dp", axis=0, tiled=True),
        (((1,), (1,)), ((), ())),
        preferred_element_type=jnp.float32,
    )
    scaled = back * gain
    inner = jnp.mean(scaled * unit, axis=1, keepdims=True)
    branch = (scaled - unit * inner) / radius
    later = entering(branch, "section", add_later, jnp.zeros_like(branch))
    section_grad = (branch + later).astype(jnp.bfloat16)[None]
    block_cols = keys_width // block
    count = width // block * block_cols
    partial_value = (
        lax.dot_general(
            normed, upstream, (((0,), (0,)), ((), ())), preferred_element_type=jnp.float32
        )
        * scale
    )
    owners = owner_slot[0]
    my_slots = lax.axis_index("dp") * places + jnp.arange(places, dtype=jnp.int32)
    match = owners[None, :] == my_slots[:, None]
    present = jnp.any(match, axis=1)
    which = jnp.sum(jnp.where(match, jnp.arange(count, dtype=jnp.int32)[None, :], 0), axis=1)
    row_low = which // block_cols * block
    col_low = which % block_cols * block
    offsets = jnp.arange(block, dtype=jnp.int32)
    summed = lax.psum(partial_value.astype(jnp.bfloat16), "dp")
    length = summed.shape[0]
    index = row_low[:, None] + offsets[None, :]
    inside = (index >= 0) & (index < length) & present[:, None]
    taken = summed[jnp.clip(index, 0, length - 1)]

    def cut_columns(rows, low):
        return rows

    chosen = jax.vmap(cut_columns)(taken, col_low).astype(jnp.float32)
    picked = jnp.where(inside[:, :, None], chosen, 0.0)
    grads = picked.astype(jnp.bfloat16)
    gram_left = jnp.einsum("cij,ckj->cik", grads, grads, preferred_element_type=jnp.float32) / block
    gram_right = (
        jnp.einsum("cji,cjk->cik", grads, grads, preferred_element_type=jnp.float32) / block
    )
    left_gram = gram_left.astype(jnp.bfloat16)[None]
    right_gram = gram_right.astype(jnp.bfloat16)[None]
    middle = jnp.einsum(
        "cij,cjk->cik", left_root[0], grads, preferred_element_type=jnp.float32
    ).astype(jnp.bfloat16)
    precond = jnp.einsum(
        "cij,cjk->cik", middle, right_root[0], preferred_element_type=jnp.float32
    ).astype(jnp.bfloat16)[None]
    return (section_grad, left_gram, right_gram, precond)


def solution(mesh):
    in_specs = (
        P("section", "dp", None),
        P("section", None),
        P("section", "dp", None),
        P("section", "dp", None),
        P("section", None),
        P("section", "dp", None, None),
        P("section", "dp", None, None),
    )
    out_specs = (
        P("section", "dp", None),
        P("section", "dp", None, None),
        P("section", "dp", None, None),
        P("section", "dp", None, None),
    )
    return jax.shard_map(body, mesh=mesh, in_specs=in_specs, out_specs=out_specs, check_vma=False)
```

profile of v0, /device:TPU:1, one launch (start us, length us, event | category | flops | bytes accessed | tf_op | source)
XLA Modules:
  0.0 715.1 jit_solution(7785531043224473827)
XLA Ops:
  10.2 4.3 multiply_convert_fusion
  14.5 147.4 %all-gather.5.cloned.1.call-done = bf16[1,3584,512]{2,1,0:T(8,128)(2,1)} async-done(((bf16[1,112,512]{2,1,0:T(8,128)(2,1)}), bf16[1,3584,512]{2,1,0:T(8,128)(2,1)}) %all-gather.5.cloned.1.call-update) | async-done | bytes 3670032 | tf_op jit(solution)/shard_map/all_gather | solution.py:44
  161.9 3.5 multiply_reduce_fusion
  165.4 2.0 fusion.32
  170.0 331.2 %all-reduce.2.cloned.1.call-done = bf16[3584,512]{1,0:T(8,128)(2,1)} async-done(((bf16[3584,512]{1,0:T(8,128)(2,1)}), bf16[3584,512]{1,0:T(8,128)(2,1)}) %all-reduce.2.cloned.1.call-update) | async-done | bytes 3670032 | tf_op jit(solution)/shard_map/psum | solution.py:69
  501.2 4.5 gather_fusion
  508.5 1.8 fusion.10
  510.3 173.1 %all-gather.7.cloned.1.call-done = bf16[2048,3584]{1,0:T(8,128)(2,1)} async-done(((bf16[128,3584]{1,0:T(8,128)(2,1)}), bf16[2048,3584]{1,0:T(8,128)(2,1)}) %all-gather.7.cloned.1.call-update) | async-done | bytes 14680080 | tf_op jit(solution)/shard_map/all_gather | solution.py:13
  683.5 22.5 %while.12 = (s32[]{:T(128)}, f32[128,3584]{1,0:T(8,128)S(1)}, s32[]{:T(128)}, bf16[16,128,3584]{2,1,0:T(8,128)(2,1)}, s32[]{:T(128)}, /*index=5*/s32[]{:T(128)}, s32[]{:T(128)}, s32[]{:T(128)}) while((s32[]{:T(128)}, f32[128,3584]{1,0:T(8,128)S(1)}, s32[]{:T(128)}, bf16[16,128,3584]{2,1,0:T(8,128)(2,1)}, s32[]{:T(128)}, /*index=5*/s32[]{:T(128)}, ...), condition=%wide.region_3.4_spmd, body=%wide.region_2.3_spmd.sunk | while | flops 917510 | bytes 4587663 | solution.py:20
  683.5 1.6 convert_add_fusion.2
  685.1 1.6 convert_add_fusion.2
  686.7 1.6 convert_add_fusion.2
  688.3 1.6 convert_add_fusion.2
  689.9 1.6 convert_add_fusion.2
  691.5 1.6 convert_add_fusion.2
  693.1 1.6 convert_add_fusion.2
  694.8 1.6 convert_add_fusion.2
  696.4 1.6 convert_add_fusion.2
  698.0 1.6 convert_add_fusion.2
  699.6 1.6 convert_add_fusion.2
  701.2 1.6 convert_add_fusion.2
  702.8 1.6 convert_add_fusion.2
  704.4 1.6 convert_add_fusion.2
  706.0 2.6 fusion.12
  (28 shorter events, 7.9 us)
Async XLA Ops:
  7.2 501.3 %copy-start = (bf16[1,1,512,512]{3,2,1,0:T(8,128)(2,1)S(1)}, bf16[1,1,512,512]{3,2,1,0:T(8,128)(2,1)}, u32[]{:S(2)}) copy-start(bf16[1,1,512,512]{3,2,1,0:T(8,128)(2,1)} %param.15) | copy-start | bytes 1572868
  7.2 154.7 %all-gather.5.cloned.1.call-start = ((), (), s32[]{:S(2)}) async-start(), calls=%async_computation.1 | async-start | bytes 3784704 | tf_op jit(solution)/shard_map/all_gather | solution.py:44
  7.9 493.3 %all-reduce.2.cloned.1.call-start = ((), (), s32[]{:S(2)}) async-start(), calls=%async_computation | async-start | bytes 7340032 | tf_op jit(solution)/shard_map/psum | solution.py:69
  14.5 147.5 %copy-start.1 = (bf16[1,128,3584]{2,1,0:T(8,128)(2,1)S(1)}, bf16[1,128,3584]{2,1,0:T(8,128)(2,1)}, u32[]{:S(2)}) copy-start(bf16[1,128,3584]{2,1,0:T(8,128)(2,1)} %param.9) | copy-start | bytes 2752516
  14.5 147.5 %copy-start.3 = (bf16[1,128,512]{2,1,0:T(8,128)(2,1)S(1)}, bf16[1,128,512]{2,1,0:T(8,128)(2,1)}, u32[]{:S(2)}) copy-start(bf16[1,128,512]{2,1,0:T(8,128)(2,1)} %param.12) | copy-start | bytes 393220
  14.5 668.8 %all-gather.7.cloned.1.call-start = ((), (), s32[]{:S(2)}) async-start(), calls=%async_computation.2 | async-start | bytes 15597568 | tf_op jit(solution)/shard_map/all_gather | solution.py:13
  165.4 2.0 copy-start.4
  505.7 2.8 copy-start.2
Sparse Core Ops, SparseCore 0:
  10.1 151.7 all-gather.4
  164.8 336.3 all-reduce.1
  505.6 177.6 all-gather.6
where the time goes:
time: 719 us; the launch traced here: 715 us
  waiting for transfers between devices  652 us (91%)
  other arithmetic  30.9 us (4%)
  between operations  14.5 us (2%)
  matrix products  12.3 us (2%)
    psum x1, waiting for transfers between devices, body(): summed = lax.psum(partial_value.astype(jnp.bfloat16), 'dp')  331 us
    all_gather x1, waiting for transfers between devices, entering(): gathered = lax.all_gather(value.astype(jnp.bfloat16), axis)  173 us
    all_gather x1, waiting for transfers between devices, body(): lax.all_gather(shard_rows, 'dp', axis=0, tiled=True)  147 us
    add x14, other arithmetic, add_later(): return earlier + later  22.1 us
  transfers between devices with their start and end apart: 3, of which 3 were waited for; matrix products, arithmetic and copies ran while one was open for 3% of the time, Pallas kernels for 0%

commit v1 on v0

v1 whole, which is shorter than its diff:
```python
import jax
import jax.numpy as jnp
from jax import lax
from jax.sharding import Mesh, PartitionSpec as P

norm_eps = 1e-06
SEC = ("x", "yh", "c")
DP = ("z", "yl")
PAIRS = ("x", "yh")
NX, NYH, NC, NZ, NYL = 4, 2, 2, 8, 4
NPAIR = NX * NYH


def swap_cores(value):
    return lax.ppermute(value, "c", [(0, 1), (1, 0)])


def shift_z(value, by):
    return lax.ppermute(value, "z", [(i, (i + by) % NZ) for i in range(NZ)])


def gather_rows(shard):
    rows, width = shard.shape
    copies = jnp.broadcast_to(shard[None], (NYL, rows, width))
    mine = lax.all_to_all(copies, "yl", 0, 0).reshape(NYL * rows, width)
    block = NYL * rows
    half = block // 2
    z = lax.axis_index("z")
    up = down = mine
    parts = [(mine, 0, 0)]
    for step in range(1, NZ // 2):
        up = shift_z(up, 1)
        down = shift_z(down, -1)
        parts += [(up, -step, 0), (down, step, 0)]
    parts += [(shift_z(up[:half], 1), NZ // 2, 0), (shift_z(down[half:], -1), NZ // 2, half)]
    full = jnp.zeros((NZ * block, width), shard.dtype)
    for value, offset, low in parts:
        place = lax.rem(z + offset + NZ, NZ) * block + low
        full = lax.dynamic_update_slice(full, value, (place, 0))
    return full


def later_sections(branch):
    tokens, width = branch.shape
    half = tokens // 2
    core = lax.axis_index("c")
    last = core == 1
    rounded = branch.astype(jnp.bfloat16)
    own_half = jnp.where(last, branch[half:], branch[:half])
    away = jnp.where(last, rounded[:half], rounded[half:])
    other = swap_cores(away).astype(jnp.float32)
    total = (own_half + other).astype(jnp.bfloat16)
    spread = lax.all_to_all(total.reshape(NPAIR, half // NPAIR, width), PAIRS, 0, 0)
    run = jnp.zeros(spread.shape[1:], jnp.float32)
    sums = [None] * NPAIR
    for pair in range(NPAIR - 1, -1, -1):
        sums[pair] = run.astype(jnp.bfloat16)
        run = run + spread[pair].astype(jnp.float32)
    after = lax.all_to_all(jnp.stack(sums), PAIRS, 0, 0).reshape(half, width)
    after = after.astype(jnp.float32)
    give = after + jnp.where(last, own_half, 0.0)
    take = swap_cores(give.astype(jnp.bfloat16)).astype(jnp.float32)
    kept = own_half + after + jnp.where(last, 0.0, other)
    low = jnp.where(last, branch[:half] + take, kept)
    high = jnp.where(last, kept, branch[half:] + take)
    return jnp.concatenate([low, high]).astype(jnp.bfloat16)


def grad_shard(acts, shared, gain, scale):
    tokens, width = acts.shape
    keys = shared.shape[1]
    block = 512
    count = width // block
    part = block // NYL
    piece = part // NZ
    j = lax.axis_index("yl")
    z = lax.axis_index("z")
    quarters = acts.reshape(tokens, count, NYL, part).transpose(2, 0, 1, 3).reshape(NYL, tokens, count * part)
    rows = []
    for k in range(NYL):
        mine = lax.dynamic_index_in_dim(quarters, j ^ k, 0, False)
        load = jnp.concatenate([mine, shared], axis=1)
        if k:
            load = lax.ppermute(load, "yl", [(i, i ^ k) for i in range(NYL)])
        rows.append(load)
    rows = jnp.concatenate(rows)
    partial = lax.dot_general(
        rows[:, : count * part], rows[:, count * part :], (((0,), (0,)), ((), ())), preferred_element_type=jnp.float32
    )
    partial = partial.astype(jnp.bfloat16).reshape(count, NZ, piece, keys).transpose(1, 0, 2, 3)
    total = 0.0
    for k in range(NZ):
        term = lax.dynamic_index_in_dim(partial, lax.rem(z + k, NZ), 0, False)
        if k:
            term = shift_z(term, k)
        total = total + term.astype(jnp.float32)
    gains = gain.reshape(count, NYL, NZ, piece)
    gains = lax.dynamic_index_in_dim(gains, j, 1, False)
    gains = lax.dynamic_index_in_dim(gains, z, 1, False)
    return (total * (gains * scale)[:, :, None]).astype(jnp.bfloat16)


def to_owner(shard, owners):
    count, piece, keys = shard.shape
    places = jnp.arange(NZ * NYL, dtype=jnp.int32)
    match = (owners[None, :] == places[:, None]).astype(jnp.bfloat16)
    send = jnp.einsum("pb,brk->prk", match, shard, preferred_element_type=jnp.float32).astype(jnp.bfloat16)
    got = lax.all_to_all(send, DP, 0, 0)
    return got.reshape(NZ, NYL, piece, keys).transpose(1, 0, 2, 3).reshape(NZ * NYL * piece, keys)


def body(acts, norm_gain, proj, out_grad, owner_slot, left_root, right_root):
    acts, gain, upstream = acts[0], norm_gain[0], out_grad[0]
    tokens = acts.shape[0] * NZ * NYL
    stream = acts.astype(jnp.float32)
    radius = jnp.sqrt(jnp.mean(stream * stream, axis=1, keepdims=True) + norm_eps)
    weights = gather_rows(proj[0])
    shared = (upstream.astype(jnp.float32) / radius).astype(jnp.bfloat16)
    shard = grad_shard(acts, shared, gain, tokens ** (-0.5))

    back = lax.dot_general(upstream, weights, (((1,), (1,)), ((), ())), preferred_element_type=jnp.float32)
    unit = stream / radius
    scaled = back * gain
    inner = jnp.mean(scaled * unit, axis=1, keepdims=True)
    branch = (scaled - unit * inner) / radius
    section_grad = later_sections(branch)[None]

    grads = to_owner(shard, owner_slot[0])
    block = grads.shape[0]

    def dot(a, b, dims):
        return lax.dot_general(a, b, (dims, ((), ())), preferred_element_type=jnp.float32)

    left_gram = (dot(grads, grads, ((1,), (1,))) / block).astype(jnp.bfloat16)
    right_gram = (dot(grads, grads, ((0,), (0,))) / block).astype(jnp.bfloat16)
    middle = dot(left_root[0, 0], grads, ((1,), (0,))).astype(jnp.bfloat16)
    precond = dot(middle, right_root[0, 0], ((1,), (0,))).astype(jnp.bfloat16)
    return section_grad, left_gram[None, None], right_gram[None, None], precond[None, None]


def solution(mesh):
    split = Mesh(mesh.devices.reshape(NX, NYH, NC, NZ, NYL), (*SEC, *DP))
    in_specs = (
        P(SEC, DP, None),
        P(SEC, None),
        P(SEC, DP, None),
        P(SEC, DP, None),
        P(SEC, None),
        P(SEC, DP, None, None),
        P(SEC, DP, None, None),
    )
    out_specs = (
        P(SEC, DP, None),
        P(SEC, DP, None, None),
        P(SEC, DP, None, None),
        P(SEC, DP, None, None),
    )
    return jax.shard_map(body, mesh=split, in_specs=in_specs, out_specs=out_specs, check_vma=False)
```

time: 719 us -> 209 us (0.29)
  waiting for transfers between devices: 652 us -> 30.2 us
  starting transfers between devices: 0.12 us -> 111 us
  local copies, waits for them, and re-layouts: 4.69 us -> 18.8 us
  blocking collectives: 0 us -> 13.9 us
  between operations: 14.5 us -> 1.36 us
  other arithmetic: 30.9 us -> 20.1 us
    psum x1 -> x0, waiting for transfers between devices: 331 us -> none  [body(): summed = lax.psum(partial_value.astype(jnp.bfloat16), 'dp')]
    all_gather x2 -> x0, waiting for transfers between devices: 320 us -> none  [the longest x1 173 us: entering(): gathered = lax.all_gather(value.astype(jnp.bfloat16), axis)]
    ppermute x0 -> x20, starting transfers between devices: none -> 88.6 us  [the longest x15 62.1 us: shift_z(): return lax.ppermute(value, 'z', [(i, (i + by) % NZ) for i in range(NZ)])]
    all_to_all x0 -> x3, starting transfers between devices: none -> 22.5 us  [the longest x1 7.92 us: later_sections(): lax.all_to_all(total.reshape(NPAIR, half // NPAIR, width), PAIRS, 0, 0)]
    add x14 -> x0, other arithmetic: 22.1 us -> none  [add_later(): return earlier + later]
    ppermute x0 -> x20, waiting for transfers between devices: none -> 20.5 us  [the longest x15 20.5 us: shift_z(): return lax.ppermute(value, 'z', [(i, (i + by) % NZ) for i in range(NZ)])]
    all_to_all x0 -> x1, blocking collectives: none -> 13.9 us  [gather_rows(): mine = lax.all_to_all(copies, 'yl', 0, 0).reshape(NYL * rows, width)]
    all_to_all x0 -> x3, waiting for transfers between devices: none -> 9.75 us  [the longest x1 5.66 us: later_sections(): after = lax.all_to_all(jnp.stack(sums), PAIRS, 0, 0).reshape(half, width)]
  transfers between devices with their start and end apart: 3 -> 23, of which waited for: 3 -> 9; matrix products, arithmetic and copies ran while one was open for 3% -> 21% of each run, Pallas kernels for 0% -> 0%
where the time goes in v1:
time: 209 us; the launch traced here: 207 us
  starting transfers between devices  111 us (53%)
  waiting for transfers between devices  30.2 us (14%)
  other arithmetic  20.1 us (10%)
  local copies, waits for them, and re-layouts  18.8 us (9%)
  blocking collectives  13.9 us (7%)
  matrix products  11.6 us (6%)
    ppermute x15, starting transfers between devices, shift_z(): return lax.ppermute(value, 'z', [(i, (i + by) % NZ) for i in range(NZ)])  62.1 us
    ppermute x15, waiting for transfers between devices, shift_z(): return lax.ppermute(value, 'z', [(i, (i + by) % NZ) for i in range(NZ)])  20.5 us
    ppermute x2, starting transfers between devices, swap_cores(): return lax.ppermute(value, 'c', [(0, 1), (1, 0)])  17.3 us
    all_to_all x1, blocking collectives, gather_rows(): mine = lax.all_to_all(copies, 'yl', 0, 0).reshape(NYL * rows, width)  13.9 us
    ppermute x3, starting transfers between devices, grad_shard(): load = lax.ppermute(load, 'yl', [(i, i ^ k) for i in range(NYL)])  9.27 us
    unnamed x7, other arithmetic  8.32 us
    all_to_all x1, starting transfers between devices, later_sections(): lax.all_to_all(total.reshape(NPAIR, half // NPAIR, width), PAIRS, 0, 0)  7.92 us
    all_to_all x1, starting transfers between devices, later_sections(): after = lax.all_to_all(jnp.stack(sums), PAIRS, 0, 0).reshape(half, width)  7.61 us
  transfers between devices with their start and end apart: 23, of which 9 were waited for; matrix products, arithmetic and copies ran while one was open for 21% of the time, Pallas kernels for 0%

profile of v1, /device:TPU:1, one launch (start us, length us, event | category | flops | bytes accessed | tf_op | source)
XLA Modules:
  0.0 207.1 jit_solution(10845320025424984469)
XLA Ops:
  1.7 13.9 %all_to_all.20 = bf16[4,112,512]{2,1,0:T(8,128)(2,1)} all-to-all(bf16[4,112,512]{2,1,0:T(8,128)(2,1)S(1)} %broadcast_in_dim.32), channel_id=1, replica_groups=mesh['x'=4,'yh'=2,'c'=2,'z'=8,'yl'=4] {'yl'}, dimensions={0} | all-to-all | bytes 917504 | tf_op jit(solution)/shard_map/all_to_all | solution.py:25
  15.6 8.1 %collective-permute-start = (bf16[448,512]{1,0:T(8,128)(2,1)}, bf16[448,512]{1,0:T(8,128)(2,1)}, u32[]{:S(2)}, u32[]{:S(2)}) collective-permute-start(bf16[448,512]{1,0:T(8,128)(2,1)} %bitcast.1), channel_id=1, source_target_pairs={{0,4},{4,8},{8,12},{12,16},{16,20},{20,24},{24,28},{28,0},{1,5},{5... | collective-permute-start | bytes 1376264 | tf_op jit(solution)/shard_map/ppermute | solution.py:19
  23.7 8.6 %collective-permute-start.1 = (bf16[448,512]{1,0:T(8,128)(2,1)}, bf16[448,512]{1,0:T(8,128)(2,1)}, u32[]{:S(2)}, u32[]{:S(2)}) collective-permute-start(bf16[448,512]{1,0:T(8,128)(2,1)} %bitcast.1), channel_id=1, source_target_pairs={{0,28},{4,0},{8,4},{12,8},{16,12},{20,16},{24,20},{28,24},{1,29},{... | collective-permute-start | bytes 1376264 | tf_op jit(solution)/shard_map/ppermute | solution.py:19
  34.6 5.3 %collective-permute-done = bf16[448,512]{1,0:T(8,128)(2,1)} collective-permute-done((bf16[448,512]{1,0:T(8,128)(2,1)}, bf16[448,512]{1,0:T(8,128)(2,1)}, u32[]{:S(2)}, u32[]{:S(2)}) %collective-permute-start) | collective-permute-done | bytes 458784 | tf_op jit(solution)/shard_map/ppermute | solution.py:19
  41.9 4.6 %collective-permute-start.3 = (bf16[448,512]{1,0:T(8,128)(2,1)}, bf16[448,512]{1,0:T(8,128)(2,1)}, u32[]{:S(2)}, u32[]{:S(2)}) collective-permute-start(bf16[448,512]{1,0:T(8,128)(2,1)} %collective-permute-done.1), channel_id=1, source_target_pairs={{0,28},{4,0},{8,4},{12,8},{16,12},{20,16},{24,20},{28,24},{1,29},{... | collective-permute-start | bytes 1376264 | tf_op jit(solution)/shard_map/ppermute | solution.py:19
  48.4 3.2 %collective-permute-start.12 = (bf16[128,1408]{0,1:T(8,128)(2,1)}, bf16[128,1408]{0,1:T(8,128)(2,1)}, u32[]{:S(2)}, u32[]{:S(2)}) collective-permute-start(bf16[128,1408]{0,1:T(8,128)(2,1)} %get-tuple-element.26), channel_id=1, source_target_pairs={{0,3},{1,2},{2,1},{3,0},{4,7},{5,6},{6,5},{7,4},{8,11},{9,10},{10,... | collective-permute-start | bytes 1081352 | tf_op jit(solution)/shard_map/ppermute | solution.py:84
  53.6 4.1 %collective-permute-start.10 = (bf16[128,1408]{0,1:T(8,128)(2,1)}, bf16[128,1408]{0,1:T(8,128)(2,1)}, u32[]{:S(2)}, u32[]{:S(2)}) collective-permute-start(bf16[128,1408]{0,1:T(8,128)(2,1)} %get-tuple-element.24), channel_id=1, source_target_pairs={{0,1},{1,0},{2,3},{3,2},{4,5},{5,4},{6,7},{7,6},{8,9},{9,8},{10,11... | collective-permute-start | bytes 1081352 | tf_op jit(solution)/shard_map/ppermute | solution.py:84
  61.1 4.6 %collective-permute-start.5 = (bf16[448,512]{1,0:T(8,128)(2,1)}, bf16[448,512]{1,0:T(8,128)(2,1)S(1)}, u32[]{:S(2)}, u32[]{:S(2)}) collective-permute-start(bf16[448,512]{1,0:T(8,128)(2,1)} %collective-permute-done.3), channel_id=1, source_target_pairs={{0,28},{4,0},{8,4},{12,8},{16,12},{20,16},{24,20},{28,24},{1,29},{... | collective-permute-start | bytes 1376264 | tf_op jit(solution)/shard_map/ppermute | solution.py:19
  72.9 4.6 %collective-permute-start.7 = (bf16[224,512]{1,0:T(8,128)(2,1)S(1)}, bf16[224,512]{1,0:T(8,128)(2,1)S(1)}, u32[]{:S(2)}, u32[]{:S(2)}) collective-permute-start(bf16[224,512]{1,0:T(8,128)(2,1)S(1)} %slice.63), channel_id=1, source_target_pairs={{0,28},{4,0},{8,4},{12,8},{16,12},{20,16},{24,20},{28,24},{1,29},{... | collective-permute-start | bytes 688136 | tf_op jit(solution)/shard_map/ppermute | solution.py:19
  82.5 7.5 %collective-permute-start.8 = (bf16[64,3584]{1,0:T(8,128)(2,1)S(1)}, bf16[64,3584]{1,0:T(8,128)(2,1)S(1)}, u32[]{:S(2)}, u32[]{:S(2)}) collective-permute-start(bf16[64,3584]{1,0:T(8,128)(2,1)S(1)} %slice_select_fusion.1), channel_id=1, source_target_pairs={{0,32},{32,0},{1,33},{33,1},{2,34},{34,2},{3,35},{35,3},{4,36},{36... | collective-permute-start | bytes 1376264 | tf_op jit(solution)/shard_map/ppermute | solution.py:15
  90.1 2.6 %pad_maximum_fusion = bf16[512,1408]{0,1:T(8,128)(2,1)} fusion(bf16[128,1408]{0,1:T(8,128)(2,1)} %collective-permute-done.12, bf16[128,1408]{0,1:T(8,128)(2,1)} %collective-permute-done.11, bf16[128,1408]{0,1:T(8,128)(2,1)} %collective-permute-done.10, bf16[128,512]{0,1:T(8,128)(2,1)S(1)} %copy.69, bf16[128,896]{0,1:T(8,128)(2,1)} %get-tuple-element.20), kind=kLoop, calls=%fused_computation.8 | loop fusion | flops 7208960 | bytes 2883584 | tf_op jit(solution)/shard_map/concatenate | solution.py:86
  95.4 7.9 %all-to-all-start.1 = ((bf16[8,8,3584]{2,1,0:T(8,128)(2,1)}), bf16[8,8,3584]{2,1,0:T(8,128)(2,1)}, u32[]{:S(2)}, u32[]{:S(2)}) async-start(bf16[8,8,3584]{2,1,0:T(8,128)(2,1)} %get-tuple-element.6), calls=%async_computation.1 | async-start | bytes 917504 | tf_op jit(solution)/shard_map/all_to_all | solution.py:53
  105.4 5.3 %collective-permute-start.19 = (bf16[7,16,512]{2,0,1:T(8,128)(2,1)S(1)}, bf16[7,16,512]{2,0,1:T(8,128)(2,1)S(1)}, u32[]{:S(2)}, u32[]{:S(2)}) collective-permute-start(bf16[7,16,512]{2,0,1:T(8,128)(2,1)S(1)} %bitcast.114), channel_id=1, source_target_pairs={{0,28},{4,0},{8,4},{12,8},{16,12},{20,16},{24,20},{28,24},{1,29},{... | collective-permute-start | bytes 344072 | tf_op jit(solution)/shard_map/ppermute | solution.py:19
  113.5 4.3 %collective-permute-start.17 = (bf16[7,16,512]{2,0,1:T(8,128)(2,1)}, bf16[7,16,512]{2,0,1:T(8,128)(2,1)}, u32[]{:S(2)}, u32[]{:S(2)}) collective-permute-start(bf16[7,16,512]{2,0,1:T(8,128)(2,1)} %bitcast.103), channel_id=1, source_target_pairs={{0,20},{4,24},{8,28},{12,0},{16,4},{20,8},{24,12},{28,16},{1,21},{... | collective-permute-start | bytes 344072 | tf_op jit(solution)/shard_map/ppermute | solution.py:19
  118.5 4.9 %collective-permute-start.16 = (bf16[7,16,512]{2,0,1:T(8,128)(2,1)}, bf16[7,16,512]{2,0,1:T(8,128)(2,1)}, u32[]{:S(2)}, u32[]{:S(2)}) collective-permute-start(bf16[7,16,512]{2,0,1:T(8,128)(2,1)} %bitcast.104), channel_id=1, source_target_pairs={{0,16},{4,20},{8,24},{12,28},{16,0},{20,4},{24,8},{28,12},{1,17},{... | collective-permute-start | bytes 344072 | tf_op jit(solution)/shard_map/ppermute | solution.py:19
  127.7 5.5 %collective-permute-start.14 = (bf16[7,16,512]{2,0,1:T(8,128)(2,1)}, bf16[7,16,512]{2,0,1:T(8,128)(2,1)}, u32[]{:S(2)}, u32[]{:S(2)}) collective-permute-start(bf16[7,16,512]{2,0,1:T(8,128)(2,1)} %bitcast.106), channel_id=1, source_target_pairs={{0,8},{4,12},{8,16},{12,20},{16,24},{20,28},{24,0},{28,4},{1,9},{5... | collective-permute-start | bytes 344072 | tf_op jit(solution)/shard_map/ppermute | solution.py:19
  136.7 5.0 %collective-permute-done.15 = bf16[7,16,512]{2,0,1:T(8,128)(2,1)} collective-permute-done((bf16[7,16,512]{2,0,1:T(8,128)(2,1)}, bf16[7,16,512]{2,0,1:T(8,128)(2,1)}, u32[]{:S(2)}, u32[]{:S(2)}) %collective-permute-start.15) | collective-permute-done | bytes 114720 | tf_op jit(solution)/shard_map/ppermute | solution.py:19
  143.4 4.6 %collective-permute-done.13 = bf16[7,16,512]{2,0,1:T(8,128)(2,1)} collective-permute-done((bf16[7,16,512]{2,0,1:T(8,128)(2,1)}, bf16[7,16,512]{2,0,1:T(8,128)(2,1)}, u32[]{:S(2)}, u32[]{:S(2)}) %collective-permute-start.13) | collective-permute-done | bytes 114720 | tf_op jit(solution)/shard_map/ppermute | solution.py:19
  150.7 6.9 %all-to-all-start.3 = ((bf16[32,16,512]{2,1,0:T(8,128)(2,1)}), bf16[32,16,512]{2,1,0:T(8,128)(2,1)}, u32[]{:S(2)}, u32[]{:S(2)}) async-start(bf16[32,16,512]{2,1,0:T(8,128)(2,1)} %copy.82), calls=%async_computation.3 | async-start | bytes 1048576 | tf_op jit(solution)/shard_map/all_to_all | solution.py:108
  168.0 4.1 %all-to-all-done.3 = bf16[32,16,512]{2,1,0:T(8,128)(2,1)} async-done(((bf16[32,16,512]{2,1,0:T(8,128)(2,1)}), bf16[32,16,512]{2,1,0:T(8,128)(2,1)}, u32[]{:S(2)}, u32[]{:S(2)}) %all-to-all-start.3) | async-done | bytes 524320 | tf_op jit(solution)/shard_map/all_to_all | solution.py:108
  172.1 7.6 %all-to-all-start.2 = ((bf16[8,8,3584]{2,1,0:T(8,128)(2,1)}), bf16[8,8,3584]{2,1,0:T(8,128)(2,1)}, u32[]{:S(2)}, u32[]{:S(2)}) async-start(bf16[8,8,3584]{2,1,0:T(8,128)(2,1)} %broadcast_dynamic-update-slice_fusion), calls=%async_computation.2 | async-start | bytes 917504 | tf_op jit(solution)/shard_map/all_to_all | solution.py:59
  182.9 2.8 %fusion.7 = bf16[1,1,512,512]{3,2,1,0:T(8,128)(2,1)} fusion(bf16[512,512]{1,0:T(8,128)(2,1)} %bitcast.112, bf16[1,1,512,512]{3,2,1,0:T(8,128)(2,1)S(1)} %copy-done, bf16[1,1,512,512]{3,2,1,0:T(8,128)(2,1)} %param.12), kind=kOutput, calls=%fused_computation.19 | convolution fusion | flops 537395200 | bytes 2097152 | tf_op jit(solution)/shard_map/dot_general | solution.py:132
  185.7 5.7 %all-to-all-done.2 = bf16[8,8,3584]{2,1,0:T(8,128)(2,1)} async-done(((bf16[8,8,3584]{2,1,0:T(8,128)(2,1)}), bf16[8,8,3584]{2,1,0:T(8,128)(2,1)}, u32[]{:S(2)}, u32[]{:S(2)}) %all-to-all-start.2) | async-done | bytes 458784 | tf_op jit(solution)/shard_map/all_to_all | solution.py:59
  192.5 9.7 %collective-permute-start.9 = (bf16[64,3584]{1,0:T(8,128)(2,1)S(1)}, bf16[64,3584]{1,0:T(8,128)(2,1)S(1)}, u32[]{:S(2)}, u32[]{:S(2)}) collective-permute-start(bf16[64,3584]{1,0:T(8,128)(2,1)S(1)} %fusion.14), channel_id=1, source_target_pairs={{0,32},{32,0},{1,33},{33,1},{2,34},{34,2},{3,35},{35,3},{4,36},{36... | collective-permute-start | bytes 1376264 | tf_op jit(solution)/shard_map/ppermute | solution.py:15
  (100 shorter events, 64.4 us)
Async XLA Ops:
  0.6 182.2 %copy-start = (bf16[1,1,512,512]{3,2,1,0:T(8,128)(2,1)S(1)}, bf16[1,1,512,512]{3,2,1,0:T(8,128)(2,1)}, u32[]{:S(2)}) copy-start(bf16[1,1,512,512]{3,2,1,0:T(8,128)(2,1)} %param.13) | copy-start | bytes 1572868
  15.6 24.4 %collective-permute-start = (bf16[448,512]{1,0:T(8,128)(2,1)}, bf16[448,512]{1,0:T(8,128)(2,1)}, u32[]{:S(2)}, u32[]{:S(2)}) collective-permute-start(bf16[448,512]{1,0:T(8,128)(2,1)} %bitcast.1), channel_id=1, source_target_pairs={{0,4},{4,8},{8,12},{12,16},{16,20},{20,24},{24,28},{28,0},{1,5},{5... | collective-permute-start | bytes 1376264 | tf_op jit(solution)/shard_map/ppermute | solution.py:19
  23.7 18.2 %collective-permute-start.1 = (bf16[448,512]{1,0:T(8,128)(2,1)}, bf16[448,512]{1,0:T(8,128)(2,1)}, u32[]{:S(2)}, u32[]{:S(2)}) collective-permute-start(bf16[448,512]{1,0:T(8,128)(2,1)} %bitcast.1), channel_id=1, source_target_pairs={{0,28},{4,0},{8,4},{12,8},{16,12},{20,16},{24,20},{28,24},{1,29},{... | collective-permute-start | bytes 1376264 | tf_op jit(solution)/shard_map/ppermute | solution.py:19
  40.0 19.2 %collective-permute-start.2 = (bf16[448,512]{1,0:T(8,128)(2,1)}, bf16[448,512]{1,0:T(8,128)(2,1)}, u32[]{:S(2)}, u32[]{:S(2)}) collective-permute-start(bf16[448,512]{1,0:T(8,128)(2,1)} %collective-permute-done), channel_id=1, source_target_pairs={{0,4},{4,8},{8,12},{12,16},{16,20},{20,24},{24,28},{28,0},{1,5},{5... | collective-permute-start | bytes 1376264 | tf_op jit(solution)/shard_map/ppermute | solution.py:19
  41.9 19.2 %collective-permute-start.3 = (bf16[448,512]{1,0:T(8,128)(2,1)}, bf16[448,512]{1,0:T(8,128)(2,1)}, u32[]{:S(2)}, u32[]{:S(2)}) collective-permute-start(bf16[448,512]{1,0:T(8,128)(2,1)} %collective-permute-done.1), channel_id=1, source_target_pairs={{0,28},{4,0},{8,4},{12,8},{16,12},{20,16},{24,20},{28,24},{1,29},{... | collective-permute-start | bytes 1376264 | tf_op jit(solution)/shard_map/ppermute | solution.py:19
  48.4 41.7 %collective-permute-start.12 = (bf16[128,1408]{0,1:T(8,128)(2,1)}, bf16[128,1408]{0,1:T(8,128)(2,1)}, u32[]{:S(2)}, u32[]{:S(2)}) collective-permute-start(bf16[128,1408]{0,1:T(8,128)(2,1)} %get-tuple-element.26), channel_id=1, source_target_pairs={{0,3},{1,2},{2,1},{3,0},{4,7},{5,6},{6,5},{7,4},{8,11},{9,10},{10,... | collective-permute-start | bytes 1081352 | tf_op jit(solution)/shard_map/ppermute | solution.py:84
  51.6 38.4 %collective-permute-start.11 = (bf16[128,1408]{0,1:T(8,128)(2,1)}, bf16[128,1408]{0,1:T(8,128)(2,1)}, u32[]{:S(2)}, u32[]{:S(2)}) collective-permute-start(bf16[128,1408]{0,1:T(8,128)(2,1)} %get-tuple-element.25), channel_id=1, source_target_pairs={{0,2},{1,3},{2,0},{3,1},{4,6},{5,7},{6,4},{7,5},{8,10},{9,11},{10,... | collective-permute-start | bytes 1081352 | tf_op jit(solution)/shard_map/ppermute | solution.py:84
  53.6 36.5 %collective-permute-start.10 = (bf16[128,1408]{0,1:T(8,128)(2,1)}, bf16[128,1408]{0,1:T(8,128)(2,1)}, u32[]{:S(2)}, u32[]{:S(2)}) collective-permute-start(bf16[128,1408]{0,1:T(8,128)(2,1)} %get-tuple-element.24), channel_id=1, source_target_pairs={{0,1},{1,0},{2,3},{3,2},{4,5},{5,4},{6,7},{7,6},{8,9},{9,8},{10,11... | collective-permute-start | bytes 1081352 | tf_op jit(solution)/shard_map/ppermute | solution.py:84
  59.2 11.8 %collective-permute-start.4 = (bf16[448,512]{1,0:T(8,128)(2,1)}, bf16[448,512]{1,0:T(8,128)(2,1)S(1)}, u32[]{:S(2)}, u32[]{:S(2)}) collective-permute-start(bf16[448,512]{1,0:T(8,128)(2,1)} %collective-permute-done.2), channel_id=1, source_target_pairs={{0,4},{4,8},{8,12},{12,16},{16,20},{20,24},{24,28},{28,0},{1,5},{5... | collective-permute-start | bytes 1376264 | tf_op jit(solution)/shard_map/ppermute | solution.py:19
  61.1 11.8 %collective-permute-start.5 = (bf16[448,512]{1,0:T(8,128)(2,1)}, bf16[448,512]{1,0:T(8,128)(2,1)S(1)}, u32[]{:S(2)}, u32[]{:S(2)}) collective-permute-start(bf16[448,512]{1,0:T(8,128)(2,1)} %collective-permute-done.3), channel_id=1, source_target_pairs={{0,28},{4,0},{8,4},{12,8},{16,12},{20,16},{24,20},{28,24},{1,29},{... | collective-permute-start | bytes 1376264 | tf_op jit(solution)/shard_map/ppermute | solution.py:19
  71.0 8.2 %collective-permute-start.6 = (bf16[224,512]{1,0:T(8,128)(2,1)S(1)}, bf16[224,512]{1,0:T(8,128)(2,1)S(1)}, u32[]{:S(2)}, u32[]{:S(2)}) collective-permute-start(bf16[224,512]{1,0:T(8,128)(2,1)S(1)} %slice.62), channel_id=1, source_target_pairs={{0,4},{4,8},{8,12},{12,16},{16,20},{20,24},{24,28},{28,0},{1,5},{5... | collective-permute-start | bytes 688136 | tf_op jit(solution)/shard_map/ppermute | solution.py:19
  72.9 7.5 %collective-permute-start.7 = (bf16[224,512]{1,0:T(8,128)(2,1)S(1)}, bf16[224,512]{1,0:T(8,128)(2,1)S(1)}, u32[]{:S(2)}, u32[]{:S(2)}) collective-permute-start(bf16[224,512]{1,0:T(8,128)(2,1)S(1)} %slice.63), channel_id=1, source_target_pairs={{0,28},{4,0},{8,4},{12,8},{16,12},{20,16},{24,20},{28,24},{1,29},{... | collective-permute-start | bytes 688136 | tf_op jit(solution)/shard_map/ppermute | solution.py:19
  82.5 10.2 %collective-permute-start.8 = (bf16[64,3584]{1,0:T(8,128)(2,1)S(1)}, bf16[64,3584]{1,0:T(8,128)(2,1)S(1)}, u32[]{:S(2)}, u32[]{:S(2)}) collective-permute-start(bf16[64,3584]{1,0:T(8,128)(2,1)S(1)} %slice_select_fusion.1), channel_id=1, source_target_pairs={{0,32},{32,0},{1,33},{33,1},{2,34},{34,2},{3,35},{35,3},{4,36},{36... | collective-permute-start | bytes 1376264 | tf_op jit(solution)/shard_map/ppermute | solution.py:15
  95.4 55.4 %all-to-all-start.1 = ((bf16[8,8,3584]{2,1,0:T(8,128)(2,1)}), bf16[8,8,3584]{2,1,0:T(8,128)(2,1)}, u32[]{:S(2)}, u32[]{:S(2)}) async-start(bf16[8,8,3584]{2,1,0:T(8,128)(2,1)} %get-tuple-element.6), calls=%async_computation.1 | async-start | bytes 917504 | tf_op jit(solution)/shard_map/all_to_all | solution.py:53
  105.4 22.3 %collective-permute-start.19 = (bf16[7,16,512]{2,0,1:T(8,128)(2,1)S(1)}, bf16[7,16,512]{2,0,1:T(8,128)(2,1)S(1)}, u32[]{:S(2)}, u32[]{:S(2)}) collective-permute-start(bf16[7,16,512]{2,0,1:T(8,128)(2,1)S(1)} %bitcast.114), channel_id=1, source_target_pairs={{0,28},{4,0},{8,4},{12,8},{16,12},{20,16},{24,20},{28,24},{1,29},{... | collective-permute-start | bytes 344072 | tf_op jit(solution)/shard_map/ppermute | solution.py:19
  110.8 22.4 %collective-permute-start.18 = (bf16[7,16,512]{2,0,1:T(8,128)(2,1)S(1)}, bf16[7,16,512]{2,0,1:T(8,128)(2,1)}, u32[]{:S(2)}, u32[]{:S(2)}) collective-permute-start(bf16[7,16,512]{2,0,1:T(8,128)(2,1)S(1)} %bitcast.113), channel_id=1, source_target_pairs={{0,24},{4,28},{8,0},{12,4},{16,8},{20,12},{24,16},{28,20},{1,25},{... | collective-permute-start | bytes 344072 | tf_op jit(solution)/shard_map/ppermute | solution.py:19
  113.5 23.2 %collective-permute-start.17 = (bf16[7,16,512]{2,0,1:T(8,128)(2,1)}, bf16[7,16,512]{2,0,1:T(8,128)(2,1)}, u32[]{:S(2)}, u32[]{:S(2)}) collective-permute-start(bf16[7,16,512]{2,0,1:T(8,128)(2,1)} %bitcast.103), channel_id=1, source_target_pairs={{0,20},{4,24},{8,28},{12,0},{16,4},{20,8},{24,12},{28,16},{1,21},{... | collective-permute-start | bytes 344072 | tf_op jit(solution)/shard_map/ppermute | solution.py:19
  118.5 18.2 %collective-permute-start.16 = (bf16[7,16,512]{2,0,1:T(8,128)(2,1)}, bf16[7,16,512]{2,0,1:T(8,128)(2,1)}, u32[]{:S(2)}, u32[]{:S(2)}) collective-permute-start(bf16[7,16,512]{2,0,1:T(8,128)(2,1)} %bitcast.104), channel_id=1, source_target_pairs={{0,16},{4,20},{8,24},{12,28},{16,0},{20,4},{24,8},{28,12},{1,17},{... | collective-permute-start | bytes 344072 | tf_op jit(solution)/shard_map/ppermute | solution.py:19
  124.1 17.6 %collective-permute-start.15 = (bf16[7,16,512]{2,0,1:T(8,128)(2,1)}, bf16[7,16,512]{2,0,1:T(8,128)(2,1)}, u32[]{:S(2)}, u32[]{:S(2)}) collective-permute-start(bf16[7,16,512]{2,0,1:T(8,128)(2,1)} %bitcast.105), channel_id=1, source_target_pairs={{0,12},{4,16},{8,20},{12,24},{16,28},{20,0},{24,4},{28,8},{1,13},{... | collective-permute-start | bytes 344072 | tf_op jit(solution)/shard_map/ppermute | solution.py:19
  127.7 15.7 %collective-permute-start.14 = (bf16[7,16,512]{2,0,1:T(8,128)(2,1)}, bf16[7,16,512]{2,0,1:T(8,128)(2,1)}, u32[]{:S(2)}, u32[]{:S(2)}) collective-permute-start(bf16[7,16,512]{2,0,1:T(8,128)(2,1)} %bitcast.106), channel_id=1, source_target_pairs={{0,8},{4,12},{8,16},{12,20},{16,24},{20,28},{24,0},{28,4},{1,9},{5... | collective-permute-start | bytes 344072 | tf_op jit(solution)/shard_map/ppermute | solution.py:19
  133.2 14.8 %collective-permute-start.13 = (bf16[7,16,512]{2,0,1:T(8,128)(2,1)}, bf16[7,16,512]{2,0,1:T(8,128)(2,1)}, u32[]{:S(2)}, u32[]{:S(2)}) collective-permute-start(bf16[7,16,512]{2,0,1:T(8,128)(2,1)} %bitcast.107), channel_id=1, source_target_pairs={{0,4},{4,8},{8,12},{12,16},{16,20},{20,24},{24,28},{28,0},{1,5},{5... | collective-permute-start | bytes 344072 | tf_op jit(solution)/shard_map/ppermute | solution.py:19
  150.7 21.4 %all-to-all-start.3 = ((bf16[32,16,512]{2,1,0:T(8,128)(2,1)}), bf16[32,16,512]{2,1,0:T(8,128)(2,1)}, u32[]{:S(2)}, u32[]{:S(2)}) async-start(bf16[32,16,512]{2,1,0:T(8,128)(2,1)} %copy.82), calls=%async_computation.3 | async-start | bytes 1048576 | tf_op jit(solution)/shard_map/all_to_all | solution.py:108
  172.1 19.3 %all-to-all-start.2 = ((bf16[8,8,3584]{2,1,0:T(8,128)(2,1)}), bf16[8,8,3584]{2,1,0:T(8,128)(2,1)}, u32[]{:S(2)}, u32[]{:S(2)}) async-start(bf16[8,8,3584]{2,1,0:T(8,128)(2,1)} %broadcast_dynamic-update-slice_fusion), calls=%async_computation.2 | async-start | bytes 917504 | tf_op jit(solution)/shard_map/all_to_all | solution.py:59
  192.5 12.2 %collective-permute-start.9 = (bf16[64,3584]{1,0:T(8,128)(2,1)S(1)}, bf16[64,3584]{1,0:T(8,128)(2,1)S(1)}, u32[]{:S(2)}, u32[]{:S(2)}) collective-permute-start(bf16[64,3584]{1,0:T(8,128)(2,1)S(1)} %fusion.14), channel_id=1, source_target_pairs={{0,32},{32,0},{1,33},{33,1},{2,34},{34,2},{3,35},{35,3},{4,36},{36... | collective-permute-start | bytes 1376264 | tf_op jit(solution)/shard_map/ppermute | solution.py:15
  (9 other events, 182.0 us)

commit v2 on v0

v2 whole, which is shorter than its diff:
```python
import jax
import jax.numpy as jnp
from jax import lax
from jax.experimental import pallas as pl
from jax.experimental.pallas import tpu as pltpu
from jax.sharding import Mesh, PartitionSpec as P

norm_eps = 1e-06
SEC = ("x", "yh", "c")
DP = ("z", "yl")
NX, NYH, NC, NZ, NYL = 4, 2, 2, 8, 4
NSEC = NX * NYH * NC
LANES = 128
GROUP = 16
BF16, F32 = jnp.bfloat16, jnp.float32


def call(kernel, outs, args, scratch=(), flops=0, smem=()):
    specs = [pl.BlockSpec(memory_space=pltpu.SMEM if i in smem else pltpu.VMEM) for i in range(len(args))]
    moved = sum(a.size * a.dtype.itemsize for a in (*args, *outs))
    return pl.pallas_call(
        kernel,
        out_shape=outs,
        in_specs=specs,
        out_specs=[pl.BlockSpec(memory_space=pltpu.VMEM) for _ in outs],
        scratch_shapes=list(scratch),
        compiler_params=pltpu.CompilerParams(vmem_limit_bytes=16 * 2**20),
        cost_estimate=pl.CostEstimate(flops=flops, bytes_accessed=moved, transcendentals=0),
    )(*args)


def shape(*dims, dtype=BF16):
    return jax.ShapeDtypeStruct(dims, dtype)


def shift_z(value, by):
    return lax.ppermute(value, "z", [(i, (i + by) % NZ) for i in range(NZ)])


def swap_y(value, k):
    return lax.ppermute(value, "yl", [(i, i ^ k) for i in range(NYL)])


def dot(a, b, dims):
    return lax.dot_general(a, b, (dims, ((), ())), preferred_element_type=F32)


def tie(*values):
    return lax.optimization_barrier(values)


def prepare_kernel(acts, upstream, send, turned):
    tokens, width = acts.shape
    keys = upstream.shape[1]
    rows = width // (NZ * NYL)
    stream = acts[...].astype(F32)
    radius = jnp.sqrt(jnp.mean(stream * stream, axis=1, keepdims=True) + norm_eps)
    for i in range(width // LANES):
        at = slice(i * LANES, (i + 1) * LANES)
        turned[at, :] = acts[:, at].astype(F32).T.astype(BF16)
    for j in range(NYL):
        for z in range(NZ):
            low = (z * NYL + j) * rows
            send[j, z * rows : (z + 1) * rows, :] = turned[low : low + rows, :]
    for i in range(keys // LANES):
        at = slice(i * LANES, (i + 1) * LANES)
        shared = (upstream[:, at].astype(F32) / radius).T.astype(BF16)
        low = NZ * rows + i * LANES
        for j in range(NYL):
            send[j, low : low + LANES, :] = shared


def product_kernel(scale, got, weights, gains, scaled, stats, tile, *rest):
    chunks, shared, held = rest
    tokens = got.shape[2]
    width = weights.shape[0]
    rows = width // NZ
    for t in range(NYL):
        at = slice(t * tokens, (t + 1) * tokens)
        tile[:, at] = got[t, :width, :]
        shared[:, at] = got[t, width:, :]
    up = shared[...]
    cross = jnp.zeros((1, NYL * tokens), F32)
    square = jnp.zeros((1, NYL * tokens), F32)
    for z in range(NZ):
        at = slice(z * rows, (z + 1) * rows)
        here = tile[at, :]
        value = dot(weights[at, :], up, ((1,), (0,))) * gains[at, :]
        scaled[at, :] = value
        wide = here.astype(F32)
        cross = cross + jnp.sum(value * wide, axis=0, keepdims=True)
        square = square + jnp.sum(wide * wide, axis=0, keepdims=True)
        held[at, :] = (dot(here, up, ((1,), (1,))) * (gains[at, :] * scale)).astype(BF16)
    stats[0:1, :] = cross
    stats[1:2, :] = square
    j = lax.axis_index("yl")
    for k in range(NZ):
        for i in range(rows // GROUP):
            z = lax.rem(lax.div(7 * j + i, 4) - k + NZ, NZ)
            chunks[k, i] = held[pl.ds(pl.multiple_of(z * rows + i * GROUP, GROUP), GROUP), :]


def branch_kernel(full, scaled, tile, stats, out):
    pull = stats[0:1, :] / full / (stats[1:2, :] / full + norm_eps)
    width = scaled.shape[0]
    rows = width // NZ
    half = rows // 2
    for z in range(NZ):
        at = slice(z * rows, (z + 1) * rows)
        value = scaled[at, :] - tile[at, :].astype(F32) * pull
        out[2 * z] = value[:half].astype(BF16)
        out[2 * z + 1] = value[half:].astype(BF16)


def suffix_kernel(spread, out):
    run = jnp.zeros(spread.shape[1:], F32)
    for section in range(NSEC - 1, -1, -1):
        run = run + spread[section].astype(F32)
        for t in range(NYL):
            out[section * NYL + t] = run[:, t * LANES : (t + 1) * LANES].astype(BF16)


def final_kernel(got, out, turned):
    half = got.shape[1]
    for i in range(NSEC):
        for j in range(NYL):
            low = ((i // 2) * NYL + j) * 2 * half + (i % 2) * half
            turned[low : low + half, :] = got[i * NYL + j].astype(F32)
    for i in range(out.shape[1] // LANES):
        at = slice(i * LANES, (i + 1) * LANES)
        out[:, at] = turned[at, :].T.astype(BF16)


def sum_kernel(terms, out):
    total = terms[0].astype(F32)
    for k in range(1, NZ):
        total = total + terms[k].astype(F32)
    out[...] = total.astype(BF16)


def route_kernel(owners, *refs):
    parts, outs, stage = refs[:NYL], refs[NYL:-1], refs[-1]
    for k, part in enumerate(parts):
        stage[k] = part[...]
    z = lax.axis_index("z")
    j = lax.axis_index("yl")
    per = parts[0].shape[0]
    for k, out in enumerate(outs):
        out[...] = jnp.zeros_like(out)
        place = lax.rem(z + k, NZ) * NYL + j
        for b in range(owners.shape[1]):

            @pl.when(owners[0, b] == place)
            def _():
                for q in range(NYL):
                    group = 32 * b + NYL * z + q
                    shard = lax.div(group, per)
                    which = lax.rem(shard, NYL) ^ j
                    out[q * GROUP : (q + 1) * GROUP, :] = stage[which, group - shard * per]


def shampoo_kernel(*refs):
    *parts, left, right, left_gram, right_gram, precond, grads = refs
    z = lax.axis_index("z")
    rows = parts[0].shape[0]
    for k, part in enumerate(parts):
        grads[pl.ds(pl.multiple_of(lax.rem(z + NZ - k, NZ) * rows, rows), rows), :] = part[...]
    block = grads[...]
    middle = dot(left[...], block, ((1,), (0,))).astype(BF16)
    precond[...] = dot(middle, right[...], ((1,), (0,))).astype(BF16)
    left_gram[...] = (dot(block, block, ((1,), (1,))) / block.shape[0]).astype(BF16)
    right_gram[...] = (dot(block, block, ((0,), (0,))) / block.shape[0]).astype(BF16)


def body(acts, norm_gain, proj, out_grad, owner_slot, left_root, right_root):
    acts, gain, upstream, shard = acts[0], norm_gain[0], out_grad[0], proj[0]
    tokens, width = acts.shape
    rows, keys = shard.shape
    side = left_root.shape[-1]
    quarter = width // NYL
    line = NYL * tokens
    per = rows // GROUP

    (send,) = call(
        prepare_kernel,
        [shape(NYL, quarter + keys, tokens)],
        [acts, upstream],
        scratch=[pltpu.VMEM((width, tokens), BF16)],
    )
    got = lax.all_to_all(send, "yl", 0, 0)
    gains = lax.dynamic_index_in_dim(gain.reshape(NZ, NYL, rows), lax.axis_index("yl"), 1, False)
    gains = gains.reshape(quarter, 1)
    weights = lax.all_gather(shard, "z", axis=0, tiled=True)
    got, weights, gains = tie(got, weights, gains)
    scale = (tokens * NZ * NYL) ** (-0.5)
    scaled, stats, tile, chunks = call(
        lambda *refs: product_kernel(scale, *refs),
        [
            shape(quarter, line, dtype=F32),
            shape(2, line, dtype=F32),
            shape(quarter, line),
            shape(NZ, per, GROUP, keys),
        ],
        [got, weights, gains],
        scratch=[pltpu.VMEM((keys, line), BF16), pltpu.VMEM((quarter, keys), BF16)],
        flops=4 * quarter * line * keys,
    )
    terms = lax.all_to_all(chunks, "z", 0, 0)
    stats = lax.psum(stats, "yl")
    (branch,) = call(
        lambda *refs: branch_kernel(width, *refs),
        [shape(NSEC, quarter // NSEC, line)],
        [scaled, tile, stats],
    )
    branch, terms = tie(branch, terms)
    spread = lax.all_to_all(branch, SEC, 0, 0)

    (grads,) = call(sum_kernel, [shape(per, GROUP, keys)], [terms])
    parts = [grads] + [swap_y(grads, k) for k in range(1, NYL)]
    spread, *parts = tie(spread, *parts)
    (sums,) = call(suffix_kernel, [shape(NSEC * NYL, quarter // NSEC, tokens)], [spread])
    home = lax.all_to_all(sums, (*SEC, "yl"), 0, 0)
    parts = call(
        route_kernel,
        [shape(side // NZ, keys)] * NZ,
        [owner_slot, *parts],
        scratch=[pltpu.VMEM((NYL, per, GROUP, keys), BF16)],
        smem=(0,),
    )
    parts = [parts[0]] + [shift_z(parts[k], k) for k in range(1, NZ)]
    home, *parts = tie(home, *parts)
    (section_grad,) = call(
        final_kernel, [shape(tokens, width)], [home], scratch=[pltpu.VMEM((width, tokens), F32)]
    )
    out = shape(side, side)
    left_gram, right_gram, precond = call(
        shampoo_kernel,
        [out, out, out],
        [*parts, left_root[0, 0], right_root[0, 0]],
        scratch=[pltpu.VMEM((side, side), BF16)],
        flops=8 * side**3,
    )
    return section_grad[None], left_gram[None, None], right_gram[None, None], precond[None, None]


def solution(mesh):
    split = Mesh(mesh.devices.reshape(NX, NYH, NC, NZ, NYL), (*SEC, *DP))
    in_specs = (
        P(SEC, DP, None),
        P(SEC, None),
        P(SEC, DP, None),
        P(SEC, DP, None),
        P(SEC, None),
        P(SEC, DP, None, None),
        P(SEC, DP, None, None),
    )
    out_specs = (
        P(SEC, DP, None),
        P(SEC, DP, None, None),
        P(SEC, DP, None, None),
        P(SEC, DP, None, None),
    )
    return jax.shard_map(body, mesh=split, in_specs=in_specs, out_specs=out_specs, check_vma=False)
```

time: 719 us -> 169 us (0.24)
  waiting for transfers between devices: 652 us -> 46.5 us
  starting transfers between devices: 0.12 us -> 65.3 us
  blocking collectives: 0 us -> 37.1 us
  other arithmetic: 30.9 us -> 0.04 us
  between operations: 14.5 us -> 0.86 us
  matrix products: 12.3 us -> 0 us
  Pallas kernels: 0 us -> 12 us
    psum x1 -> x0, waiting for transfers between devices: 331 us -> none  [body(): summed = lax.psum(partial_value.astype(jnp.bfloat16), 'dp')]
    all_gather x2 -> x0, waiting for transfers between devices: 320 us -> none  [the longest x1 173 us: entering(): gathered = lax.all_gather(value.astype(jnp.bfloat16), axis)]
    all_to_all x0 -> x4, starting transfers between devices: none -> 32.8 us  [the longest x1 10.6 us: body(): terms = lax.all_to_all(chunks, 'z', 0, 0)]
    ppermute x0 -> x10, starting transfers between devices: none -> 32.5 us  [the longest x7 23.2 us: shift_z(): return lax.ppermute(value, 'z', [(i, (i + by) % NZ) for i in range(NZ)])]
    all_gather x0 -> x1, blocking collectives: none -> 29.8 us  [body(): weights = lax.all_gather(shard, 'z', axis=0, tiled=True)]
    ppermute x0 -> x10, waiting for transfers between devices: none -> 27.1 us  [the longest x3 22.5 us: swap_y(): return lax.ppermute(value, 'yl', [(i, i ^ k) for i in range(NYL)])]
    add x14 -> x0, other arithmetic: 22.1 us -> none  [add_later(): return earlier + later]
    all_to_all x0 -> x4, waiting for transfers between devices: none -> 19.4 us  [the longest x1 16.3 us: body(): terms = lax.all_to_all(chunks, 'z', 0, 0)]
  transfers between devices with their start and end apart: 3 -> 14, of which waited for: 3 -> 6; matrix products, arithmetic and copies ran while one was open for 3% -> 0% of each run, Pallas kernels for 0% -> 1%
where the time goes in v2:
time: 169 us; the launch traced here: 168 us
  starting transfers between devices  65.3 us (39%)
  waiting for transfers between devices  46.5 us (28%)
  blocking collectives  37.1 us (22%)
  Pallas kernels  12 us (7%)
  local copies, waits for them, and re-layouts  6.42 us (4%)
    all_gather x1, blocking collectives, body(): weights = lax.all_gather(shard, 'z', axis=0, tiled=True)  29.8 us
    ppermute x7, starting transfers between devices, shift_z(): return lax.ppermute(value, 'z', [(i, (i + by) % NZ) for i in range(NZ)])  23.2 us
    ppermute x3, waiting for transfers between devices, swap_y(): return lax.ppermute(value, 'yl', [(i, i ^ k) for i in range(NYL)])  22.5 us
    all_to_all x1, waiting for transfers between devices, body(): terms = lax.all_to_all(chunks, 'z', 0, 0)  16.3 us
    pallas_call x8, Pallas kernels, call(): pl.pallas_call(kernel, out_shape=outs, in_specs=specs, out_specs=[pl.Bloc...  12 us
    all_to_all x1, starting transfers between devices, body(): terms = lax.all_to_all(chunks, 'z', 0, 0)  10.6 us
    ppermute x3, starting transfers between devices, swap_y(): return lax.ppermute(value, 'yl', [(i, i ^ k) for i in range(NYL)])  9.3 us
    all_to_all x1, starting transfers between devices, body(): spread = lax.all_to_all(branch, SEC, 0, 0)  9.03 us
  transfers between devices with their start and end apart: 14, of which 6 were waited for; matrix products, arithmetic and copies ran while one was open for 0% of the time, Pallas kernels for 1%

profile of v2, /device:TPU:1, one launch (start us, length us, event | category | flops | bytes accessed | tf_op | source)
XLA Modules:
  0.0 168.3 jit_solution(15620344064773344647)
XLA Ops:
  4.5 5.6 %all-to-all-start = ((bf16[4,1408,128]{2,1,0:T(8,128)(2,1)}), bf16[4,1408,128]{2,1,0:T(8,128)(2,1)S(1)}, u32[]{:S(2)}, u32[]{:S(2)}) async-start(bf16[4,1408,128]{2,1,0:T(8,128)(2,1)} %shard_map.102), calls=%async_computation | async-start | bytes 2883584 | tf_op jit(solution)/shard_map/all_to_all | solution.py:190
  10.3 29.8 %all-gather = bf16[1,896,512]{2,1,0:T(8,128)(2,1)} all-gather(bf16[1,112,512]{2,1,0:T(8,128)(2,1)S(1)} %copy-done.8), channel_id=2, replica_groups=mesh['x'=4,'yh'=2,'c'=2,'z'=8,'yl'=4] {'z'}, dimensions={1}, use_global_device_ids=true | all-gather | bytes 1032192 | tf_op jit(solution)/shard_map/all_gather | solution.py:193
  40.1 3.1 %all-to-all-done.refs_0_ = bf16[4,1408,128]{2,1,0:T(8,128)(2,1)S(1)} async-done(((bf16[4,1408,128]{2,1,0:T(8,128)(2,1)}), bf16[4,1408,128]{2,1,0:T(8,128)(2,1)S(1)}, u32[]{:S(2)}, u32[]{:S(2)}) %all-to-all-start) | async-done | bytes 1441824 | tf_op jit(solution)/shard_map/all_to_all | solution.py:190
  44.5 3.3 %shard_map.103 = (f32[896,512]{1,0:T(8,128)S(1)}, f32[2,512]{1,0:T(2,128)S(1)}, bf16[896,512]{1,0:T(8,128)(2,1)S(1)}, bf16[8,7,16,512]{3,2,1,0:T(8,128)(2,1)}) custom-call(bf16[4,1408,128]{2,1,0:T(8,128)(2,1)S(1)} %all-to-all-done.refs_0_, bf16[896,512]{1,0:T(8,128)(2,1)S(1)} %bitcast.13, f32[896,1]{1,0:T(8,128)S(1)} %copy.13.refs_2_), custom_call_target="tpu_custom_call" | custom-call | flops 939524096 | bytes 6036992 | tf_op jit(solution)/shard_map/pallas_call | solution.py:21
  49.1 10.6 %all-to-all-start.1 = ((bf16[8,7,16,512]{3,2,1,0:T(8,128)(2,1)}), bf16[8,7,16,512]{3,2,1,0:T(8,128)(2,1)S(1)}, u32[]{:S(2)}, u32[]{:S(2)}) async-start(bf16[8,7,16,512]{3,2,1,0:T(8,128)(2,1)} %get-tuple-element.44), calls=%async_computation.1 | async-start | bytes 1835008 | tf_op jit(solution)/shard_map/all_to_all | solution.py:208
  59.7 7.4 %psum.7.refs_2_ = f32[2,512]{1,0:T(2,128)S(1)} all-reduce(f32[2,512]{1,0:T(2,128)S(1)} %get-tuple-element.43), channel_id=1, replica_groups=mesh['x'=4,'yh'=2,'c'=2,'z'=8,'yl'=4] {'yl'}, use_global_device_ids=true, to_apply=%region_0.1 | all-reduce | flops 1024 | bytes 8192 | tf_op jit(solution)/shard_map/psum | solution.py:209
  69.8 16.3 %all-to-all-done.1.terms = bf16[8,7,16,512]{3,2,1,0:T(8,128)(2,1)S(1)} async-done(((bf16[8,7,16,512]{3,2,1,0:T(8,128)(2,1)}), bf16[8,7,16,512]{3,2,1,0:T(8,128)(2,1)S(1)}, u32[]{:S(2)}, u32[]{:S(2)}) %all-to-all-start.1) | async-done | bytes 917536 | tf_op jit(solution)/shard_map/all_to_all | solution.py:208
  86.1 9.0 %all-to-all-start.2 = ((bf16[16,56,512]{2,1,0:T(8,128)(2,1)}), bf16[16,56,512]{2,1,0:T(8,128)(2,1)S(1)}, u32[]{:S(2)}, u32[]{:S(2)}) async-start(bf16[16,56,512]{2,1,0:T(8,128)(2,1)} %shard_map.104), calls=%async_computation.2 | async-start | bytes 1835008 | tf_op jit(solution)/shard_map/all_to_all | solution.py:216
  95.3 3.0 %collective-permute-start.2 = (bf16[7,16,512]{2,1,0:T(8,128)(2,1)S(1)}, bf16[7,16,512]{2,1,0:T(8,128)(2,1)S(1)}, u32[]{:S(2)}, u32[]{:S(2)}) collective-permute-start(bf16[7,16,512]{2,1,0:T(8,128)(2,1)S(1)} %shard_map.105.refs_0_), channel_id=1, source_target_pairs={{0,3},{1,2},{2,1},{3,0},{4,7},{5,6},{6,5},{7,4},{8,11},{9,10},{10,... | collective-permute-start | bytes 344072 | tf_op jit(solution)/shard_map/ppermute | solution.py:41
  98.3 1.9 %collective-permute-start.1 = (bf16[7,16,512]{2,1,0:T(8,128)(2,1)S(1)}, bf16[7,16,512]{2,1,0:T(8,128)(2,1)S(1)}, u32[]{:S(2)}, u32[]{:S(2)}) collective-permute-start(bf16[7,16,512]{2,1,0:T(8,128)(2,1)S(1)} %shard_map.105.refs_0_), channel_id=1, source_target_pairs={{0,2},{1,3},{2,0},{3,1},{4,6},{5,7},{6,4},{7,5},{8,10},{9,11},{10,... | collective-permute-start | bytes 344072 | tf_op jit(solution)/shard_map/ppermute | solution.py:41
  100.2 4.4 %collective-permute-start = (bf16[7,16,512]{2,1,0:T(8,128)(2,1)S(1)}, bf16[7,16,512]{2,1,0:T(8,128)(2,1)S(1)}, u32[]{:S(2)}, u32[]{:S(2)}) collective-permute-start(bf16[7,16,512]{2,1,0:T(8,128)(2,1)S(1)} %shard_map.105.refs_0_), channel_id=1, source_target_pairs={{0,1},{1,0},{2,3},{3,2},{4,5},{5,4},{6,7},{7,6},{8,9},{9,8},{10,11... | collective-permute-start | bytes 344072 | tf_op jit(solution)/shard_map/ppermute | solution.py:41
  104.6 15.0 %collective-permute-done.2.refs_3_ = bf16[7,16,512]{2,1,0:T(8,128)(2,1)S(1)} collective-permute-done((bf16[7,16,512]{2,1,0:T(8,128)(2,1)S(1)}, bf16[7,16,512]{2,1,0:T(8,128)(2,1)S(1)}, u32[]{:S(2)}, u32[]{:S(2)}) %collective-permute-start.2) | collective-permute-done | bytes 114720 | tf_op jit(solution)/shard_map/ppermute | solution.py:41
  119.6 7.5 %collective-permute-done.1.refs_2_ = bf16[7,16,512]{2,1,0:T(8,128)(2,1)S(1)} collective-permute-done((bf16[7,16,512]{2,1,0:T(8,128)(2,1)S(1)}, bf16[7,16,512]{2,1,0:T(8,128)(2,1)S(1)}, u32[]{:S(2)}, u32[]{:S(2)}) %collective-permute-start.1) | collective-permute-done | bytes 114720 | tf_op jit(solution)/shard_map/ppermute | solution.py:41
  128.2 7.6 %all-to-all-start.3 = ((bf16[64,56,128]{2,1,0:T(8,128)(2,1)}), bf16[64,56,128]{2,1,0:T(8,128)(2,1)S(1)}, u32[]{:S(2)}, u32[]{:S(2)}) async-start(bf16[64,56,128]{2,1,0:T(8,128)(2,1)} %shard_map.106), calls=%async_computation.3 | async-start | bytes 1835008 | tf_op jit(solution)/shard_map/all_to_all | solution.py:222
  136.9 2.2 %collective-permute-start.3 = (bf16[64,512]{1,0:T(8,128)(2,1)S(1)}, bf16[64,512]{1,0:T(8,128)(2,1)S(1)}, u32[]{:S(2)}, u32[]{:S(2)}) collective-permute-start(bf16[64,512]{1,0:T(8,128)(2,1)S(1)} %get-tuple-element.53), channel_id=1, source_target_pairs={{0,4},{4,8},{8,12},{12,16},{16,20},{20,24},{24,28},{28,0},{1,5},{5... | collective-permute-start | bytes 196616 | tf_op jit(solution)/shard_map/ppermute | solution.py:37
  139.1 2.1 %collective-permute-start.4 = (bf16[64,512]{1,0:T(8,128)(2,1)S(1)}, bf16[64,512]{1,0:T(8,128)(2,1)S(1)}, u32[]{:S(2)}, u32[]{:S(2)}) collective-permute-start(bf16[64,512]{1,0:T(8,128)(2,1)S(1)} %get-tuple-element.54), channel_id=1, source_target_pairs={{0,8},{4,12},{8,16},{12,20},{16,24},{20,28},{24,0},{28,4},{1,9},{5... | collective-permute-start | bytes 196616 | tf_op jit(solution)/shard_map/ppermute | solution.py:37
  141.2 3.9 %collective-permute-start.5 = (bf16[64,512]{1,0:T(8,128)(2,1)S(1)}, bf16[64,512]{1,0:T(8,128)(2,1)S(1)}, u32[]{:S(2)}, u32[]{:S(2)}) collective-permute-start(bf16[64,512]{1,0:T(8,128)(2,1)S(1)} %get-tuple-element.55), channel_id=1, source_target_pairs={{0,12},{4,16},{8,20},{12,24},{16,28},{20,0},{24,4},{28,8},{1,13},{... | collective-permute-start | bytes 196616 | tf_op jit(solution)/shard_map/ppermute | solution.py:37
  145.0 5.1 %collective-permute-start.6 = (bf16[64,512]{1,0:T(8,128)(2,1)S(1)}, bf16[64,512]{1,0:T(8,128)(2,1)S(1)}, u32[]{:S(2)}, u32[]{:S(2)}) collective-permute-start(bf16[64,512]{1,0:T(8,128)(2,1)S(1)} %get-tuple-element.56), channel_id=1, source_target_pairs={{0,16},{4,20},{8,24},{12,28},{16,0},{20,4},{24,8},{28,12},{1,17},{... | collective-permute-start | bytes 196616 | tf_op jit(solution)/shard_map/ppermute | solution.py:37
  150.2 3.1 %collective-permute-start.7 = (bf16[64,512]{1,0:T(8,128)(2,1)S(1)}, bf16[64,512]{1,0:T(8,128)(2,1)S(1)}, u32[]{:S(2)}, u32[]{:S(2)}) collective-permute-start(bf16[64,512]{1,0:T(8,128)(2,1)S(1)} %get-tuple-element.57), channel_id=1, source_target_pairs={{0,20},{4,24},{8,28},{12,0},{16,4},{20,8},{24,12},{28,16},{1,21},{... | collective-permute-start | bytes 196616 | tf_op jit(solution)/shard_map/ppermute | solution.py:37
  153.3 4.3 %collective-permute-start.8 = (bf16[64,512]{1,0:T(8,128)(2,1)S(1)}, bf16[64,512]{1,0:T(8,128)(2,1)S(1)}, u32[]{:S(2)}, u32[]{:S(2)}) collective-permute-start(bf16[64,512]{1,0:T(8,128)(2,1)S(1)} %get-tuple-element.58), channel_id=1, source_target_pairs={{0,24},{4,28},{8,0},{12,4},{16,8},{20,12},{24,16},{28,20},{1,25},{... | collective-permute-start | bytes 196616 | tf_op jit(solution)/shard_map/ppermute | solution.py:37
  157.6 2.5 %collective-permute-start.9 = (bf16[64,512]{1,0:T(8,128)(2,1)S(1)}, bf16[64,512]{1,0:T(8,128)(2,1)S(1)}, u32[]{:S(2)}, u32[]{:S(2)}) collective-permute-start(bf16[64,512]{1,0:T(8,128)(2,1)S(1)} %get-tuple-element.59), channel_id=1, source_target_pairs={{0,28},{4,0},{8,4},{12,8},{16,12},{20,16},{24,20},{28,24},{1,29},{... | collective-permute-start | bytes 196616 | tf_op jit(solution)/shard_map/ppermute | solution.py:37
  160.1 2.6 %collective-permute-done.8.refs_6_ = bf16[64,512]{1,0:T(8,128)(2,1)S(1)} collective-permute-done((bf16[64,512]{1,0:T(8,128)(2,1)S(1)}, bf16[64,512]{1,0:T(8,128)(2,1)S(1)}, u32[]{:S(2)}, u32[]{:S(2)}) %collective-permute-start.8) | collective-permute-done | bytes 65568 | tf_op jit(solution)/shard_map/ppermute | solution.py:37
  162.7 2.0 %collective-permute-done.9.refs_7_ = bf16[64,512]{1,0:T(8,128)(2,1)S(1)} collective-permute-done((bf16[64,512]{1,0:T(8,128)(2,1)S(1)}, bf16[64,512]{1,0:T(8,128)(2,1)S(1)}, u32[]{:S(2)}, u32[]{:S(2)}) %collective-permute-start.9) | collective-permute-done | bytes 65568 | tf_op jit(solution)/shard_map/ppermute | solution.py:37
  166.0 2.3 %shard_map.109 = (bf16[512,512]{1,0:T(8,128)(2,1)}, bf16[512,512]{1,0:T(8,128)(2,1)}, bf16[512,512]{1,0:T(8,128)(2,1)}) custom-call(bf16[64,512]{1,0:T(8,128)(2,1)S(1)} %get-tuple-element.61.refs_0_, bf16[64,512]{1,0:T(8,128)(2,1)S(1)} %collective-permute-done.3.refs_1_, bf16[64,512]{1,0:T(8,128)(2,1)S(1)} %collective-permute-done.4.refs_2_, ...), custom_call_target="tpu_custom_call" | custom-call | flops 1073741824 | bytes 3145728 | tf_op jit(solution)/shard_map/pallas_call | solution.py:21
  (39 shorter events, 12.9 us)
Async XLA Ops:
  0.6 1.2 copy-start.2
  1.8 0.9 copy-start.4
  4.5 5.6 %copy-start.9 = (f32[1,3584]{1,0:T(1,128)S(1)}, f32[1,3584]{1,0:T(1,128)}, u32[]{:S(2)}) copy-start(f32[1,3584]{1,0:T(1,128)} %param.8) | copy-start | bytes 43012
  4.5 5.8 %copy-start.8 = (bf16[1,112,512]{2,1,0:T(8,128)(2,1)S(1)}, bf16[1,112,512]{2,1,0:T(8,128)(2,1)}, u32[]{:S(2)}) copy-start(bf16[1,112,512]{2,1,0:T(8,128)(2,1)} %param.9) | copy-start | bytes 344068
  4.5 38.6 %all-to-all-start = ((bf16[4,1408,128]{2,1,0:T(8,128)(2,1)}), bf16[4,1408,128]{2,1,0:T(8,128)(2,1)S(1)}, u32[]{:S(2)}, u32[]{:S(2)}) async-start(bf16[4,1408,128]{2,1,0:T(8,128)(2,1)} %shard_map.102), calls=%async_computation | async-start | bytes 2883584 | tf_op jit(solution)/shard_map/all_to_all | solution.py:190
  43.4 1.2 copy-start.3
  47.9 1.3 copy-start
  49.1 37.0 %all-to-all-start.1 = ((bf16[8,7,16,512]{3,2,1,0:T(8,128)(2,1)}), bf16[8,7,16,512]{3,2,1,0:T(8,128)(2,1)S(1)}, u32[]{:S(2)}, u32[]{:S(2)}) async-start(bf16[8,7,16,512]{3,2,1,0:T(8,128)(2,1)} %get-tuple-element.44), calls=%async_computation.1 | async-start | bytes 1835008 | tf_op jit(solution)/shard_map/all_to_all | solution.py:208
  67.1 1.5 copy-start.1
  86.1 41.0 %all-to-all-start.2 = ((bf16[16,56,512]{2,1,0:T(8,128)(2,1)}), bf16[16,56,512]{2,1,0:T(8,128)(2,1)S(1)}, u32[]{:S(2)}, u32[]{:S(2)}) async-start(bf16[16,56,512]{2,1,0:T(8,128)(2,1)} %shard_map.104), calls=%async_computation.2 | async-start | bytes 1835008 | tf_op jit(solution)/shard_map/all_to_all | solution.py:216
  95.3 40.5 %copy-start.5 = (s32[1,7]{1,0:T(1,128)S(1)}, s32[1,7]{1,0:T(1,128)}, u32[]{:S(2)}) copy-start(s32[1,7]{1,0:T(1,128)} %owners.1) | copy-start | bytes 88
  95.3 24.3 %collective-permute-start.2 = (bf16[7,16,512]{2,1,0:T(8,128)(2,1)S(1)}, bf16[7,16,512]{2,1,0:T(8,128)(2,1)S(1)}, u32[]{:S(2)}, u32[]{:S(2)}) collective-permute-start(bf16[7,16,512]{2,1,0:T(8,128)(2,1)S(1)} %shard_map.105.refs_0_), channel_id=1, source_target_pairs={{0,3},{1,2},{2,1},{3,0},{4,7},{5,6},{6,5},{7,4},{8,11},{9,10},{10,... | collective-permute-start | bytes 344072 | tf_op jit(solution)/shard_map/ppermute | solution.py:41
  98.3 28.8 %collective-permute-start.1 = (bf16[7,16,512]{2,1,0:T(8,128)(2,1)S(1)}, bf16[7,16,512]{2,1,0:T(8,128)(2,1)S(1)}, u32[]{:S(2)}, u32[]{:S(2)}) collective-permute-start(bf16[7,16,512]{2,1,0:T(8,128)(2,1)S(1)} %shard_map.105.refs_0_), channel_id=1, source_target_pairs={{0,2},{1,3},{2,0},{3,1},{4,6},{5,7},{6,4},{7,5},{8,10},{9,11},{10,... | collective-permute-start | bytes 344072 | tf_op jit(solution)/shard_map/ppermute | solution.py:41
  100.2 26.9 %collective-permute-start = (bf16[7,16,512]{2,1,0:T(8,128)(2,1)S(1)}, bf16[7,16,512]{2,1,0:T(8,128)(2,1)S(1)}, u32[]{:S(2)}, u32[]{:S(2)}) collective-permute-start(bf16[7,16,512]{2,1,0:T(8,128)(2,1)S(1)} %shard_map.105.refs_0_), channel_id=1, source_target_pairs={{0,1},{1,0},{2,3},{3,2},{4,5},{5,4},{6,7},{7,6},{8,9},{9,8},{10,11... | collective-permute-start | bytes 344072 | tf_op jit(solution)/shard_map/ppermute | solution.py:41
  128.2 36.6 %all-to-all-start.3 = ((bf16[64,56,128]{2,1,0:T(8,128)(2,1)}), bf16[64,56,128]{2,1,0:T(8,128)(2,1)S(1)}, u32[]{:S(2)}, u32[]{:S(2)}) async-start(bf16[64,56,128]{2,1,0:T(8,128)(2,1)} %shard_map.106), calls=%async_computation.3 | async-start | bytes 1835008 | tf_op jit(solution)/shard_map/all_to_all | solution.py:222
  135.8 30.2 %copy-start.6 = (bf16[1,1,512,512]{3,2,1,0:T(8,128)(2,1)S(1)}, bf16[1,1,512,512]{3,2,1,0:T(8,128)(2,1)}, u32[]{:S(2)}) copy-start(bf16[1,1,512,512]{3,2,1,0:T(8,128)(2,1)} %param.12) | copy-start | bytes 1572868
  135.8 30.2 %copy-start.7 = (bf16[1,1,512,512]{3,2,1,0:T(8,128)(2,1)S(1)}, bf16[1,1,512,512]{3,2,1,0:T(8,128)(2,1)}, u32[]{:S(2)}) copy-start(bf16[1,1,512,512]{3,2,1,0:T(8,128)(2,1)} %param.13) | copy-start | bytes 1572868
  136.9 16.4 %collective-permute-start.3 = (bf16[64,512]{1,0:T(8,128)(2,1)S(1)}, bf16[64,512]{1,0:T(8,128)(2,1)S(1)}, u32[]{:S(2)}, u32[]{:S(2)}) collective-permute-start(bf16[64,512]{1,0:T(8,128)(2,1)S(1)} %get-tuple-element.53), channel_id=1, source_target_pairs={{0,4},{4,8},{8,12},{12,16},{16,20},{20,24},{24,28},{28,0},{1,5},{5... | collective-permute-start | bytes 196616 | tf_op jit(solution)/shard_map/ppermute | solution.py:37
  139.1 18.6 %collective-permute-start.4 = (bf16[64,512]{1,0:T(8,128)(2,1)S(1)}, bf16[64,512]{1,0:T(8,128)(2,1)S(1)}, u32[]{:S(2)}, u32[]{:S(2)}) collective-permute-start(bf16[64,512]{1,0:T(8,128)(2,1)S(1)} %get-tuple-element.54), channel_id=1, source_target_pairs={{0,8},{4,12},{8,16},{12,20},{16,24},{20,28},{24,0},{28,4},{1,9},{5... | collective-permute-start | bytes 196616 | tf_op jit(solution)/shard_map/ppermute | solution.py:37
  141.2 18.9 %collective-permute-start.5 = (bf16[64,512]{1,0:T(8,128)(2,1)S(1)}, bf16[64,512]{1,0:T(8,128)(2,1)S(1)}, u32[]{:S(2)}, u32[]{:S(2)}) collective-permute-start(bf16[64,512]{1,0:T(8,128)(2,1)S(1)} %get-tuple-element.55), channel_id=1, source_target_pairs={{0,12},{4,16},{8,20},{12,24},{16,28},{20,0},{24,4},{28,8},{1,13},{... | collective-permute-start | bytes 196616 | tf_op jit(solution)/shard_map/ppermute | solution.py:37
  145.0 15.1 %collective-permute-start.6 = (bf16[64,512]{1,0:T(8,128)(2,1)S(1)}, bf16[64,512]{1,0:T(8,128)(2,1)S(1)}, u32[]{:S(2)}, u32[]{:S(2)}) collective-permute-start(bf16[64,512]{1,0:T(8,128)(2,1)S(1)} %get-tuple-element.56), channel_id=1, source_target_pairs={{0,16},{4,20},{8,24},{12,28},{16,0},{20,4},{24,8},{28,12},{1,17},{... | collective-permute-start | bytes 196616 | tf_op jit(solution)/shard_map/ppermute | solution.py:37
  150.2 9.9 %collective-permute-start.7 = (bf16[64,512]{1,0:T(8,128)(2,1)S(1)}, bf16[64,512]{1,0:T(8,128)(2,1)S(1)}, u32[]{:S(2)}, u32[]{:S(2)}) collective-permute-start(bf16[64,512]{1,0:T(8,128)(2,1)S(1)} %get-tuple-element.57), channel_id=1, source_target_pairs={{0,20},{4,24},{8,28},{12,0},{16,4},{20,8},{24,12},{28,16},{1,21},{... | collective-permute-start | bytes 196616 | tf_op jit(solution)/shard_map/ppermute | solution.py:37
  153.3 9.4 %collective-permute-start.8 = (bf16[64,512]{1,0:T(8,128)(2,1)S(1)}, bf16[64,512]{1,0:T(8,128)(2,1)S(1)}, u32[]{:S(2)}, u32[]{:S(2)}) collective-permute-start(bf16[64,512]{1,0:T(8,128)(2,1)S(1)} %get-tuple-element.58), channel_id=1, source_target_pairs={{0,24},{4,28},{8,0},{12,4},{16,8},{20,12},{24,16},{28,20},{1,25},{... | collective-permute-start | bytes 196616 | tf_op jit(solution)/shard_map/ppermute | solution.py:37
  157.6 7.1 %collective-permute-start.9 = (bf16[64,512]{1,0:T(8,128)(2,1)S(1)}, bf16[64,512]{1,0:T(8,128)(2,1)S(1)}, u32[]{:S(2)}, u32[]{:S(2)}) collective-permute-start(bf16[64,512]{1,0:T(8,128)(2,1)S(1)} %get-tuple-element.59), channel_id=1, source_target_pairs={{0,28},{4,0},{8,4},{12,8},{16,12},{20,16},{24,20},{28,24},{1,29},{... | collective-permute-start | bytes 196616 | tf_op jit(solution)/shard_map/ppermute | solution.py:37

commit v3 on v2

v3 whole, which is shorter than its diff:
```python
import jax
import jax.numpy as jnp
from jax import lax
from jax.experimental import pallas as pl
from jax.experimental.pallas import tpu as pltpu
from jax.sharding import Mesh, PartitionSpec as P

norm_eps = 1e-06
SEC = ("x", "yh", "c")
DP = ("z", "yl")
NX, NYH, NC, NZ, NYL = 4, 2, 2, 8, 4
PAIRS = ("x", "yh")
NPAIR = NX * NYH
LANES = 128
GROUP = 16
BF16, F32 = jnp.bfloat16, jnp.float32


def call(kernel, outs, args, scratch=(), flops=0, smem=()):
    specs = [pl.BlockSpec(memory_space=pltpu.SMEM if i in smem else pltpu.VMEM) for i in range(len(args))]
    moved = sum(a.size * a.dtype.itemsize for a in (*args, *outs))
    return pl.pallas_call(
        kernel,
        out_shape=outs,
        in_specs=specs,
        out_specs=[pl.BlockSpec(memory_space=pltpu.VMEM) for _ in outs],
        scratch_shapes=list(scratch),
        compiler_params=pltpu.CompilerParams(vmem_limit_bytes=16 * 2**20),
        cost_estimate=pl.CostEstimate(flops=flops, bytes_accessed=moved, transcendentals=0),
    )(*args)


def shape(*dims, dtype=BF16):
    return jax.ShapeDtypeStruct(dims, dtype)


def shift_z(value, by):
    return lax.ppermute(value, "z", [(i, (i + by) % NZ) for i in range(NZ)])


def swap_cores(value):
    return lax.ppermute(value, "c", [(0, 1), (1, 0)])


def swap_y(value, k):
    return lax.ppermute(value, "yl", [(i, i ^ k) for i in range(NYL)])


def dot(a, b, dims):
    return lax.dot_general(a, b, (dims, ((), ())), preferred_element_type=F32)


def tie(*values):
    return lax.optimization_barrier(values)


def prepare_kernel(acts, upstream, send, turned):
    tokens, width = acts.shape
    keys = upstream.shape[1]
    rows = width // (NZ * NYL)
    stream = acts[...].astype(F32)
    radius = jnp.sqrt(jnp.mean(stream * stream, axis=1, keepdims=True) + norm_eps)
    for i in range(width // LANES):
        at = slice(i * LANES, (i + 1) * LANES)
        turned[at, :] = acts[:, at].astype(F32).T.astype(BF16)
    for j in range(NYL):
        for z in range(NZ):
            low = (z * NYL + j) * rows
            send[j, z * rows : (z + 1) * rows, :] = turned[low : low + rows, :]
    for i in range(keys // LANES):
        at = slice(i * LANES, (i + 1) * LANES)
        shared = (upstream[:, at].astype(F32) / radius).T.astype(BF16)
        low = NZ * rows + i * LANES
        for j in range(NYL):
            send[j, low : low + LANES, :] = shared


def gradient_kernel(scale, got, gains, keep, give, tile, shared, held):
    tokens = got.shape[2]
    width = gains.shape[0]
    rows = width // NZ
    for t in range(NYL):
        at = slice(t * tokens, (t + 1) * tokens)
        tile[:, at] = got[t, :width, :]
        shared[:, at] = got[t, width:, :]
    up = shared[...]
    for z in range(NZ):
        at = slice(z * rows, (z + 1) * rows)
        held[at, :] = (dot(tile[at, :], up, ((1,), (1,))) * (gains[at, :] * scale)).astype(BF16)
    j = lax.axis_index("yl")
    mine = lax.axis_index("z")
    for k in range(NZ):
        out = give if k % 2 else keep
        to = k - k % 2 + lax.rem(mine + k, 2)
        for i in range(rows // GROUP):
            z = lax.rem(lax.div(7 * j + i, 4) - to + NZ, NZ)
            out[k // 2, i] = held[pl.ds(pl.multiple_of(z * rows + i * GROUP, GROUP), GROUP), :]


def back_kernel(got, weights, gains, scaled, stats, shared):
    tokens = got.shape[2]
    width = weights.shape[0]
    rows = width // NZ
    for t in range(NYL):
        shared[:, t * tokens : (t + 1) * tokens] = got[t, width:, :]
    up = shared[...]
    cross = [jnp.zeros((1, tokens), F32) for _ in range(NYL)]
    square = [jnp.zeros((1, tokens), F32) for _ in range(NYL)]
    for z in range(NZ):
        at = slice(z * rows, (z + 1) * rows)
        value = dot(weights[at, :], up, ((1,), (0,))) * gains[at, :]
        scaled[at, :] = value
        for t in range(NYL):
            wide = got[t, at, :].astype(F32)
            cross[t] = cross[t] + jnp.sum(value[:, t * tokens : (t + 1) * tokens] * wide, axis=0, keepdims=True)
            square[t] = square[t] + jnp.sum(wide * wide, axis=0, keepdims=True)
    for t in range(NYL):
        stats[0:1, t * tokens : (t + 1) * tokens] = cross[t]
        stats[1:2, t * tokens : (t + 1) * tokens] = square[t]


def branch_kernel(full, scaled, got, stats, out):
    pull = stats[0:1, :] / full / (stats[1:2, :] / full + norm_eps)
    tokens = got.shape[2]
    rows = out.shape[1]
    for i in range(NPAIR):
        at = slice(i * rows, (i + 1) * rows)
        for t in range(NYL):
            to = slice(t * tokens, (t + 1) * tokens)
            out[i, :, to] = (scaled[at, to] - got[t, at, :].astype(F32) * pull[:, to]).astype(BF16)


def suffix_kernel(spread, out):
    last = (lax.axis_index("c") == 1).astype(F32)
    run = jnp.zeros(spread.shape[1:], F32)
    for pair in range(NPAIR - 1, -1, -1):
        value = spread[pair].astype(F32)
        out[pair] = (run + value * last).astype(BF16)
        run = run + value


def section_kernel(spread, got, out):
    run = jnp.zeros(spread.shape[1:], F32)
    for pair in range(NPAIR - 1, -1, -1):
        run = run + spread[pair].astype(F32)
        value = run + got[pair].astype(F32)
        for t in range(NYL):
            out[pair * NYL + t] = value[:, t * LANES : (t + 1) * LANES].astype(BF16)


def final_kernel(turned, out):
    for i in range(out.shape[1] // LANES):
        at = slice(i * LANES, (i + 1) * LANES)
        out[:, at] = turned[at, :].astype(F32).T.astype(BF16)


def add_kernel(keep, got, *outs):
    h = lax.div(lax.axis_index("z"), 2)
    for k, out in enumerate(outs):
        at = lax.rem(h + k, NZ // 2)
        out[...] = (keep[at].astype(F32) + got[at].astype(F32)).astype(BF16)


def sum_kernel(*refs):
    *terms, out = refs
    total = terms[0][...].astype(F32)
    for term in terms[1:]:
        total = total + term[...].astype(F32)
    out[...] = total.astype(BF16)


def route_kernel(owners, *refs):
    parts, (keep, give, stage) = refs[:NYL], refs[NYL:]
    for k, part in enumerate(parts):
        stage[k] = part[...]
    z = lax.axis_index("z")
    j = lax.axis_index("yl")
    per = parts[0].shape[0]
    for i in range(NZ):
        out = give if i % 2 else keep
        out[i // 2] = jnp.zeros(out.shape[1:], BF16)
        place = (i - i % 2 + lax.rem(z + i, 2)) * NYL + j
        for b in range(owners.shape[1]):

            @pl.when(owners[0, b] == place)
            def _():
                for q in range(NYL):
                    group = 32 * b + NYL * z + q
                    shard = lax.div(group, per)
                    which = lax.rem(shard, NYL) ^ j
                    out[i // 2, q * GROUP : (q + 1) * GROUP, :] = stage[which, group - shard * per]


def pair_kernel(keep, got, *outs):
    h = lax.div(lax.axis_index("z"), 2)
    for k, out in enumerate(outs):
        at = lax.rem(h + k, NZ // 2)
        out[0] = keep[at]
        out[1] = got[at]


def shampoo_kernel(*refs):
    *parts, left, right, left_gram, right_gram, precond, grads = refs
    z = lax.axis_index("z")
    rows = parts[0].shape[1]
    for k, part in enumerate(parts):
        source = lax.rem(z + NZ - 2 * k, NZ)
        grads[pl.ds(pl.multiple_of(source * rows, rows), rows), :] = part[0]
        grads[pl.ds(pl.multiple_of((source ^ 1) * rows, rows), rows), :] = part[1]
    block = grads[...]
    middle = dot(left[...], block, ((1,), (0,))).astype(BF16)
    precond[...] = dot(middle, right[...], ((1,), (0,))).astype(BF16)
    left_gram[...] = (dot(block, block, ((1,), (1,))) / block.shape[0]).astype(BF16)
    right_gram[...] = (dot(block, block, ((0,), (0,))) / block.shape[0]).astype(BF16)


def body(acts, norm_gain, proj, out_grad, owner_slot, left_root, right_root):
    acts, gain, upstream, shard = acts[0], norm_gain[0], out_grad[0], proj[0]
    tokens, width = acts.shape
    rows, keys = shard.shape
    side = left_root.shape[-1]
    quarter = width // NYL
    line = NYL * tokens
    per = rows // GROUP

    (send,) = call(
        prepare_kernel,
        [shape(NYL, quarter + keys, tokens)],
        [acts, upstream],
        scratch=[pltpu.VMEM((width, tokens), BF16)],
    )
    got = lax.all_to_all(send, "yl", 0, 0)
    gains = lax.dynamic_index_in_dim(gain.reshape(NZ, NYL, rows), lax.axis_index("yl"), 1, False)
    gains = gains.reshape(quarter, 1)
    weights = lax.all_gather(shard, "z", axis=0, tiled=True)
    got, weights, gains = tie(got, weights, gains)
    scale = (tokens * NZ * NYL) ** (-0.5)
    chunk = shape(NZ // 2, per, GROUP, keys)
    chunks, away = call(
        lambda *refs: gradient_kernel(scale, *refs),
        [chunk, chunk],
        [got, gains],
        scratch=[pltpu.VMEM((quarter, line), BF16), pltpu.VMEM((keys, line), BF16), pltpu.VMEM((quarter, keys), BF16)],
        flops=2 * quarter * line * keys,
    )

    near = lax.ppermute(away, "z", [(i, i ^ 1) for i in range(NZ)])
    scaled, stats = call(
        back_kernel,
        [shape(quarter, line, dtype=F32), shape(2, line, dtype=F32)],
        [got, weights, gains],
        scratch=[pltpu.VMEM((keys, line), BF16)],
        flops=2 * quarter * line * keys,
    )
    stats = lax.psum(stats, "yl")
    (branch,) = call(
        lambda *refs: branch_kernel(width, *refs),
        [shape(NPAIR, quarter // NPAIR, line)],
        [scaled, got, stats],
    )
    branch, near = tie(branch, near)

    spread = lax.all_to_all(branch, PAIRS, 0, 0)
    terms = call(add_kernel, [shape(per, GROUP, keys)] * (NZ // 2), [chunks, near])
    terms = [terms[0]] + [shift_z(terms[k], 2 * k) for k in range(1, NZ // 2)]
    (grads,) = call(sum_kernel, [shape(per, GROUP, keys)], terms)
    spread, grads = tie(spread, grads)
    (give,) = call(suffix_kernel, [shape(NPAIR, quarter // NPAIR, line)], [spread])
    take = swap_cores(give)
    parts = [grads] + [swap_y(grads, k) for k in range(1, NYL)]
    (sums,) = call(section_kernel, [shape(NPAIR * NYL, quarter // NPAIR, tokens)], [spread, take])
    sums, *parts = tie(sums, *parts)
    home = lax.all_to_all(sums, (*PAIRS, "yl"), 0, 0).reshape(width, tokens)

    half = shape(NZ // 2, side // NZ, keys)
    keep, away = call(
        route_kernel,
        [half, half],
        [owner_slot, *parts],
        scratch=[pltpu.VMEM((NYL, per, GROUP, keys), BF16)],
        smem=(0,),
    )
    near = lax.ppermute(away, "z", [(i, i ^ 1) for i in range(NZ)])
    parts = call(pair_kernel, [shape(2, side // NZ, keys)] * (NZ // 2), [keep, near])
    parts = [parts[0]] + [shift_z(parts[k], 2 * k) for k in range(1, NZ // 2)]
    out = shape(side, side)
    left_gram, right_gram, precond = call(
        shampoo_kernel,
        [out, out, out],
        [*parts, left_root[0, 0], right_root[0, 0]],
        scratch=[pltpu.VMEM((side, side), BF16)],
        flops=8 * side**3,
    )
    home, left_gram, right_gram, precond = tie(home, left_gram, right_gram, precond)
    (section_grad,) = call(final_kernel, [shape(tokens, width)], [home])
    return section_grad[None], left_gram[None, None], right_gram[None, None], precond[None, None]


def solution(mesh):
    split = Mesh(mesh.devices.reshape(NX, NYH, NC, NZ, NYL), (*SEC, *DP))
    in_specs = (
        P(SEC, DP, None),
        P(SEC, None),
        P(SEC, DP, None),
        P(SEC, DP, None),
        P(SEC, None),
        P(SEC, DP, None, None),
        P(SEC, DP, None, None),
    )
    out_specs = (
        P(SEC, DP, None),
        P(SEC, DP, None, None),
        P(SEC, DP, None, None),
        P(SEC, DP, None, None),
    )
    return jax.shard_map(body, mesh=split, in_specs=in_specs, out_specs=out_specs, check_vma=False)
```

time: 169 us -> 161 us (0.953)
  waiting for transfers between devices: 46.5 us -> 31.2 us
  starting transfers between devices: 65.3 us -> 73.9 us
  blocking collectives: 37.1 us -> 35.2 us
    ppermute x3, waiting for transfers between devices: 22.5 us -> 4.83 us  [swap_y(): return lax.ppermute(value, 'yl', [(i, i ^ k) for i in range(NYL)])]
    all_to_all x3 -> x2, waiting for transfers between devices: 16.3 us -> 0.01 us  [the longest x1 0.01 us: body(): spread = lax.all_to_all(branch, PAIRS, 0, 0)]
    ppermute x0 -> x3, starting transfers between devices: none -> 12.3 us  [the longest x2 6.5 us: body(): near = lax.ppermute(away, 'z', [(i, i ^ 1) for i in range(NZ)])]
    ppermute x7 -> x6, waiting for transfers between devices: 4.63 us -> 15 us  [shift_z(): return lax.ppermute(value, 'z', [(i, (i + by) % NZ) for i in range(NZ)])]
    all_to_all x3 -> x2, starting transfers between devices: 27.3 us -> 18.8 us  [the longest x1 10.3 us: body(): home = lax.all_to_all(sums, (*PAIRS, 'yl'), 0, 0).reshape(width, tokens)]
    ppermute x0 -> x3, waiting for transfers between devices: none -> 6.4 us  [the longest x2 6.4 us: body(): near = lax.ppermute(away, 'z', [(i, i ^ 1) for i in range(NZ)])]
    ppermute x7 -> x6, starting transfers between devices: 23.2 us -> 28 us  [shift_z(): return lax.ppermute(value, 'z', [(i, (i + by) % NZ) for i in range(NZ)])]
    all_gather x1, blocking collectives: 29.8 us -> 27.9 us  [body(): weights = lax.all_gather(shard, 'z', axis=0, tiled=True)]
  transfers between devices with their start and end apart: 14 -> 15, of which waited for: 6 -> 5; matrix products, arithmetic and copies ran while one was open for 0% -> 0% of each run, Pallas kernels for 1% -> 5%
where the time goes in v3:
time: 161 us; the launch traced here: 160 us
  starting transfers between devices  73.9 us (46%)
  blocking collectives  35.2 us (22%)
  waiting for transfers between devices  31.2 us (19%)
  Pallas kernels  13.6 us (8%)
  local copies, waits for them, and re-layouts  5.22 us (3%)
    ppermute x6, starting transfers between devices, shift_z(): return lax.ppermute(value, 'z', [(i, (i + by) % NZ) for i in range(NZ)])  28 us
    all_gather x1, blocking collectives, body(): weights = lax.all_gather(shard, 'z', axis=0, tiled=True)  27.9 us
    ppermute x6, waiting for transfers between devices, shift_z(): return lax.ppermute(value, 'z', [(i, (i + by) % NZ) for i in range(NZ)])  15 us
    pallas_call x12, Pallas kernels, call(): pl.pallas_call(kernel, out_shape=outs, in_specs=specs, out_specs=[pl.Bloc...  13.6 us
    all_to_all x1, starting transfers between devices, body(): home = lax.all_to_all(sums, (*PAIRS, 'yl'), 0, 0).reshape(width, tokens)  10.3 us
    ppermute x3, starting transfers between devices, swap_y(): return lax.ppermute(value, 'yl', [(i, i ^ k) for i in range(NYL)])  9.27 us
    all_to_all x1, starting transfers between devices, body(): spread = lax.all_to_all(branch, PAIRS, 0, 0)  8.53 us
    psum x1, blocking collectives, body(): stats = lax.psum(stats, 'yl')  7.36 us
  transfers between devices with their start and end apart: 15, of which 5 were waited for; matrix products, arithmetic and copies ran while one was open for 0% of the time, Pallas kernels for 5%

profile of v3, /device:TPU:1, one launch (start us, length us, event | category | flops | bytes accessed | tf_op | source)
XLA Modules:
  0.0 160.1 jit_solution(8948604826963075869)
XLA Ops:
  4.5 5.6 %all-to-all-start = ((bf16[4,1408,128]{2,1,0:T(8,128)(2,1)}), bf16[4,1408,128]{2,1,0:T(8,128)(2,1)S(1)}, u32[]{:S(2)}, u32[]{:S(2)}) async-start(bf16[4,1408,128]{2,1,0:T(8,128)(2,1)} %shard_map.102), calls=%async_computation | async-start | bytes 2883584 | tf_op jit(solution)/shard_map/all_to_all | solution.py:232
  10.3 27.9 %all-gather = bf16[1,896,512]{2,1,0:T(8,128)(2,1)S(1)} all-gather(bf16[1,112,512]{2,1,0:T(8,128)(2,1)S(1)} %copy-done.7), channel_id=2, replica_groups=mesh['x'=4,'yh'=2,'c'=2,'z'=8,'yl'=4] {'z'}, dimensions={1}, use_global_device_ids=true | all-gather | bytes 1032192 | tf_op jit(solution)/shard_map/all_gather | solution.py:235
  38.2 5.0 %all-to-all-done.got.refs_1_.refs_0_ = bf16[4,1408,128]{2,1,0:T(8,128)(2,1)S(1)} async-done(((bf16[4,1408,128]{2,1,0:T(8,128)(2,1)}), bf16[4,1408,128]{2,1,0:T(8,128)(2,1)S(1)}, u32[]{:S(2)}, u32[]{:S(2)}) %all-to-all-start) | async-done | bytes 1441824 | tf_op jit(solution)/shard_map/all_to_all | solution.py:232
  43.4 2.4 %shard_map.105 = (bf16[4,7,16,512]{3,2,1,0:T(8,128)(2,1)S(1)}, bf16[4,7,16,512]{3,2,1,0:T(8,128)(2,1)}) custom-call(bf16[4,1408,128]{2,1,0:T(8,128)(2,1)S(1)} %all-to-all-done.got.refs_1_.refs_0_, f32[896,1]{1,0:T(8,128)S(1)} %copy.13.gains.refs_1_), custom_call_target="tpu_custom_call" | custom-call | flops 469762048 | bytes 2362880 | tf_op jit(solution)/shard_map/pallas_call | solution.py:22
  45.8 4.6 %collective-permute-start = (bf16[4,7,16,512]{3,2,1,0:T(8,128)(2,1)}, bf16[4,7,16,512]{3,2,1,0:T(8,128)(2,1)}, u32[]{:S(2)}, u32[]{:S(2)}) collective-permute-start(bf16[4,7,16,512]{3,2,1,0:T(8,128)(2,1)} %get-tuple-element.42), channel_id=1, source_target_pairs={{0,4},{4,0},{8,12},{12,8},{16,20},{20,16},{24,28},{28,24},{1,5},{5... | collective-permute-start | bytes 1376264 | tf_op jit(solution)/shard_map/ppermute | solution.py:247
  52.5 7.4 %psum.7.refs_2_ = f32[2,512]{1,0:T(2,128)S(1)} all-reduce(f32[2,512]{1,0:T(2,128)S(1)} %get-tuple-element.41), channel_id=1, replica_groups=mesh['x'=4,'yh'=2,'c'=2,'z'=8,'yl'=4] {'yl'}, use_global_device_ids=true, to_apply=%region_0.1 | all-reduce | flops 1024 | bytes 8192 | tf_op jit(solution)/shard_map/psum | solution.py:255
  62.5 8.5 %all-to-all-start.1 = ((bf16[8,112,512]{2,1,0:T(8,128)(2,1)}), bf16[8,112,512]{2,1,0:T(8,128)(2,1)S(1)}, u32[]{:S(2)}, u32[]{:S(2)}) async-start(bf16[8,112,512]{2,1,0:T(8,128)(2,1)} %shard_map.104), calls=%async_computation.1 | async-start | bytes 1835008 | tf_op jit(solution)/shard_map/all_to_all | solution.py:263
  72.2 5.8 %collective-permute-start.1 = (bf16[7,16,512]{2,1,0:T(8,128)(2,1)S(1)}, bf16[7,16,512]{2,1,0:T(8,128)(2,1)S(1)}, u32[]{:S(2)}, u32[]{:S(2)}) collective-permute-start(bf16[7,16,512]{2,1,0:T(8,128)(2,1)S(1)} %get-tuple-element.47), channel_id=1, source_target_pairs={{0,8},{4,12},{8,16},{12,20},{16,24},{20,28},{24,0},{28,4},{1,9},{5... | collective-permute-start | bytes 344072 | tf_op jit(solution)/shard_map/ppermute | solution.py:38
  78.0 7.9 %collective-permute-start.2 = (bf16[7,16,512]{2,1,0:T(8,128)(2,1)S(1)}, bf16[7,16,512]{2,1,0:T(8,128)(2,1)S(1)}, u32[]{:S(2)}, u32[]{:S(2)}) collective-permute-start(bf16[7,16,512]{2,1,0:T(8,128)(2,1)S(1)} %get-tuple-element.48), channel_id=1, source_target_pairs={{0,16},{4,20},{8,24},{12,28},{16,0},{20,4},{24,8},{28,12},{1,17},{... | collective-permute-start | bytes 344072 | tf_op jit(solution)/shard_map/ppermute | solution.py:38
  85.9 3.4 %collective-permute-start.3 = (bf16[7,16,512]{2,1,0:T(8,128)(2,1)S(1)}, bf16[7,16,512]{2,1,0:T(8,128)(2,1)S(1)}, u32[]{:S(2)}, u32[]{:S(2)}) collective-permute-start(bf16[7,16,512]{2,1,0:T(8,128)(2,1)S(1)} %get-tuple-element.49), channel_id=1, source_target_pairs={{0,24},{4,28},{8,0},{12,4},{16,8},{20,12},{24,16},{28,20},{1,25},{... | collective-permute-start | bytes 344072 | tf_op jit(solution)/shard_map/ppermute | solution.py:38
  89.3 6.2 %collective-permute-done.3.refs_3_ = bf16[7,16,512]{2,1,0:T(8,128)(2,1)S(1)} collective-permute-done((bf16[7,16,512]{2,1,0:T(8,128)(2,1)S(1)}, bf16[7,16,512]{2,1,0:T(8,128)(2,1)S(1)}, u32[]{:S(2)}, u32[]{:S(2)}) %collective-permute-start.3) | collective-permute-done | bytes 114720 | tf_op jit(solution)/shard_map/ppermute | solution.py:38
  95.9 5.8 %collective-permute-start.4 = (bf16[8,112,512]{2,1,0:T(8,128)(2,1)S(1)}, bf16[8,112,512]{2,1,0:T(8,128)(2,1)S(1)}, u32[]{:S(2)}, u32[]{:S(2)}) collective-permute-start(bf16[8,112,512]{2,1,0:T(8,128)(2,1)S(1)} %shard_map.108), channel_id=1, source_target_pairs={{0,32},{32,0},{1,33},{33,1},{2,34},{34,2},{3,35},{35,3},{4,36},{36... | collective-permute-start | bytes 2752520 | tf_op jit(solution)/shard_map/ppermute | solution.py:42
  101.7 2.8 %collective-permute-start.5 = (bf16[7,16,512]{2,1,0:T(8,128)(2,1)S(1)}, bf16[7,16,512]{2,1,0:T(8,128)(2,1)S(1)}, u32[]{:S(2)}, u32[]{:S(2)}) collective-permute-start(bf16[7,16,512]{2,1,0:T(8,128)(2,1)S(1)} %shard_map.107.refs_0_), channel_id=1, source_target_pairs={{0,1},{1,0},{2,3},{3,2},{4,5},{5,4},{6,7},{7,6},{8,9},{9,8},{10,11... | collective-permute-start | bytes 344072 | tf_op jit(solution)/shard_map/ppermute | solution.py:46
  104.5 1.9 %collective-permute-start.6 = (bf16[7,16,512]{2,1,0:T(8,128)(2,1)S(1)}, bf16[7,16,512]{2,1,0:T(8,128)(2,1)S(1)}, u32[]{:S(2)}, u32[]{:S(2)}) collective-permute-start(bf16[7,16,512]{2,1,0:T(8,128)(2,1)S(1)} %shard_map.107.refs_0_), channel_id=1, source_target_pairs={{0,2},{1,3},{2,0},{3,1},{4,6},{5,7},{6,4},{7,5},{8,10},{9,11},{10,... | collective-permute-start | bytes 344072 | tf_op jit(solution)/shard_map/ppermute | solution.py:46
  106.5 4.5 %collective-permute-start.7 = (bf16[7,16,512]{2,1,0:T(8,128)(2,1)S(1)}, bf16[7,16,512]{2,1,0:T(8,128)(2,1)S(1)}, u32[]{:S(2)}, u32[]{:S(2)}) collective-permute-start(bf16[7,16,512]{2,1,0:T(8,128)(2,1)S(1)} %shard_map.107.refs_0_), channel_id=1, source_target_pairs={{0,3},{1,2},{2,1},{3,0},{4,7},{5,6},{6,5},{7,4},{8,11},{9,10},{10,... | collective-permute-start | bytes 344072 | tf_op jit(solution)/shard_map/ppermute | solution.py:46
  112.2 4.8 %collective-permute-done.6.refs_2_ = bf16[7,16,512]{2,1,0:T(8,128)(2,1)S(1)} collective-permute-done((bf16[7,16,512]{2,1,0:T(8,128)(2,1)S(1)}, bf16[7,16,512]{2,1,0:T(8,128)(2,1)S(1)}, u32[]{:S(2)}, u32[]{:S(2)}) %collective-permute-start.6) | collective-permute-done | bytes 114720 | tf_op jit(solution)/shard_map/ppermute | solution.py:46
  117.1 10.3 %all-to-all-start.2 = ((bf16[32,112,128]{2,1,0:T(8,128)(2,1)}), bf16[32,112,128]{2,1,0:T(8,128)(2,1)S(1)}, u32[]{:S(2)}, u32[]{:S(2)}) async-start(bf16[32,112,128]{2,1,0:T(8,128)(2,1)} %shard_map.109), calls=%async_computation.2 | async-start | bytes 1835008 | tf_op jit(solution)/shard_map/all_to_all | solution.py:273
  128.5 1.9 %collective-permute-start.8 = (bf16[4,64,512]{2,1,0:T(8,128)(2,1)S(1)}, bf16[4,64,512]{2,1,0:T(8,128)(2,1)S(1)}, u32[]{:S(2)}, u32[]{:S(2)}) collective-permute-start(bf16[4,64,512]{2,1,0:T(8,128)(2,1)S(1)} %get-tuple-element.58), channel_id=1, source_target_pairs={{0,4},{4,0},{8,12},{12,8},{16,20},{20,16},{24,28},{28,24},{1,5},{5... | collective-permute-start | bytes 786440 | tf_op jit(solution)/shard_map/ppermute | solution.py:283
  130.4 6.4 %collective-permute-done.8.got = bf16[4,64,512]{2,1,0:T(8,128)(2,1)S(1)} collective-permute-done((bf16[4,64,512]{2,1,0:T(8,128)(2,1)S(1)}, bf16[4,64,512]{2,1,0:T(8,128)(2,1)S(1)}, u32[]{:S(2)}, u32[]{:S(2)}) %collective-permute-start.8) | collective-permute-done | bytes 262176 | tf_op jit(solution)/shard_map/ppermute | solution.py:283
  136.8 4.3 %collective-permute-start.10 = (bf16[2,64,512]{2,1,0:T(8,128)(2,1)S(1)}, bf16[2,64,512]{2,1,0:T(8,128)(2,1)S(1)}, u32[]{:S(2)}, u32[]{:S(2)}) collective-permute-start(bf16[2,64,512]{2,1,0:T(8,128)(2,1)S(1)} %get-tuple-element.61), channel_id=1, source_target_pairs={{0,16},{4,20},{8,24},{12,28},{16,0},{20,4},{24,8},{28,12},{1,17},{... | collective-permute-start | bytes 393224 | tf_op jit(solution)/shard_map/ppermute | solution.py:38
  141.1 4.0 %collective-permute-start.11 = (bf16[2,64,512]{2,1,0:T(8,128)(2,1)S(1)}, bf16[2,64,512]{2,1,0:T(8,128)(2,1)S(1)}, u32[]{:S(2)}, u32[]{:S(2)}) collective-permute-start(bf16[2,64,512]{2,1,0:T(8,128)(2,1)S(1)} %get-tuple-element.62), channel_id=1, source_target_pairs={{0,24},{4,28},{8,0},{12,4},{16,8},{20,12},{24,16},{28,20},{1,25},{... | collective-permute-start | bytes 393224 | tf_op jit(solution)/shard_map/ppermute | solution.py:38
  145.1 2.6 %collective-permute-start.9 = (bf16[2,64,512]{2,1,0:T(8,128)(2,1)S(1)}, bf16[2,64,512]{2,1,0:T(8,128)(2,1)S(1)}, u32[]{:S(2)}, u32[]{:S(2)}) collective-permute-start(bf16[2,64,512]{2,1,0:T(8,128)(2,1)S(1)} %get-tuple-element.60), channel_id=1, source_target_pairs={{0,8},{4,12},{8,16},{12,20},{16,24},{20,28},{24,0},{28,4},{1,9},{5... | collective-permute-start | bytes 393224 | tf_op jit(solution)/shard_map/ppermute | solution.py:38
  147.7 8.8 %collective-permute-done.11.refs_3_ = bf16[2,64,512]{2,1,0:T(8,128)(2,1)S(1)} collective-permute-done((bf16[2,64,512]{2,1,0:T(8,128)(2,1)S(1)}, bf16[2,64,512]{2,1,0:T(8,128)(2,1)S(1)}, u32[]{:S(2)}, u32[]{:S(2)}) %collective-permute-start.11) | collective-permute-done | bytes 131104 | tf_op jit(solution)/shard_map/ppermute | solution.py:38
  156.5 2.3 %shard_map.112 = (bf16[512,512]{1,0:T(8,128)(2,1)}, bf16[512,512]{1,0:T(8,128)(2,1)}, bf16[512,512]{1,0:T(8,128)(2,1)}) custom-call(bf16[2,64,512]{2,1,0:T(8,128)(2,1)S(1)} %get-tuple-element.59.refs_0_, bf16[2,64,512]{2,1,0:T(8,128)(2,1)S(1)} %collective-permute-done.9.refs_1_, bf16[2,64,512]{2,1,0:T(8,128)(2,1)S(1)} %collective-permute-done.10.refs_2_, ...), custom_call_target="tpu_custom_call" | custom-call | flops 1073741824 | bytes 3145728 | tf_op jit(solution)/shard_map/pallas_call | solution.py:22
  (43 shorter events, 14.2 us)
Async XLA Ops:
  0.6 1.2 copy-start.2
  1.8 0.9 copy-start.3
  4.5 5.6 %copy-start.8 = (f32[1,3584]{1,0:T(1,128)S(1)}, f32[1,3584]{1,0:T(1,128)}, u32[]{:S(2)}) copy-start(f32[1,3584]{1,0:T(1,128)} %param.8) | copy-start | bytes 43012
  4.5 5.8 %copy-start.7 = (bf16[1,112,512]{2,1,0:T(8,128)(2,1)S(1)}, bf16[1,112,512]{2,1,0:T(8,128)(2,1)}, u32[]{:S(2)}) copy-start(bf16[1,112,512]{2,1,0:T(8,128)(2,1)} %param.9) | copy-start | bytes 344068
  4.5 38.6 %all-to-all-start = ((bf16[4,1408,128]{2,1,0:T(8,128)(2,1)}), bf16[4,1408,128]{2,1,0:T(8,128)(2,1)S(1)}, u32[]{:S(2)}, u32[]{:S(2)}) async-start(bf16[4,1408,128]{2,1,0:T(8,128)(2,1)} %shard_map.102), calls=%async_computation | async-start | bytes 2883584 | tf_op jit(solution)/shard_map/all_to_all | solution.py:232
  45.8 16.7 %collective-permute-start = (bf16[4,7,16,512]{3,2,1,0:T(8,128)(2,1)}, bf16[4,7,16,512]{3,2,1,0:T(8,128)(2,1)}, u32[]{:S(2)}, u32[]{:S(2)}) collective-permute-start(bf16[4,7,16,512]{3,2,1,0:T(8,128)(2,1)} %get-tuple-element.42), channel_id=1, source_target_pairs={{0,4},{4,0},{8,12},{12,8},{16,20},{20,16},{24,28},{28,24},{1,5},{5... | collective-permute-start | bytes 1376264 | tf_op jit(solution)/shard_map/ppermute | solution.py:247
  51.2 1.3 copy-start
  59.8 1.5 copy-start.1
  62.5 33.1 %all-to-all-start.1 = ((bf16[8,112,512]{2,1,0:T(8,128)(2,1)}), bf16[8,112,512]{2,1,0:T(8,128)(2,1)S(1)}, u32[]{:S(2)}, u32[]{:S(2)}) async-start(bf16[8,112,512]{2,1,0:T(8,128)(2,1)} %shard_map.104), calls=%async_computation.1 | async-start | bytes 1835008 | tf_op jit(solution)/shard_map/all_to_all | solution.py:263
  72.2 17.2 %collective-permute-start.1 = (bf16[7,16,512]{2,1,0:T(8,128)(2,1)S(1)}, bf16[7,16,512]{2,1,0:T(8,128)(2,1)S(1)}, u32[]{:S(2)}, u32[]{:S(2)}) collective-permute-start(bf16[7,16,512]{2,1,0:T(8,128)(2,1)S(1)} %get-tuple-element.47), channel_id=1, source_target_pairs={{0,8},{4,12},{8,16},{12,20},{16,24},{20,28},{24,0},{28,4},{1,9},{5... | collective-permute-start | bytes 344072 | tf_op jit(solution)/shard_map/ppermute | solution.py:38
  78.0 11.4 %collective-permute-start.2 = (bf16[7,16,512]{2,1,0:T(8,128)(2,1)S(1)}, bf16[7,16,512]{2,1,0:T(8,128)(2,1)S(1)}, u32[]{:S(2)}, u32[]{:S(2)}) collective-permute-start(bf16[7,16,512]{2,1,0:T(8,128)(2,1)S(1)} %get-tuple-element.48), channel_id=1, source_target_pairs={{0,16},{4,20},{8,24},{12,28},{16,0},{20,4},{24,8},{28,12},{1,17},{... | collective-permute-start | bytes 344072 | tf_op jit(solution)/shard_map/ppermute | solution.py:38
  85.9 9.6 %collective-permute-start.3 = (bf16[7,16,512]{2,1,0:T(8,128)(2,1)S(1)}, bf16[7,16,512]{2,1,0:T(8,128)(2,1)S(1)}, u32[]{:S(2)}, u32[]{:S(2)}) collective-permute-start(bf16[7,16,512]{2,1,0:T(8,128)(2,1)S(1)} %get-tuple-element.49), channel_id=1, source_target_pairs={{0,24},{4,28},{8,0},{12,4},{16,8},{20,12},{24,16},{28,20},{1,25},{... | collective-permute-start | bytes 344072 | tf_op jit(solution)/shard_map/ppermute | solution.py:38
  95.9 15.1 %collective-permute-start.4 = (bf16[8,112,512]{2,1,0:T(8,128)(2,1)S(1)}, bf16[8,112,512]{2,1,0:T(8,128)(2,1)S(1)}, u32[]{:S(2)}, u32[]{:S(2)}) collective-permute-start(bf16[8,112,512]{2,1,0:T(8,128)(2,1)S(1)} %shard_map.108), channel_id=1, source_target_pairs={{0,32},{32,0},{1,33},{33,1},{2,34},{34,2},{3,35},{35,3},{4,36},{36... | collective-permute-start | bytes 2752520 | tf_op jit(solution)/shard_map/ppermute | solution.py:42
  101.7 10.5 %collective-permute-start.5 = (bf16[7,16,512]{2,1,0:T(8,128)(2,1)S(1)}, bf16[7,16,512]{2,1,0:T(8,128)(2,1)S(1)}, u32[]{:S(2)}, u32[]{:S(2)}) collective-permute-start(bf16[7,16,512]{2,1,0:T(8,128)(2,1)S(1)} %shard_map.107.refs_0_), channel_id=1, source_target_pairs={{0,1},{1,0},{2,3},{3,2},{4,5},{5,4},{6,7},{7,6},{8,9},{9,8},{10,11... | collective-permute-start | bytes 344072 | tf_op jit(solution)/shard_map/ppermute | solution.py:46
  104.5 12.5 %collective-permute-start.6 = (bf16[7,16,512]{2,1,0:T(8,128)(2,1)S(1)}, bf16[7,16,512]{2,1,0:T(8,128)(2,1)S(1)}, u32[]{:S(2)}, u32[]{:S(2)}) collective-permute-start(bf16[7,16,512]{2,1,0:T(8,128)(2,1)S(1)} %shard_map.107.refs_0_), channel_id=1, source_target_pairs={{0,2},{1,3},{2,0},{3,1},{4,6},{5,7},{6,4},{7,5},{8,10},{9,11},{10,... | collective-permute-start | bytes 344072 | tf_op jit(solution)/shard_map/ppermute | solution.py:46
  106.5 10.6 %collective-permute-start.7 = (bf16[7,16,512]{2,1,0:T(8,128)(2,1)S(1)}, bf16[7,16,512]{2,1,0:T(8,128)(2,1)S(1)}, u32[]{:S(2)}, u32[]{:S(2)}) collective-permute-start(bf16[7,16,512]{2,1,0:T(8,128)(2,1)S(1)} %shard_map.107.refs_0_), channel_id=1, source_target_pairs={{0,3},{1,2},{2,1},{3,0},{4,7},{5,6},{6,5},{7,4},{8,11},{9,10},{10,... | collective-permute-start | bytes 344072 | tf_op jit(solution)/shard_map/ppermute | solution.py:46
  112.2 15.1 %copy-start.4 = (s32[1,7]{1,0:T(1,128)S(1)}, s32[1,7]{1,0:T(1,128)}, u32[]{:S(2)}) copy-start(s32[1,7]{1,0:T(1,128)} %owners.1) | copy-start | bytes 88
  112.2 44.3 %copy-start.5 = (bf16[1,1,512,512]{3,2,1,0:T(8,128)(2,1)S(1)}, bf16[1,1,512,512]{3,2,1,0:T(8,128)(2,1)}, u32[]{:S(2)}) copy-start(bf16[1,1,512,512]{3,2,1,0:T(8,128)(2,1)} %param.12) | copy-start | bytes 1572868
  112.2 44.3 %copy-start.6 = (bf16[1,1,512,512]{3,2,1,0:T(8,128)(2,1)S(1)}, bf16[1,1,512,512]{3,2,1,0:T(8,128)(2,1)}, u32[]{:S(2)}) copy-start(bf16[1,1,512,512]{3,2,1,0:T(8,128)(2,1)} %param.13) | copy-start | bytes 1572868
  117.1 41.8 %all-to-all-start.2 = ((bf16[32,112,128]{2,1,0:T(8,128)(2,1)}), bf16[32,112,128]{2,1,0:T(8,128)(2,1)S(1)}, u32[]{:S(2)}, u32[]{:S(2)}) async-start(bf16[32,112,128]{2,1,0:T(8,128)(2,1)} %shard_map.109), calls=%async_computation.2 | async-start | bytes 1835008 | tf_op jit(solution)/shard_map/all_to_all | solution.py:273
  128.5 8.3 %collective-permute-start.8 = (bf16[4,64,512]{2,1,0:T(8,128)(2,1)S(1)}, bf16[4,64,512]{2,1,0:T(8,128)(2,1)S(1)}, u32[]{:S(2)}, u32[]{:S(2)}) collective-permute-start(bf16[4,64,512]{2,1,0:T(8,128)(2,1)S(1)} %get-tuple-element.58), channel_id=1, source_target_pairs={{0,4},{4,0},{8,12},{12,8},{16,20},{20,16},{24,28},{28,24},{1,5},{5... | collective-permute-start | bytes 786440 | tf_op jit(solution)/shard_map/ppermute | solution.py:283
  136.8 10.9 %collective-permute-start.10 = (bf16[2,64,512]{2,1,0:T(8,128)(2,1)S(1)}, bf16[2,64,512]{2,1,0:T(8,128)(2,1)S(1)}, u32[]{:S(2)}, u32[]{:S(2)}) collective-permute-start(bf16[2,64,512]{2,1,0:T(8,128)(2,1)S(1)} %get-tuple-element.61), channel_id=1, source_target_pairs={{0,16},{4,20},{8,24},{12,28},{16,0},{20,4},{24,8},{28,12},{1,17},{... | collective-permute-start | bytes 393224 | tf_op jit(solution)/shard_map/ppermute | solution.py:38
  141.1 15.4 %collective-permute-start.11 = (bf16[2,64,512]{2,1,0:T(8,128)(2,1)S(1)}, bf16[2,64,512]{2,1,0:T(8,128)(2,1)S(1)}, u32[]{:S(2)}, u32[]{:S(2)}) collective-permute-start(bf16[2,64,512]{2,1,0:T(8,128)(2,1)S(1)} %get-tuple-element.62), channel_id=1, source_target_pairs={{0,24},{4,28},{8,0},{12,4},{16,8},{20,12},{24,16},{28,20},{1,25},{... | collective-permute-start | bytes 393224 | tf_op jit(solution)/shard_map/ppermute | solution.py:38
  145.1 11.4 %collective-permute-start.9 = (bf16[2,64,512]{2,1,0:T(8,128)(2,1)S(1)}, bf16[2,64,512]{2,1,0:T(8,128)(2,1)S(1)}, u32[]{:S(2)}, u32[]{:S(2)}) collective-permute-start(bf16[2,64,512]{2,1,0:T(8,128)(2,1)S(1)} %get-tuple-element.60), channel_id=1, source_target_pairs={{0,8},{4,12},{8,16},{12,20},{16,24},{20,28},{24,0},{28,4},{1,9},{5... | collective-permute-start | bytes 393224 | tf_op jit(solution)/shard_map/ppermute | solution.py:38

commit v4 on v3

--- a/solution.py
+++ b/solution.py
@@ -97,37 +97,48 @@
             out[k // 2, i] = held[pl.ds(pl.multiple_of(z * rows + i * GROUP, GROUP), GROUP), :]
 
 
-def back_kernel(got, weights, gains, scaled, stats, shared):
+def load_shared(got, width, shared):
+    tokens = got.shape[2]
+    for t in range(NYL):
+        shared[:, t * tokens : (t + 1) * tokens] = got[t, width:, :]
+    return shared[...]
+
+
+def stats_kernel(got, weights, gains, stats, shared):
     tokens = got.shape[2]
     width = weights.shape[0]
     rows = width // NZ
-    for t in range(NYL):
-        shared[:, t * tokens : (t + 1) * tokens] = got[t, width:, :]
-    up = shared[...]
+    up = load_shared(got, width, shared)
     cross = [jnp.zeros((1, tokens), F32) for _ in range(NYL)]
     square = [jnp.zeros((1, tokens), F32) for _ in range(NYL)]
     for z in range(NZ):
         at = slice(z * rows, (z + 1) * rows)
         value = dot(weights[at, :], up, ((1,), (0,))) * gains[at, :]
-        scaled[at, :] = value
         for t in range(NYL):
             wide = got[t, at, :].astype(F32)
             cross[t] = cross[t] + jnp.sum(value[:, t * tokens : (t + 1) * tokens] * wide, axis=0, keepdims=True)
             square[t] = square[t] + jnp.sum(wide * wide, axis=0, keepdims=True)
     for t in range(NYL):
-        stats[0:1, t * tokens : (t + 1) * tokens] = cross[t]
-        stats[1:2, t * tokens : (t + 1) * tokens] = square[t]
-
-
-def branch_kernel(full, scaled, got, stats, out):
-    pull = stats[0:1, :] / full / (stats[1:2, :] / full + norm_eps)
+        to = slice(t * tokens, (t + 1) * tokens)
+        for copy in range(NYL):
+            stats[copy, 0:1, to] = cross[t]
+            stats[copy, 1:2, to] = square[t]
+
+
+def branch_kernel(full, got, weights, gains, stats, out, shared):
+    total = stats[0]
+    for k in range(1, NYL):
+        total = total + stats[k]
+    pull = total[0:1, :] / full / (total[1:2, :] / full + norm_eps)
     tokens = got.shape[2]
     rows = out.shape[1]
+    up = load_shared(got, weights.shape[0], shared)
     for i in range(NPAIR):
         at = slice(i * rows, (i + 1) * rows)
+        value = dot(weights[at, :], up, ((1,), (0,))) * gains[at, :]
         for t in range(NYL):
             to = slice(t * tokens, (t + 1) * tokens)
-            out[i, :, to] = (scaled[at, to] - got[t, at, :].astype(F32) * pull[:, to]).astype(BF16)
+            out[i, :, to] = (value[:, to] - got[t, at, :].astype(F32) * pull[:, to]).astype(BF16)
 
 
 def suffix_kernel(spread, out):
@@ -245,18 +256,21 @@
     )
 
     near = lax.ppermute(away, "z", [(i, i ^ 1) for i in range(NZ)])
-    scaled, stats = call(
-        back_kernel,
-        [shape(quarter, line, dtype=F32), shape(2, line, dtype=F32)],
+    got, away = tie(got, away)
+    (stats,) = call(
+        stats_kernel,
+        [shape(NYL, 2, line, dtype=F32)],
         [got, weights, gains],
         scratch=[pltpu.VMEM((keys, line), BF16)],
         flops=2 * quarter * line * keys,
     )
-    stats = lax.psum(stats, "yl")
+    stats = lax.all_to_all(stats, "yl", 0, 0)
     (branch,) = call(
         lambda *refs: branch_kernel(width, *refs),
         [shape(NPAIR, quarter // NPAIR, line)],
-        [scaled, got, stats],
+        [got, weights, gains, stats],
+        scratch=[pltpu.VMEM((keys, line), BF16)],
+        flops=2 * quarter * line * keys,
     )
     branch, near = tie(branch, near)
 

time: 161 us -> 158 us (0.981)
  Pallas kernels: 13.6 us -> 11.4 us
    psum x1 -> x0, blocking collectives: 7.36 us -> none  [body(): stats = lax.psum(stats, 'yl')]
    all_to_all x0 -> x1, blocking collectives: none -> 6.81 us  [body(): stats = lax.all_to_all(stats, 'yl', 0, 0)]
    pallas_call x12, Pallas kernels: 13.6 us -> 11.4 us  [call(): pl.pallas_call(kernel, out_shape=outs, in_specs=specs, out_specs=[pl.Bloc...]
    ppermute x6, waiting for transfers between devices: 15 us -> 16.8 us  [shift_z(): return lax.ppermute(value, 'z', [(i, (i + by) % NZ) for i in range(NZ)])]
    unnamed x18 -> x20, local copies, waits for them, and re-layouts: 4.84 us -> 4.79 us
  transfers between devices with their start and end apart: 15 -> 15, of which waited for: 5 -> 6; matrix products, arithmetic and copies ran while one was open for 0% -> 0% of each run, Pallas kernels for 5% -> 4%
where the time goes in v4:
time: 158 us
  starting transfers between devices  72.6 us (46%)
  blocking collectives  34.7 us (22%)
  waiting for transfers between devices  32.8 us (21%)
  Pallas kernels  11.4 us (7%)
  local copies, waits for them, and re-layouts  5.17 us (3%)
    ppermute x6, starting transfers between devices, shift_z(): return lax.ppermute(value, 'z', [(i, (i + by) % NZ) for i in range(NZ)])  29.1 us
    all_gather x1, blocking collectives, body(): weights = lax.all_gather(shard, 'z', axis=0, tiled=True)  27.9 us
    ppermute x6, waiting for transfers between devices, shift_z(): return lax.ppermute(value, 'z', [(i, (i + by) % NZ) for i in range(NZ)])  16.8 us
    pallas_call x12, Pallas kernels, call(): pl.pallas_call(kernel, out_shape=outs, in_specs=specs, out_specs=[pl.Bloc...  11.4 us
    ppermute x3, starting transfers between devices, swap_y(): return lax.ppermute(value, 'yl', [(i, i ^ k) for i in range(NYL)])  9.27 us
    all_to_all x1, starting transfers between devices, body(): home = lax.all_to_all(sums, (*PAIRS, 'yl'), 0, 0).reshape(width, tokens)  9.24 us
    all_to_all x1, starting transfers between devices, body(): spread = lax.all_to_all(branch, PAIRS, 0, 0)  8.24 us
    all_to_all x1, blocking collectives, body(): stats = lax.all_to_all(stats, 'yl', 0, 0)  6.81 us
  transfers between devices with their start and end apart: 15, of which 6 were waited for; matrix products, arithmetic and copies ran while one was open for 0% of the time, Pallas kernels for 4%

profile of v4, /device:TPU:1, one launch (start us, length us, event | category | flops | bytes accessed | tf_op | source)
XLA Modules:
  0.0 157.6 jit_solution(8445414340798833902)
XLA Ops:
  4.5 5.6 %all-to-all-start = ((bf16[4,1408,128]{2,1,0:T(8,128)(2,1)}), bf16[4,1408,128]{2,1,0:T(8,128)(2,1)S(1)}, u32[]{:S(2)}, u32[]{:S(2)}) async-start(bf16[4,1408,128]{2,1,0:T(8,128)(2,1)} %shard_map.102), calls=%async_computation | async-start | bytes 2883584 | tf_op jit(solution)/shard_map/all_to_all | solution.py:243
  10.3 27.9 %all-gather = bf16[1,896,512]{2,1,0:T(8,128)(2,1)S(1)} all-gather(bf16[1,112,512]{2,1,0:T(8,128)(2,1)S(1)} %copy-done.8), channel_id=2, replica_groups=mesh['x'=4,'yh'=2,'c'=2,'z'=8,'yl'=4] {'z'}, dimensions={1}, use_global_device_ids=true | all-gather | bytes 1032192 | tf_op jit(solution)/shard_map/all_gather | solution.py:246
  38.2 5.0 %all-to-all-done.refs_0_.got = bf16[4,1408,128]{2,1,0:T(8,128)(2,1)S(1)} async-done(((bf16[4,1408,128]{2,1,0:T(8,128)(2,1)}), bf16[4,1408,128]{2,1,0:T(8,128)(2,1)S(1)}, u32[]{:S(2)}, u32[]{:S(2)}) %all-to-all-start) | async-done | bytes 1441824 | tf_op jit(solution)/shard_map/all_to_all | solution.py:243
  45.0 4.6 %collective-permute-start = (bf16[4,7,16,512]{3,2,1,0:T(8,128)(2,1)S(1)}, bf16[4,7,16,512]{3,2,1,0:T(8,128)(2,1)S(1)}, u32[]{:S(2)}, u32[]{:S(2)}) collective-permute-start(bf16[4,7,16,512]{3,2,1,0:T(8,128)(2,1)S(1)} %get-tuple-element.38), channel_id=1, source_target_pairs={{0,4},{4,0},{8,12},{12,8},{16,20},{20,16},{24,28},{28,24},{1,5},{5... | collective-permute-start | bytes 1376264 | tf_op jit(solution)/shard_map/ppermute | solution.py:258
  50.4 6.8 %all_to_all.20.refs_3_ = f32[4,2,512]{2,1,0:T(2,128)S(1)} all-to-all(f32[4,2,512]{2,1,0:T(2,128)S(1)} %shard_map.104), channel_id=1, replica_groups=mesh['x'=4,'yh'=2,'c'=2,'z'=8,'yl'=4] {'yl'}, dimensions={0} | all-to-all | bytes 32768 | tf_op jit(solution)/shard_map/all_to_all | solution.py:267
  59.8 8.2 %all-to-all-start.2 = ((bf16[8,112,512]{2,1,0:T(8,128)(2,1)}), bf16[8,112,512]{2,1,0:T(8,128)(2,1)S(1)}, u32[]{:S(2)}, u32[]{:S(2)}) async-start(bf16[8,112,512]{2,1,0:T(8,128)(2,1)} %copy-done), calls=%async_computation.2 | async-start | bytes 1835008 | tf_op jit(solution)/shard_map/all_to_all | solution.py:277
  69.1 5.8 %collective-permute-start.1 = (bf16[7,16,512]{2,1,0:T(8,128)(2,1)S(1)}, bf16[7,16,512]{2,1,0:T(8,128)(2,1)S(1)}, u32[]{:S(2)}, u32[]{:S(2)}) collective-permute-start(bf16[7,16,512]{2,1,0:T(8,128)(2,1)S(1)} %get-tuple-element.45), channel_id=1, source_target_pairs={{0,8},{4,12},{8,16},{12,20},{16,24},{20,28},{24,0},{28,4},{1,9},{5... | collective-permute-start | bytes 344072 | tf_op jit(solution)/shard_map/ppermute | solution.py:38
  75.0 7.9 %collective-permute-start.2 = (bf16[7,16,512]{2,1,0:T(8,128)(2,1)S(1)}, bf16[7,16,512]{2,1,0:T(8,128)(2,1)S(1)}, u32[]{:S(2)}, u32[]{:S(2)}) collective-permute-start(bf16[7,16,512]{2,1,0:T(8,128)(2,1)S(1)} %get-tuple-element.46), channel_id=1, source_target_pairs={{0,16},{4,20},{8,24},{12,28},{16,0},{20,4},{24,8},{28,12},{1,17},{... | collective-permute-start | bytes 344072 | tf_op jit(solution)/shard_map/ppermute | solution.py:38
  82.9 3.4 %collective-permute-start.3 = (bf16[7,16,512]{2,1,0:T(8,128)(2,1)S(1)}, bf16[7,16,512]{2,1,0:T(8,128)(2,1)S(1)}, u32[]{:S(2)}, u32[]{:S(2)}) collective-permute-start(bf16[7,16,512]{2,1,0:T(8,128)(2,1)S(1)} %get-tuple-element.47), channel_id=1, source_target_pairs={{0,24},{4,28},{8,0},{12,4},{16,8},{20,12},{24,16},{28,20},{1,25},{... | collective-permute-start | bytes 344072 | tf_op jit(solution)/shard_map/ppermute | solution.py:38
  86.3 6.9 %collective-permute-done.3.refs_3_ = bf16[7,16,512]{2,1,0:T(8,128)(2,1)S(1)} collective-permute-done((bf16[7,16,512]{2,1,0:T(8,128)(2,1)S(1)}, bf16[7,16,512]{2,1,0:T(8,128)(2,1)S(1)}, u32[]{:S(2)}, u32[]{:S(2)}) %collective-permute-start.3) | collective-permute-done | bytes 114720 | tf_op jit(solution)/shard_map/ppermute | solution.py:38
  93.6 4.6 %collective-permute-start.4 = (bf16[8,112,512]{2,1,0:T(8,128)(2,1)S(1)}, bf16[8,112,512]{2,1,0:T(8,128)(2,1)S(1)}, u32[]{:S(2)}, u32[]{:S(2)}) collective-permute-start(bf16[8,112,512]{2,1,0:T(8,128)(2,1)S(1)} %shard_map.108), channel_id=1, source_target_pairs={{0,32},{32,0},{1,33},{33,1},{2,34},{34,2},{3,35},{35,3},{4,36},{36... | collective-permute-start | bytes 2752520 | tf_op jit(solution)/shard_map/ppermute | solution.py:42
  98.3 3.0 %collective-permute-start.7 = (bf16[7,16,512]{2,1,0:T(8,128)(2,1)S(1)}, bf16[7,16,512]{2,1,0:T(8,128)(2,1)S(1)}, u32[]{:S(2)}, u32[]{:S(2)}) collective-permute-start(bf16[7,16,512]{2,1,0:T(8,128)(2,1)S(1)} %shard_map.107.refs_0_), channel_id=1, source_target_pairs={{0,3},{1,2},{2,1},{3,0},{4,7},{5,6},{6,5},{7,4},{8,11},{9,10},{10,... | collective-permute-start | bytes 344072 | tf_op jit(solution)/shard_map/ppermute | solution.py:46
  101.2 3.4 %collective-permute-start.6 = (bf16[7,16,512]{2,1,0:T(8,128)(2,1)S(1)}, bf16[7,16,512]{2,1,0:T(8,128)(2,1)S(1)}, u32[]{:S(2)}, u32[]{:S(2)}) collective-permute-start(bf16[7,16,512]{2,1,0:T(8,128)(2,1)S(1)} %shard_map.107.refs_0_), channel_id=1, source_target_pairs={{0,2},{1,3},{2,0},{3,1},{4,6},{5,7},{6,4},{7,5},{8,10},{9,11},{10,... | collective-permute-start | bytes 344072 | tf_op jit(solution)/shard_map/ppermute | solution.py:46
  104.6 2.9 %collective-permute-start.5 = (bf16[7,16,512]{2,1,0:T(8,128)(2,1)S(1)}, bf16[7,16,512]{2,1,0:T(8,128)(2,1)S(1)}, u32[]{:S(2)}, u32[]{:S(2)}) collective-permute-start(bf16[7,16,512]{2,1,0:T(8,128)(2,1)S(1)} %shard_map.107.refs_0_), channel_id=1, source_target_pairs={{0,1},{1,0},{2,3},{3,2},{4,5},{5,4},{6,7},{7,6},{8,9},{9,8},{10,11... | collective-permute-start | bytes 344072 | tf_op jit(solution)/shard_map/ppermute | solution.py:46
  108.8 4.6 %collective-permute-done.6.refs_2_ = bf16[7,16,512]{2,1,0:T(8,128)(2,1)S(1)} collective-permute-done((bf16[7,16,512]{2,1,0:T(8,128)(2,1)S(1)}, bf16[7,16,512]{2,1,0:T(8,128)(2,1)S(1)}, u32[]{:S(2)}, u32[]{:S(2)}) %collective-permute-start.6) | collective-permute-done | bytes 114720 | tf_op jit(solution)/shard_map/ppermute | solution.py:46
  113.4 9.2 %all-to-all-start.3 = ((bf16[32,112,128]{2,1,0:T(8,128)(2,1)}), bf16[32,112,128]{2,1,0:T(8,128)(2,1)S(1)}, u32[]{:S(2)}, u32[]{:S(2)}) async-start(bf16[32,112,128]{2,1,0:T(8,128)(2,1)} %shard_map.109), calls=%async_computation.3 | async-start | bytes 1835008 | tf_op jit(solution)/shard_map/all_to_all | solution.py:287
  123.8 1.9 %collective-permute-start.8 = (bf16[4,64,512]{2,1,0:T(8,128)(2,1)S(1)}, bf16[4,64,512]{2,1,0:T(8,128)(2,1)S(1)}, u32[]{:S(2)}, u32[]{:S(2)}) collective-permute-start(bf16[4,64,512]{2,1,0:T(8,128)(2,1)S(1)} %get-tuple-element.56), channel_id=1, source_target_pairs={{0,4},{4,0},{8,12},{12,8},{16,20},{20,16},{24,28},{28,24},{1,5},{5... | collective-permute-start | bytes 786440 | tf_op jit(solution)/shard_map/ppermute | solution.py:297
  125.7 6.4 %collective-permute-done.8.got = bf16[4,64,512]{2,1,0:T(8,128)(2,1)S(1)} collective-permute-done((bf16[4,64,512]{2,1,0:T(8,128)(2,1)S(1)}, bf16[4,64,512]{2,1,0:T(8,128)(2,1)S(1)}, u32[]{:S(2)}, u32[]{:S(2)}) %collective-permute-start.8) | collective-permute-done | bytes 262176 | tf_op jit(solution)/shard_map/ppermute | solution.py:297
  132.1 3.2 %collective-permute-start.9 = (bf16[2,64,512]{2,1,0:T(8,128)(2,1)S(1)}, bf16[2,64,512]{2,1,0:T(8,128)(2,1)S(1)}, u32[]{:S(2)}, u32[]{:S(2)}) collective-permute-start(bf16[2,64,512]{2,1,0:T(8,128)(2,1)S(1)} %get-tuple-element.58), channel_id=1, source_target_pairs={{0,8},{4,12},{8,16},{12,20},{16,24},{20,28},{24,0},{28,4},{1,9},{5... | collective-permute-start | bytes 393224 | tf_op jit(solution)/shard_map/ppermute | solution.py:38
  135.4 5.5 %collective-permute-start.10 = (bf16[2,64,512]{2,1,0:T(8,128)(2,1)S(1)}, bf16[2,64,512]{2,1,0:T(8,128)(2,1)S(1)}, u32[]{:S(2)}, u32[]{:S(2)}) collective-permute-start(bf16[2,64,512]{2,1,0:T(8,128)(2,1)S(1)} %get-tuple-element.59), channel_id=1, source_target_pairs={{0,16},{4,20},{8,24},{12,28},{16,0},{20,4},{24,8},{28,12},{1,17},{... | collective-permute-start | bytes 393224 | tf_op jit(solution)/shard_map/ppermute | solution.py:38
  140.9 3.3 %collective-permute-start.11 = (bf16[2,64,512]{2,1,0:T(8,128)(2,1)S(1)}, bf16[2,64,512]{2,1,0:T(8,128)(2,1)S(1)}, u32[]{:S(2)}, u32[]{:S(2)}) collective-permute-start(bf16[2,64,512]{2,1,0:T(8,128)(2,1)S(1)} %get-tuple-element.60), channel_id=1, source_target_pairs={{0,24},{4,28},{8,0},{12,4},{16,8},{20,12},{24,16},{28,20},{1,25},{... | collective-permute-start | bytes 393224 | tf_op jit(solution)/shard_map/ppermute | solution.py:38
  144.2 4.1 %collective-permute-done.10.refs_2_ = bf16[2,64,512]{2,1,0:T(8,128)(2,1)S(1)} collective-permute-done((bf16[2,64,512]{2,1,0:T(8,128)(2,1)S(1)}, bf16[2,64,512]{2,1,0:T(8,128)(2,1)S(1)}, u32[]{:S(2)}, u32[]{:S(2)}) %collective-permute-start.10) | collective-permute-done | bytes 131104 | tf_op jit(solution)/shard_map/ppermute | solution.py:38
  148.3 5.8 %collective-permute-done.11.refs_3_ = bf16[2,64,512]{2,1,0:T(8,128)(2,1)S(1)} collective-permute-done((bf16[2,64,512]{2,1,0:T(8,128)(2,1)S(1)}, bf16[2,64,512]{2,1,0:T(8,128)(2,1)S(1)}, u32[]{:S(2)}, u32[]{:S(2)}) %collective-permute-start.11) | collective-permute-done | bytes 131104 | tf_op jit(solution)/shard_map/ppermute | solution.py:38
  154.1 2.3 %shard_map.112 = (bf16[512,512]{1,0:T(8,128)(2,1)}, bf16[512,512]{1,0:T(8,128)(2,1)}, bf16[512,512]{1,0:T(8,128)(2,1)}) custom-call(bf16[2,64,512]{2,1,0:T(8,128)(2,1)S(1)} %get-tuple-element.57.refs_0_, bf16[2,64,512]{2,1,0:T(8,128)(2,1)S(1)} %collective-permute-done.9.refs_1_, bf16[2,64,512]{2,1,0:T(8,128)(2,1)S(1)} %collective-permute-done.10.refs_2_, ...), custom_call_target="tpu_custom_call" | custom-call | flops 1073741824 | bytes 3145728 | tf_op jit(solution)/shard_map/pallas_call | solution.py:22
  (45 shorter events, 14.4 us)
Async XLA Ops:
  0.6 1.2 copy-start.1
  1.8 0.9 copy-start.4
  4.5 5.6 %copy-start.9 = (f32[1,3584]{1,0:T(1,128)S(1)}, f32[1,3584]{1,0:T(1,128)}, u32[]{:S(2)}) copy-start(f32[1,3584]{1,0:T(1,128)} %param.8) | copy-start | bytes 43012
  4.5 5.8 %copy-start.8 = (bf16[1,112,512]{2,1,0:T(8,128)(2,1)S(1)}, bf16[1,112,512]{2,1,0:T(8,128)(2,1)}, u32[]{:S(2)}) copy-start(bf16[1,112,512]{2,1,0:T(8,128)(2,1)} %param.9) | copy-start | bytes 344068
  4.5 38.6 %all-to-all-start = ((bf16[4,1408,128]{2,1,0:T(8,128)(2,1)}), bf16[4,1408,128]{2,1,0:T(8,128)(2,1)S(1)}, u32[]{:S(2)}, u32[]{:S(2)}) async-start(bf16[4,1408,128]{2,1,0:T(8,128)(2,1)} %shard_map.102), calls=%async_computation | async-start | bytes 2883584 | tf_op jit(solution)/shard_map/all_to_all | solution.py:243
  45.0 14.0 %collective-permute-start = (bf16[4,7,16,512]{3,2,1,0:T(8,128)(2,1)S(1)}, bf16[4,7,16,512]{3,2,1,0:T(8,128)(2,1)S(1)}, u32[]{:S(2)}, u32[]{:S(2)}) collective-permute-start(bf16[4,7,16,512]{3,2,1,0:T(8,128)(2,1)S(1)} %get-tuple-element.38), channel_id=1, source_target_pairs={{0,4},{4,0},{8,12},{12,8},{16,20},{20,16},{24,28},{28,24},{1,5},{5... | collective-permute-start | bytes 1376264 | tf_op jit(solution)/shard_map/ppermute | solution.py:258
  58.1 0.9 copy-start
  59.8 33.5 %all-to-all-start.2 = ((bf16[8,112,512]{2,1,0:T(8,128)(2,1)}), bf16[8,112,512]{2,1,0:T(8,128)(2,1)S(1)}, u32[]{:S(2)}, u32[]{:S(2)}) async-start(bf16[8,112,512]{2,1,0:T(8,128)(2,1)} %copy-done), calls=%async_computation.2 | async-start | bytes 1835008 | tf_op jit(solution)/shard_map/all_to_all | solution.py:277
  68.0 1.0 copy-start.3
  69.1 17.2 %collective-permute-start.1 = (bf16[7,16,512]{2,1,0:T(8,128)(2,1)S(1)}, bf16[7,16,512]{2,1,0:T(8,128)(2,1)S(1)}, u32[]{:S(2)}, u32[]{:S(2)}) collective-permute-start(bf16[7,16,512]{2,1,0:T(8,128)(2,1)S(1)} %get-tuple-element.45), channel_id=1, source_target_pairs={{0,8},{4,12},{8,16},{12,20},{16,24},{20,28},{24,0},{28,4},{1,9},{5... | collective-permute-start | bytes 344072 | tf_op jit(solution)/shard_map/ppermute | solution.py:38
  75.0 11.4 %collective-permute-start.2 = (bf16[7,16,512]{2,1,0:T(8,128)(2,1)S(1)}, bf16[7,16,512]{2,1,0:T(8,128)(2,1)S(1)}, u32[]{:S(2)}, u32[]{:S(2)}) collective-permute-start(bf16[7,16,512]{2,1,0:T(8,128)(2,1)S(1)} %get-tuple-element.46), channel_id=1, source_target_pairs={{0,16},{4,20},{8,24},{12,28},{16,0},{20,4},{24,8},{28,12},{1,17},{... | collective-permute-start | bytes 344072 | tf_op jit(solution)/shard_map/ppermute | solution.py:38
  82.9 10.3 %collective-permute-start.3 = (bf16[7,16,512]{2,1,0:T(8,128)(2,1)S(1)}, bf16[7,16,512]{2,1,0:T(8,128)(2,1)S(1)}, u32[]{:S(2)}, u32[]{:S(2)}) collective-permute-start(bf16[7,16,512]{2,1,0:T(8,128)(2,1)S(1)} %get-tuple-element.47), channel_id=1, source_target_pairs={{0,24},{4,28},{8,0},{12,4},{16,8},{20,12},{24,16},{28,20},{1,25},{... | collective-permute-start | bytes 344072 | tf_op jit(solution)/shard_map/ppermute | solution.py:38
  93.6 13.9 %collective-permute-start.4 = (bf16[8,112,512]{2,1,0:T(8,128)(2,1)S(1)}, bf16[8,112,512]{2,1,0:T(8,128)(2,1)S(1)}, u32[]{:S(2)}, u32[]{:S(2)}) collective-permute-start(bf16[8,112,512]{2,1,0:T(8,128)(2,1)S(1)} %shard_map.108), channel_id=1, source_target_pairs={{0,32},{32,0},{1,33},{33,1},{2,34},{34,2},{3,35},{35,3},{4,36},{36... | collective-permute-start | bytes 2752520 | tf_op jit(solution)/shard_map/ppermute | solution.py:42
  98.3 10.5 %collective-permute-start.7 = (bf16[7,16,512]{2,1,0:T(8,128)(2,1)S(1)}, bf16[7,16,512]{2,1,0:T(8,128)(2,1)S(1)}, u32[]{:S(2)}, u32[]{:S(2)}) collective-permute-start(bf16[7,16,512]{2,1,0:T(8,128)(2,1)S(1)} %shard_map.107.refs_0_), channel_id=1, source_target_pairs={{0,3},{1,2},{2,1},{3,0},{4,7},{5,6},{6,5},{7,4},{8,11},{9,10},{10,... | collective-permute-start | bytes 344072 | tf_op jit(solution)/shard_map/ppermute | solution.py:46
  101.2 12.2 %collective-permute-start.6 = (bf16[7,16,512]{2,1,0:T(8,128)(2,1)S(1)}, bf16[7,16,512]{2,1,0:T(8,128)(2,1)S(1)}, u32[]{:S(2)}, u32[]{:S(2)}) collective-permute-start(bf16[7,16,512]{2,1,0:T(8,128)(2,1)S(1)} %shard_map.107.refs_0_), channel_id=1, source_target_pairs={{0,2},{1,3},{2,0},{3,1},{4,6},{5,7},{6,4},{7,5},{8,10},{9,11},{10,... | collective-permute-start | bytes 344072 | tf_op jit(solution)/shard_map/ppermute | solution.py:46
  104.6 8.8 %collective-permute-start.5 = (bf16[7,16,512]{2,1,0:T(8,128)(2,1)S(1)}, bf16[7,16,512]{2,1,0:T(8,128)(2,1)S(1)}, u32[]{:S(2)}, u32[]{:S(2)}) collective-permute-start(bf16[7,16,512]{2,1,0:T(8,128)(2,1)S(1)} %shard_map.107.refs_0_), channel_id=1, source_target_pairs={{0,1},{1,0},{2,3},{3,2},{4,5},{5,4},{6,7},{7,6},{8,9},{9,8},{10,11... | collective-permute-start | bytes 344072 | tf_op jit(solution)/shard_map/ppermute | solution.py:46
  108.8 13.9 %copy-start.5 = (s32[1,7]{1,0:T(1,128)S(1)}, s32[1,7]{1,0:T(1,128)}, u32[]{:S(2)}) copy-start(s32[1,7]{1,0:T(1,128)} %owners.1) | copy-start | bytes 88
  108.8 45.3 %copy-start.6 = (bf16[1,1,512,512]{3,2,1,0:T(8,128)(2,1)S(1)}, bf16[1,1,512,512]{3,2,1,0:T(8,128)(2,1)}, u32[]{:S(2)}) copy-start(bf16[1,1,512,512]{3,2,1,0:T(8,128)(2,1)} %param.12) | copy-start | bytes 1572868
  108.8 45.3 %copy-start.7 = (bf16[1,1,512,512]{3,2,1,0:T(8,128)(2,1)S(1)}, bf16[1,1,512,512]{3,2,1,0:T(8,128)(2,1)}, u32[]{:S(2)}) copy-start(bf16[1,1,512,512]{3,2,1,0:T(8,128)(2,1)} %param.13) | copy-start | bytes 1572868
  113.4 43.0 %all-to-all-start.3 = ((bf16[32,112,128]{2,1,0:T(8,128)(2,1)}), bf16[32,112,128]{2,1,0:T(8,128)(2,1)S(1)}, u32[]{:S(2)}, u32[]{:S(2)}) async-start(bf16[32,112,128]{2,1,0:T(8,128)(2,1)} %shard_map.109), calls=%async_computation.3 | async-start | bytes 1835008 | tf_op jit(solution)/shard_map/all_to_all | solution.py:287
  123.8 8.3 %collective-permute-start.8 = (bf16[4,64,512]{2,1,0:T(8,128)(2,1)S(1)}, bf16[4,64,512]{2,1,0:T(8,128)(2,1)S(1)}, u32[]{:S(2)}, u32[]{:S(2)}) collective-permute-start(bf16[4,64,512]{2,1,0:T(8,128)(2,1)S(1)} %get-tuple-element.56), channel_id=1, source_target_pairs={{0,4},{4,0},{8,12},{12,8},{16,20},{20,16},{24,28},{28,24},{1,5},{5... | collective-permute-start | bytes 786440 | tf_op jit(solution)/shard_map/ppermute | solution.py:297
  132.1 12.0 %collective-permute-start.9 = (bf16[2,64,512]{2,1,0:T(8,128)(2,1)S(1)}, bf16[2,64,512]{2,1,0:T(8,128)(2,1)S(1)}, u32[]{:S(2)}, u32[]{:S(2)}) collective-permute-start(bf16[2,64,512]{2,1,0:T(8,128)(2,1)S(1)} %get-tuple-element.58), channel_id=1, source_target_pairs={{0,8},{4,12},{8,16},{12,20},{16,24},{20,28},{24,0},{28,4},{1,9},{5... | collective-permute-start | bytes 393224 | tf_op jit(solution)/shard_map/ppermute | solution.py:38
  135.4 12.9 %collective-permute-start.10 = (bf16[2,64,512]{2,1,0:T(8,128)(2,1)S(1)}, bf16[2,64,512]{2,1,0:T(8,128)(2,1)S(1)}, u32[]{:S(2)}, u32[]{:S(2)}) collective-permute-start(bf16[2,64,512]{2,1,0:T(8,128)(2,1)S(1)} %get-tuple-element.59), channel_id=1, source_target_pairs={{0,16},{4,20},{8,24},{12,28},{16,0},{20,4},{24,8},{28,12},{1,17},{... | collective-permute-start | bytes 393224 | tf_op jit(solution)/shard_map/ppermute | solution.py:38
  140.9 13.2 %collective-permute-start.11 = (bf16[2,64,512]{2,1,0:T(8,128)(2,1)S(1)}, bf16[2,64,512]{2,1,0:T(8,128)(2,1)S(1)}, u32[]{:S(2)}, u32[]{:S(2)}) collective-permute-start(bf16[2,64,512]{2,1,0:T(8,128)(2,1)S(1)} %get-tuple-element.60), channel_id=1, source_target_pairs={{0,24},{4,28},{8,0},{12,4},{16,8},{20,12},{24,16},{28,20},{1,25},{... | collective-permute-start | bytes 393224 | tf_op jit(solution)/shard_map/ppermute | solution.py:38
  (1 other events, 0.8 us)

commit v5 on v4

--- a/solution.py
+++ b/solution.py
@@ -297,6 +297,8 @@
     near = lax.ppermute(away, "z", [(i, i ^ 1) for i in range(NZ)])
     parts = call(pair_kernel, [shape(2, side // NZ, keys)] * (NZ // 2), [keep, near])
     parts = [parts[0]] + [shift_z(parts[k], 2 * k) for k in range(1, NZ // 2)]
+    (section_grad,) = call(final_kernel, [shape(tokens, width)], [home])
+    section_grad, *parts = tie(section_grad, *parts)
     out = shape(side, side)
     left_gram, right_gram, precond = call(
         shampoo_kernel,
@@ -305,8 +307,6 @@
         scratch=[pltpu.VMEM((side, side), BF16)],
         flops=8 * side**3,
     )
-    home, left_gram, right_gram, precond = tie(home, left_gram, right_gram, precond)
-    (section_grad,) = call(final_kernel, [shape(tokens, width)], [home])
     return section_grad[None], left_gram[None, None], right_gram[None, None], precond[None, None]
 
 

time: 158 us -> 157 us (level)
    ppermute x6, waiting for transfers between devices: 16.8 us -> 15.2 us  [shift_z(): return lax.ppermute(value, 'z', [(i, (i + by) % NZ) for i in range(NZ)])]
  transfers between devices with their start and end apart: 15 -> 15, of which waited for: 6 -> 7; matrix products, arithmetic and copies ran while one was open for 0% -> 0% of each run, Pallas kernels for 4% -> 3%
where the time goes in v5:
time: 157 us; the launch traced here: 156 us
  starting transfers between devices  72.6 us (46%)
  blocking collectives  34.7 us (22%)
  waiting for transfers between devices  31.6 us (20%)
  Pallas kernels  11.4 us (7%)
  local copies, waits for them, and re-layouts  5.18 us (3%)
    ppermute x6, starting transfers between devices, shift_z(): return lax.ppermute(value, 'z', [(i, (i + by) % NZ) for i in range(NZ)])  29.1 us
    all_gather x1, blocking collectives, body(): weights = lax.all_gather(shard, 'z', axis=0, tiled=True)  27.9 us
    ppermute x6, waiting for transfers between devices, shift_z(): return lax.ppermute(value, 'z', [(i, (i + by) % NZ) for i in range(NZ)])  15.2 us
    pallas_call x12, Pallas kernels, call(): pl.pallas_call(kernel, out_shape=outs, in_specs=specs, out_specs=[pl.Bloc...  11.4 us
    ppermute x3, starting transfers between devices, swap_y(): return lax.ppermute(value, 'yl', [(i, i ^ k) for i in range(NYL)])  9.27 us
    all_to_all x1, starting transfers between devices, body(): home = lax.all_to_all(sums, (*PAIRS, 'yl'), 0, 0).reshape(width, tokens)  9.24 us
    all_to_all x1, starting transfers between devices, body(): spread = lax.all_to_all(branch, PAIRS, 0, 0)  8.24 us
    all_to_all x1, blocking collectives, body(): stats = lax.all_to_all(stats, 'yl', 0, 0)  6.81 us
  transfers between devices with their start and end apart: 15, of which 7 were waited for; matrix products, arithmetic and copies ran while one was open for 0% of the time, Pallas kernels for 3%

profile of v5, /device:TPU:1, one launch (start us, length us, event | category | flops | bytes accessed | tf_op | source)
XLA Modules:
  0.0 156.4 jit_solution(5373001690857531108)
XLA Ops:
  4.5 5.6 %all-to-all-start = ((bf16[4,1408,128]{2,1,0:T(8,128)(2,1)}), bf16[4,1408,128]{2,1,0:T(8,128)(2,1)S(1)}, u32[]{:S(2)}, u32[]{:S(2)}) async-start(bf16[4,1408,128]{2,1,0:T(8,128)(2,1)} %shard_map.102), calls=%async_computation | async-start | bytes 2883584 | tf_op jit(solution)/shard_map/all_to_all | solution.py:243
  10.3 27.9 %all-gather = bf16[1,896,512]{2,1,0:T(8,128)(2,1)S(1)} all-gather(bf16[1,112,512]{2,1,0:T(8,128)(2,1)S(1)} %copy-done.8), channel_id=2, replica_groups=mesh['x'=4,'yh'=2,'c'=2,'z'=8,'yl'=4] {'z'}, dimensions={1}, use_global_device_ids=true | all-gather | bytes 1032192 | tf_op jit(solution)/shard_map/all_gather | solution.py:246
  38.2 5.0 %all-to-all-done.refs_0_.got = bf16[4,1408,128]{2,1,0:T(8,128)(2,1)S(1)} async-done(((bf16[4,1408,128]{2,1,0:T(8,128)(2,1)}), bf16[4,1408,128]{2,1,0:T(8,128)(2,1)S(1)}, u32[]{:S(2)}, u32[]{:S(2)}) %all-to-all-start) | async-done | bytes 1441824 | tf_op jit(solution)/shard_map/all_to_all | solution.py:243
  45.0 4.6 %collective-permute-start = (bf16[4,7,16,512]{3,2,1,0:T(8,128)(2,1)S(1)}, bf16[4,7,16,512]{3,2,1,0:T(8,128)(2,1)S(1)}, u32[]{:S(2)}, u32[]{:S(2)}) collective-permute-start(bf16[4,7,16,512]{3,2,1,0:T(8,128)(2,1)S(1)} %get-tuple-element.39), channel_id=1, source_target_pairs={{0,4},{4,0},{8,12},{12,8},{16,20},{20,16},{24,28},{28,24},{1,5},{5... | collective-permute-start | bytes 1376264 | tf_op jit(solution)/shard_map/ppermute | solution.py:258
  50.4 6.8 %all_to_all.20.refs_3_ = f32[4,2,512]{2,1,0:T(2,128)S(1)} all-to-all(f32[4,2,512]{2,1,0:T(2,128)S(1)} %shard_map.104), channel_id=1, replica_groups=mesh['x'=4,'yh'=2,'c'=2,'z'=8,'yl'=4] {'yl'}, dimensions={0} | all-to-all | bytes 32768 | tf_op jit(solution)/shard_map/all_to_all | solution.py:267
  59.8 8.2 %all-to-all-start.2 = ((bf16[8,112,512]{2,1,0:T(8,128)(2,1)}), bf16[8,112,512]{2,1,0:T(8,128)(2,1)S(1)}, u32[]{:S(2)}, u32[]{:S(2)}) async-start(bf16[8,112,512]{2,1,0:T(8,128)(2,1)} %copy-done), calls=%async_computation.2 | async-start | bytes 1835008 | tf_op jit(solution)/shard_map/all_to_all | solution.py:277
  69.1 5.8 %collective-permute-start.1 = (bf16[7,16,512]{2,1,0:T(8,128)(2,1)S(1)}, bf16[7,16,512]{2,1,0:T(8,128)(2,1)S(1)}, u32[]{:S(2)}, u32[]{:S(2)}) collective-permute-start(bf16[7,16,512]{2,1,0:T(8,128)(2,1)S(1)} %get-tuple-element.46), channel_id=1, source_target_pairs={{0,8},{4,12},{8,16},{12,20},{16,24},{20,28},{24,0},{28,4},{1,9},{5... | collective-permute-start | bytes 344072 | tf_op jit(solution)/shard_map/ppermute | solution.py:38
  75.0 7.9 %collective-permute-start.2 = (bf16[7,16,512]{2,1,0:T(8,128)(2,1)S(1)}, bf16[7,16,512]{2,1,0:T(8,128)(2,1)S(1)}, u32[]{:S(2)}, u32[]{:S(2)}) collective-permute-start(bf16[7,16,512]{2,1,0:T(8,128)(2,1)S(1)} %get-tuple-element.47), channel_id=1, source_target_pairs={{0,16},{4,20},{8,24},{12,28},{16,0},{20,4},{24,8},{28,12},{1,17},{... | collective-permute-start | bytes 344072 | tf_op jit(solution)/shard_map/ppermute | solution.py:38
  82.9 3.4 %collective-permute-start.3 = (bf16[7,16,512]{2,1,0:T(8,128)(2,1)S(1)}, bf16[7,16,512]{2,1,0:T(8,128)(2,1)S(1)}, u32[]{:S(2)}, u32[]{:S(2)}) collective-permute-start(bf16[7,16,512]{2,1,0:T(8,128)(2,1)S(1)} %get-tuple-element.48), channel_id=1, source_target_pairs={{0,24},{4,28},{8,0},{12,4},{16,8},{20,12},{24,16},{28,20},{1,25},{... | collective-permute-start | bytes 344072 | tf_op jit(solution)/shard_map/ppermute | solution.py:38
  86.3 6.9 %collective-permute-done.3.refs_3_ = bf16[7,16,512]{2,1,0:T(8,128)(2,1)S(1)} collective-permute-done((bf16[7,16,512]{2,1,0:T(8,128)(2,1)S(1)}, bf16[7,16,512]{2,1,0:T(8,128)(2,1)S(1)}, u32[]{:S(2)}, u32[]{:S(2)}) %collective-permute-start.3) | collective-permute-done | bytes 114720 | tf_op jit(solution)/shard_map/ppermute | solution.py:38
  93.6 4.6 %collective-permute-start.4 = (bf16[8,112,512]{2,1,0:T(8,128)(2,1)S(1)}, bf16[8,112,512]{2,1,0:T(8,128)(2,1)S(1)}, u32[]{:S(2)}, u32[]{:S(2)}) collective-permute-start(bf16[8,112,512]{2,1,0:T(8,128)(2,1)S(1)} %shard_map.108), channel_id=1, source_target_pairs={{0,32},{32,0},{1,33},{33,1},{2,34},{34,2},{3,35},{35,3},{4,36},{36... | collective-permute-start | bytes 2752520 | tf_op jit(solution)/shard_map/ppermute | solution.py:42
  98.3 3.0 %collective-permute-start.7 = (bf16[7,16,512]{2,1,0:T(8,128)(2,1)S(1)}, bf16[7,16,512]{2,1,0:T(8,128)(2,1)S(1)}, u32[]{:S(2)}, u32[]{:S(2)}) collective-permute-start(bf16[7,16,512]{2,1,0:T(8,128)(2,1)S(1)} %shard_map.107.refs_0_), channel_id=1, source_target_pairs={{0,3},{1,2},{2,1},{3,0},{4,7},{5,6},{6,5},{7,4},{8,11},{9,10},{10,... | collective-permute-start | bytes 344072 | tf_op jit(solution)/shard_map/ppermute | solution.py:46
  101.2 3.4 %collective-permute-start.6 = (bf16[7,16,512]{2,1,0:T(8,128)(2,1)S(1)}, bf16[7,16,512]{2,1,0:T(8,128)(2,1)S(1)}, u32[]{:S(2)}, u32[]{:S(2)}) collective-permute-start(bf16[7,16,512]{2,1,0:T(8,128)(2,1)S(1)} %shard_map.107.refs_0_), channel_id=1, source_target_pairs={{0,2},{1,3},{2,0},{3,1},{4,6},{5,7},{6,4},{7,5},{8,10},{9,11},{10,... | collective-permute-start | bytes 344072 | tf_op jit(solution)/shard_map/ppermute | solution.py:46
  104.6 2.9 %collective-permute-start.5 = (bf16[7,16,512]{2,1,0:T(8,128)(2,1)S(1)}, bf16[7,16,512]{2,1,0:T(8,128)(2,1)S(1)}, u32[]{:S(2)}, u32[]{:S(2)}) collective-permute-start(bf16[7,16,512]{2,1,0:T(8,128)(2,1)S(1)} %shard_map.107.refs_0_), channel_id=1, source_target_pairs={{0,1},{1,0},{2,3},{3,2},{4,5},{5,4},{6,7},{7,6},{8,9},{9,8},{10,11... | collective-permute-start | bytes 344072 | tf_op jit(solution)/shard_map/ppermute | solution.py:46
  108.8 4.6 %collective-permute-done.6.refs_2_ = bf16[7,16,512]{2,1,0:T(8,128)(2,1)S(1)} collective-permute-done((bf16[7,16,512]{2,1,0:T(8,128)(2,1)S(1)}, bf16[7,16,512]{2,1,0:T(8,128)(2,1)S(1)}, u32[]{:S(2)}, u32[]{:S(2)}) %collective-permute-start.6) | collective-permute-done | bytes 114720 | tf_op jit(solution)/shard_map/ppermute | solution.py:46
  113.4 9.2 %all-to-all-start.3 = ((bf16[32,112,128]{2,1,0:T(8,128)(2,1)}), bf16[32,112,128]{2,1,0:T(8,128)(2,1)S(1)}, u32[]{:S(2)}, u32[]{:S(2)}) async-start(bf16[32,112,128]{2,1,0:T(8,128)(2,1)} %shard_map.109), calls=%async_computation.3 | async-start | bytes 1835008 | tf_op jit(solution)/shard_map/all_to_all | solution.py:287
  123.8 1.9 %collective-permute-start.8 = (bf16[4,64,512]{2,1,0:T(8,128)(2,1)S(1)}, bf16[4,64,512]{2,1,0:T(8,128)(2,1)S(1)}, u32[]{:S(2)}, u32[]{:S(2)}) collective-permute-start(bf16[4,64,512]{2,1,0:T(8,128)(2,1)S(1)} %get-tuple-element.57), channel_id=1, source_target_pairs={{0,4},{4,0},{8,12},{12,8},{16,20},{20,16},{24,28},{28,24},{1,5},{5... | collective-permute-start | bytes 786440 | tf_op jit(solution)/shard_map/ppermute | solution.py:297
  125.7 6.4 %collective-permute-done.8.got = bf16[4,64,512]{2,1,0:T(8,128)(2,1)S(1)} collective-permute-done((bf16[4,64,512]{2,1,0:T(8,128)(2,1)S(1)}, bf16[4,64,512]{2,1,0:T(8,128)(2,1)S(1)}, u32[]{:S(2)}, u32[]{:S(2)}) %collective-permute-start.8) | collective-permute-done | bytes 262176 | tf_op jit(solution)/shard_map/ppermute | solution.py:297
  132.1 3.2 %collective-permute-start.9 = (bf16[2,64,512]{2,1,0:T(8,128)(2,1)S(1)}, bf16[2,64,512]{2,1,0:T(8,128)(2,1)S(1)}, u32[]{:S(2)}, u32[]{:S(2)}) collective-permute-start(bf16[2,64,512]{2,1,0:T(8,128)(2,1)S(1)} %get-tuple-element.59), channel_id=1, source_target_pairs={{0,8},{4,12},{8,16},{12,20},{16,24},{20,28},{24,0},{28,4},{1,9},{5... | collective-permute-start | bytes 393224 | tf_op jit(solution)/shard_map/ppermute | solution.py:38
  135.4 5.5 %collective-permute-start.10 = (bf16[2,64,512]{2,1,0:T(8,128)(2,1)S(1)}, bf16[2,64,512]{2,1,0:T(8,128)(2,1)S(1)}, u32[]{:S(2)}, u32[]{:S(2)}) collective-permute-start(bf16[2,64,512]{2,1,0:T(8,128)(2,1)S(1)} %get-tuple-element.60), channel_id=1, source_target_pairs={{0,16},{4,20},{8,24},{12,28},{16,0},{20,4},{24,8},{28,12},{1,17},{... | collective-permute-start | bytes 393224 | tf_op jit(solution)/shard_map/ppermute | solution.py:38
  140.9 3.3 %collective-permute-start.11 = (bf16[2,64,512]{2,1,0:T(8,128)(2,1)S(1)}, bf16[2,64,512]{2,1,0:T(8,128)(2,1)S(1)}, u32[]{:S(2)}, u32[]{:S(2)}) collective-permute-start(bf16[2,64,512]{2,1,0:T(8,128)(2,1)S(1)} %get-tuple-element.61), channel_id=1, source_target_pairs={{0,24},{4,28},{8,0},{12,4},{16,8},{20,12},{24,16},{28,20},{1,25},{... | collective-permute-start | bytes 393224 | tf_op jit(solution)/shard_map/ppermute | solution.py:38
  145.8 2.4 %collective-permute-done.10.refs_2_ = bf16[2,64,512]{2,1,0:T(8,128)(2,1)S(1)} collective-permute-done((bf16[2,64,512]{2,1,0:T(8,128)(2,1)S(1)}, bf16[2,64,512]{2,1,0:T(8,128)(2,1)S(1)}, u32[]{:S(2)}, u32[]{:S(2)}) %collective-permute-start.10) | collective-permute-done | bytes 131104 | tf_op jit(solution)/shard_map/ppermute | solution.py:38
  148.3 5.8 %collective-permute-done.11.refs_3_ = bf16[2,64,512]{2,1,0:T(8,128)(2,1)S(1)} collective-permute-done((bf16[2,64,512]{2,1,0:T(8,128)(2,1)S(1)}, bf16[2,64,512]{2,1,0:T(8,128)(2,1)S(1)}, u32[]{:S(2)}, u32[]{:S(2)}) %collective-permute-start.11) | collective-permute-done | bytes 131104 | tf_op jit(solution)/shard_map/ppermute | solution.py:38
  154.1 2.3 %shard_map.113 = (bf16[512,512]{1,0:T(8,128)(2,1)}, bf16[512,512]{1,0:T(8,128)(2,1)}, bf16[512,512]{1,0:T(8,128)(2,1)}) custom-call(bf16[2,64,512]{2,1,0:T(8,128)(2,1)S(1)} %get-tuple-element.63.refs_0_, bf16[2,64,512]{2,1,0:T(8,128)(2,1)S(1)} %collective-permute-done.9.refs_1_, bf16[2,64,512]{2,1,0:T(8,128)(2,1)S(1)} %collective-permute-done.10.refs_2_, ...), custom_call_target="tpu_custom_call" | custom-call | flops 1073741824 | bytes 3145728 | tf_op jit(solution)/shard_map/pallas_call | solution.py:22
  (45 shorter events, 14.8 us)
Async XLA Ops:
  0.6 1.2 copy-start.1
  1.8 0.9 copy-start.4
  4.5 5.6 %copy-start.9 = (f32[1,3584]{1,0:T(1,128)S(1)}, f32[1,3584]{1,0:T(1,128)}, u32[]{:S(2)}) copy-start(f32[1,3584]{1,0:T(1,128)} %param.8) | copy-start | bytes 43012
  4.5 5.8 %copy-start.8 = (bf16[1,112,512]{2,1,0:T(8,128)(2,1)S(1)}, bf16[1,112,512]{2,1,0:T(8,128)(2,1)}, u32[]{:S(2)}) copy-start(bf16[1,112,512]{2,1,0:T(8,128)(2,1)} %param.9) | copy-start | bytes 344068
  4.5 38.6 %all-to-all-start = ((bf16[4,1408,128]{2,1,0:T(8,128)(2,1)}), bf16[4,1408,128]{2,1,0:T(8,128)(2,1)S(1)}, u32[]{:S(2)}, u32[]{:S(2)}) async-start(bf16[4,1408,128]{2,1,0:T(8,128)(2,1)} %shard_map.102), calls=%async_computation | async-start | bytes 2883584 | tf_op jit(solution)/shard_map/all_to_all | solution.py:243
  45.0 14.0 %collective-permute-start = (bf16[4,7,16,512]{3,2,1,0:T(8,128)(2,1)S(1)}, bf16[4,7,16,512]{3,2,1,0:T(8,128)(2,1)S(1)}, u32[]{:S(2)}, u32[]{:S(2)}) collective-permute-start(bf16[4,7,16,512]{3,2,1,0:T(8,128)(2,1)S(1)} %get-tuple-element.39), channel_id=1, source_target_pairs={{0,4},{4,0},{8,12},{12,8},{16,20},{20,16},{24,28},{28,24},{1,5},{5... | collective-permute-start | bytes 1376264 | tf_op jit(solution)/shard_map/ppermute | solution.py:258
  58.1 0.9 copy-start
  59.8 33.5 %all-to-all-start.2 = ((bf16[8,112,512]{2,1,0:T(8,128)(2,1)}), bf16[8,112,512]{2,1,0:T(8,128)(2,1)S(1)}, u32[]{:S(2)}, u32[]{:S(2)}) async-start(bf16[8,112,512]{2,1,0:T(8,128)(2,1)} %copy-done), calls=%async_computation.2 | async-start | bytes 1835008 | tf_op jit(solution)/shard_map/all_to_all | solution.py:277
  68.0 1.0 copy-start.3
  69.1 17.2 %collective-permute-start.1 = (bf16[7,16,512]{2,1,0:T(8,128)(2,1)S(1)}, bf16[7,16,512]{2,1,0:T(8,128)(2,1)S(1)}, u32[]{:S(2)}, u32[]{:S(2)}) collective-permute-start(bf16[7,16,512]{2,1,0:T(8,128)(2,1)S(1)} %get-tuple-element.46), channel_id=1, source_target_pairs={{0,8},{4,12},{8,16},{12,20},{16,24},{20,28},{24,0},{28,4},{1,9},{5... | collective-permute-start | bytes 344072 | tf_op jit(solution)/shard_map/ppermute | solution.py:38
  75.0 11.4 %collective-permute-start.2 = (bf16[7,16,512]{2,1,0:T(8,128)(2,1)S(1)}, bf16[7,16,512]{2,1,0:T(8,128)(2,1)S(1)}, u32[]{:S(2)}, u32[]{:S(2)}) collective-permute-start(bf16[7,16,512]{2,1,0:T(8,128)(2,1)S(1)} %get-tuple-element.47), channel_id=1, source_target_pairs={{0,16},{4,20},{8,24},{12,28},{16,0},{20,4},{24,8},{28,12},{1,17},{... | collective-permute-start | bytes 344072 | tf_op jit(solution)/shard_map/ppermute | solution.py:38
  82.9 10.3 %collective-permute-start.3 = (bf16[7,16,512]{2,1,0:T(8,128)(2,1)S(1)}, bf16[7,16,512]{2,1,0:T(8,128)(2,1)S(1)}, u32[]{:S(2)}, u32[]{:S(2)}) collective-permute-start(bf16[7,16,512]{2,1,0:T(8,128)(2,1)S(1)} %get-tuple-element.48), channel_id=1, source_target_pairs={{0,24},{4,28},{8,0},{12,4},{16,8},{20,12},{24,16},{28,20},{1,25},{... | collective-permute-start | bytes 344072 | tf_op jit(solution)/shard_map/ppermute | solution.py:38
  93.6 13.9 %collective-permute-start.4 = (bf16[8,112,512]{2,1,0:T(8,128)(2,1)S(1)}, bf16[8,112,512]{2,1,0:T(8,128)(2,1)S(1)}, u32[]{:S(2)}, u32[]{:S(2)}) collective-permute-start(bf16[8,112,512]{2,1,0:T(8,128)(2,1)S(1)} %shard_map.108), channel_id=1, source_target_pairs={{0,32},{32,0},{1,33},{33,1},{2,34},{34,2},{3,35},{35,3},{4,36},{36... | collective-permute-start | bytes 2752520 | tf_op jit(solution)/shard_map/ppermute | solution.py:42
  98.3 10.5 %collective-permute-start.7 = (bf16[7,16,512]{2,1,0:T(8,128)(2,1)S(1)}, bf16[7,16,512]{2,1,0:T(8,128)(2,1)S(1)}, u32[]{:S(2)}, u32[]{:S(2)}) collective-permute-start(bf16[7,16,512]{2,1,0:T(8,128)(2,1)S(1)} %shard_map.107.refs_0_), channel_id=1, source_target_pairs={{0,3},{1,2},{2,1},{3,0},{4,7},{5,6},{6,5},{7,4},{8,11},{9,10},{10,... | collective-permute-start | bytes 344072 | tf_op jit(solution)/shard_map/ppermute | solution.py:46
  101.2 12.2 %collective-permute-start.6 = (bf16[7,16,512]{2,1,0:T(8,128)(2,1)S(1)}, bf16[7,16,512]{2,1,0:T(8,128)(2,1)S(1)}, u32[]{:S(2)}, u32[]{:S(2)}) collective-permute-start(bf16[7,16,512]{2,1,0:T(8,128)(2,1)S(1)} %shard_map.107.refs_0_), channel_id=1, source_target_pairs={{0,2},{1,3},{2,0},{3,1},{4,6},{5,7},{6,4},{7,5},{8,10},{9,11},{10,... | collective-permute-start | bytes 344072 | tf_op jit(solution)/shard_map/ppermute | solution.py:46
  104.6 8.8 %collective-permute-start.5 = (bf16[7,16,512]{2,1,0:T(8,128)(2,1)S(1)}, bf16[7,16,512]{2,1,0:T(8,128)(2,1)S(1)}, u32[]{:S(2)}, u32[]{:S(2)}) collective-permute-start(bf16[7,16,512]{2,1,0:T(8,128)(2,1)S(1)} %shard_map.107.refs_0_), channel_id=1, source_target_pairs={{0,1},{1,0},{2,3},{3,2},{4,5},{5,4},{6,7},{7,6},{8,9},{9,8},{10,11... | collective-permute-start | bytes 344072 | tf_op jit(solution)/shard_map/ppermute | solution.py:46
  108.8 13.9 %copy-start.5 = (s32[1,7]{1,0:T(1,128)S(1)}, s32[1,7]{1,0:T(1,128)}, u32[]{:S(2)}) copy-start(s32[1,7]{1,0:T(1,128)} %owners.1) | copy-start | bytes 88
  113.4 31.2 %all-to-all-start.3 = ((bf16[32,112,128]{2,1,0:T(8,128)(2,1)}), bf16[32,112,128]{2,1,0:T(8,128)(2,1)S(1)}, u32[]{:S(2)}, u32[]{:S(2)}) async-start(bf16[32,112,128]{2,1,0:T(8,128)(2,1)} %shard_map.109), calls=%async_computation.3 | async-start | bytes 1835008 | tf_op jit(solution)/shard_map/all_to_all | solution.py:287
  122.7 31.4 %copy-start.6 = (bf16[1,1,512,512]{3,2,1,0:T(8,128)(2,1)S(1)}, bf16[1,1,512,512]{3,2,1,0:T(8,128)(2,1)}, u32[]{:S(2)}) copy-start(bf16[1,1,512,512]{3,2,1,0:T(8,128)(2,1)} %param.12) | copy-start | bytes 1572868
  122.7 31.4 %copy-start.7 = (bf16[1,1,512,512]{3,2,1,0:T(8,128)(2,1)S(1)}, bf16[1,1,512,512]{3,2,1,0:T(8,128)(2,1)}, u32[]{:S(2)}) copy-start(bf16[1,1,512,512]{3,2,1,0:T(8,128)(2,1)} %param.13) | copy-start | bytes 1572868
  123.8 8.3 %collective-permute-start.8 = (bf16[4,64,512]{2,1,0:T(8,128)(2,1)S(1)}, bf16[4,64,512]{2,1,0:T(8,128)(2,1)S(1)}, u32[]{:S(2)}, u32[]{:S(2)}) collective-permute-start(bf16[4,64,512]{2,1,0:T(8,128)(2,1)S(1)} %get-tuple-element.57), channel_id=1, source_target_pairs={{0,4},{4,0},{8,12},{12,8},{16,20},{20,16},{24,28},{28,24},{1,5},{5... | collective-permute-start | bytes 786440 | tf_op jit(solution)/shard_map/ppermute | solution.py:297
  132.1 13.7 %collective-permute-start.9 = (bf16[2,64,512]{2,1,0:T(8,128)(2,1)S(1)}, bf16[2,64,512]{2,1,0:T(8,128)(2,1)S(1)}, u32[]{:S(2)}, u32[]{:S(2)}) collective-permute-start(bf16[2,64,512]{2,1,0:T(8,128)(2,1)S(1)} %get-tuple-element.59), channel_id=1, source_target_pairs={{0,8},{4,12},{8,16},{12,20},{16,24},{20,28},{24,0},{28,4},{1,9},{5... | collective-permute-start | bytes 393224 | tf_op jit(solution)/shard_map/ppermute | solution.py:38
  135.4 12.9 %collective-permute-start.10 = (bf16[2,64,512]{2,1,0:T(8,128)(2,1)S(1)}, bf16[2,64,512]{2,1,0:T(8,128)(2,1)S(1)}, u32[]{:S(2)}, u32[]{:S(2)}) collective-permute-start(bf16[2,64,512]{2,1,0:T(8,128)(2,1)S(1)} %get-tuple-element.60), channel_id=1, source_target_pairs={{0,16},{4,20},{8,24},{12,28},{16,0},{20,4},{24,8},{28,12},{1,17},{... | collective-permute-start | bytes 393224 | tf_op jit(solution)/shard_map/ppermute | solution.py:38
  140.9 13.2 %collective-permute-start.11 = (bf16[2,64,512]{2,1,0:T(8,128)(2,1)S(1)}, bf16[2,64,512]{2,1,0:T(8,128)(2,1)S(1)}, u32[]{:S(2)}, u32[]{:S(2)}) collective-permute-start(bf16[2,64,512]{2,1,0:T(8,128)(2,1)S(1)} %get-tuple-element.61), channel_id=1, source_target_pairs={{0,24},{4,28},{8,0},{12,4},{16,8},{20,12},{24,16},{28,20},{1,25},{... | collective-permute-start | bytes 393224 | tf_op jit(solution)/shard_map/ppermute | solution.py:38
  (1 other events, 0.8 us)

commit v6 on v5

--- a/solution.py
+++ b/solution.py
@@ -75,26 +75,26 @@
             send[j, low : low + LANES, :] = shared
 
 
-def gradient_kernel(scale, got, gains, keep, give, tile, shared, held):
+def gradient_kernel(scale, other, got, gains, out, tile, column, shared):
     tokens = got.shape[2]
     width = gains.shape[0]
     rows = width // NZ
-    for t in range(NYL):
-        at = slice(t * tokens, (t + 1) * tokens)
-        tile[:, at] = got[t, :width, :]
-        shared[:, at] = got[t, width:, :]
-    up = shared[...]
-    for z in range(NZ):
-        at = slice(z * rows, (z + 1) * rows)
-        held[at, :] = (dot(tile[at, :], up, ((1,), (1,))) * (gains[at, :] * scale)).astype(BF16)
+    up = load_shared(got, width, shared)
     j = lax.axis_index("yl")
-    mine = lax.axis_index("z")
-    for k in range(NZ):
-        out = give if k % 2 else keep
-        to = k - k % 2 + lax.rem(mine + k, 2)
+    parity = lax.rem(lax.axis_index("z") + other, 2)
+    for k in range(NZ // 2):
         for i in range(rows // GROUP):
-            z = lax.rem(lax.div(7 * j + i, 4) - to + NZ, NZ)
-            out[k // 2, i] = held[pl.ds(pl.multiple_of(z * rows + i * GROUP, GROUP), GROUP), :]
+            z = lax.rem(lax.div(7 * j + i, 4) - 2 * k - parity + NZ, NZ)
+            at = pl.ds(pl.multiple_of(z * rows + i * GROUP, GROUP), GROUP)
+            to = slice(k * rows + i * GROUP, k * rows + (i + 1) * GROUP)
+            for t in range(NYL):
+                tile[to, t * tokens : (t + 1) * tokens] = got[t, at, :]
+            column[to, :] = gains[at, :]
+    for k in range(NZ // 2):
+        at = slice(k * rows, (k + 1) * rows)
+        value = (dot(tile[at, :], up, ((1,), (1,))) * (column[at, :] * scale)).astype(BF16)
+        for i in range(rows // GROUP):
+            out[k, i] = value[i * GROUP : (i + 1) * GROUP, :]
 
 
 def load_shared(got, width, shared):
@@ -247,13 +247,21 @@
     got, weights, gains = tie(got, weights, gains)
     scale = (tokens * NZ * NYL) ** (-0.5)
     chunk = shape(NZ // 2, per, GROUP, keys)
-    chunks, away = call(
-        lambda *refs: gradient_kernel(scale, *refs),
-        [chunk, chunk],
-        [got, gains],
-        scratch=[pltpu.VMEM((quarter, line), BF16), pltpu.VMEM((keys, line), BF16), pltpu.VMEM((quarter, keys), BF16)],
-        flops=2 * quarter * line * keys,
-    )
+
+    def gradient(other, got, gains):
+        return call(
+            lambda *refs: gradient_kernel(scale, other, *refs),
+            [chunk],
+            [got, gains],
+            scratch=[
+                pltpu.VMEM((quarter // 2, line), BF16),
+                pltpu.VMEM((quarter // 2, 1), F32),
+                pltpu.VMEM((keys, line), BF16),
+            ],
+            flops=quarter * line * keys,
+        )[0]
+
+    away = gradient(1, got, gains)
 
     near = lax.ppermute(away, "z", [(i, i ^ 1) for i in range(NZ)])
     got, away = tie(got, away)
@@ -264,7 +272,10 @@
         scratch=[pltpu.VMEM((keys, line), BF16)],
         flops=2 * quarter * line * keys,
     )
+    got, gains, stats = tie(got, gains, stats)
     stats = lax.all_to_all(stats, "yl", 0, 0)
+    chunks = gradient(0, got, gains)
+    stats, chunks = tie(stats, chunks)
     (branch,) = call(
         lambda *refs: branch_kernel(width, *refs),
         [shape(NPAIR, quarter // NPAIR, line)],

time: 157 us -> 157 us (level)
  blocking collectives: 34.7 us -> 27.9 us
  waiting for transfers between devices: 31.6 us -> 35.4 us
  Pallas kernels: 11.4 us -> 13.9 us
  starting transfers between devices: 72.6 us -> 74.9 us
  local copies, waits for them, and re-layouts: 5.18 us -> 3.6 us
    all_to_all x1 -> x0, blocking collectives: 6.81 us -> none  [body(): stats = lax.all_to_all(stats, 'yl', 0, 0)]
    all_to_all x0 -> x1, waiting for transfers between devices: none -> 3.35 us  [body(): stats = lax.all_to_all(stats, 'yl', 0, 0)]
    all_to_all x0 -> x1, starting transfers between devices: none -> 3.25 us  [body(): stats = lax.all_to_all(stats, 'yl', 0, 0)]
    pallas_call x12 -> x13, Pallas kernels: 11.4 us -> 13.9 us  [call(): pl.pallas_call(kernel, out_shape=outs, in_specs=specs, out_specs=[pl.Bloc...]
    unnamed x20 -> x16, local copies, waits for them, and re-layouts: 4.8 us -> 3.02 us
  transfers between devices with their start and end apart: 15 -> 16, of which waited for: 7 -> 8; matrix products, arithmetic and copies ran while one was open for 0% -> 0% of each run, Pallas kernels for 3% -> 5%
where the time goes in v6:
time: 157 us
  starting transfers between devices  74.9 us (48%)
  waiting for transfers between devices  35.4 us (23%)
  blocking collectives  27.9 us (18%)
  Pallas kernels  13.9 us (9%)
  local copies, waits for them, and re-layouts  3.6 us (2%)
    ppermute x6, starting transfers between devices, shift_z(): return lax.ppermute(value, 'z', [(i, (i + by) % NZ) for i in range(NZ)])  29.2 us
    all_gather x1, blocking collectives, body(): weights = lax.all_gather(shard, 'z', axis=0, tiled=True)  27.9 us
    ppermute x6, waiting for transfers between devices, shift_z(): return lax.ppermute(value, 'z', [(i, (i + by) % NZ) for i in range(NZ)])  15.1 us
    pallas_call x13, Pallas kernels, call(): pl.pallas_call(kernel, out_shape=outs, in_specs=specs, out_specs=[pl.Bloc...  13.9 us
    ppermute x3, starting transfers between devices, swap_y(): return lax.ppermute(value, 'yl', [(i, i ^ k) for i in range(NYL)])  9.27 us
    all_to_all x1, starting transfers between devices, body(): home = lax.all_to_all(sums, (*PAIRS, 'yl'), 0, 0).reshape(width, tokens)  8.72 us
    all_to_all x1, starting transfers between devices, body(): spread = lax.all_to_all(branch, PAIRS, 0, 0)  8.25 us
    ppermute x2, starting transfers between devices, body(): near = lax.ppermute(away, 'z', [(i, i ^ 1) for i in range(NZ)])  6.51 us
  transfers between devices with their start and end apart: 16, of which 8 were waited for; matrix products, arithmetic and copies ran while one was open for 0% of the time, Pallas kernels for 5%

profile of v6, /device:TPU:1, one launch (start us, length us, event | category | flops | bytes accessed | tf_op | source)
XLA Modules:
  0.0 156.6 jit_solution(8196588799339502042)
XLA Ops:
  4.5 5.6 %all-to-all-start = ((bf16[4,1408,128]{2,1,0:T(8,128)(2,1)}), bf16[4,1408,128]{2,1,0:T(8,128)(2,1)S(1)}, u32[]{:S(2)}, u32[]{:S(2)}) async-start(bf16[4,1408,128]{2,1,0:T(8,128)(2,1)} %shard_map.102), calls=%async_computation | async-start | bytes 2883584 | tf_op jit(solution)/shard_map/all_to_all | solution.py:243
  10.3 27.9 %all-gather = bf16[1,896,512]{2,1,0:T(8,128)(2,1)S(1)} all-gather(bf16[1,112,512]{2,1,0:T(8,128)(2,1)S(1)} %copy-done.6), channel_id=2, replica_groups=mesh['x'=4,'yh'=2,'c'=2,'z'=8,'yl'=4] {'z'}, dimensions={1}, use_global_device_ids=true | all-gather | bytes 1032192 | tf_op jit(solution)/shard_map/all_gather | solution.py:246
  38.2 5.0 %all-to-all-done.refs_0_.got = bf16[4,1408,128]{2,1,0:T(8,128)(2,1)S(1)} async-done(((bf16[4,1408,128]{2,1,0:T(8,128)(2,1)}), bf16[4,1408,128]{2,1,0:T(8,128)(2,1)S(1)}, u32[]{:S(2)}, u32[]{:S(2)}) %all-to-all-start) | async-done | bytes 1441824 | tf_op jit(solution)/shard_map/all_to_all | solution.py:243
  45.0 4.6 %collective-permute-start = (bf16[4,7,16,512]{3,2,1,0:T(8,128)(2,1)}, bf16[4,7,16,512]{3,2,1,0:T(8,128)(2,1)}, u32[]{:S(2)}, u32[]{:S(2)}) collective-permute-start(bf16[4,7,16,512]{3,2,1,0:T(8,128)(2,1)} %shard_map.103), channel_id=1, source_target_pairs={{0,4},{4,0},{8,12},{12,8},{16,20},{20,16},{24,28},{28,24},{1,5},{5... | collective-permute-start | bytes 1376264 | tf_op jit(solution)/shard_map/ppermute | solution.py:266
  51.0 3.3 %all-to-all-start.1 = ((f32[4,2,512]{2,1,0:T(2,128)}), f32[4,2,512]{2,1,0:T(2,128)S(1)}, u32[]{:S(2)}, u32[]{:S(2)}) async-start(f32[4,2,512]{2,1,0:T(2,128)} %shard_map.104), calls=%async_computation.1 | async-start | bytes 32768 | tf_op jit(solution)/shard_map/all_to_all | solution.py:276
  55.3 3.3 %all-to-all-done.1.refs_3_ = f32[4,2,512]{2,1,0:T(2,128)S(1)} async-done(((f32[4,2,512]{2,1,0:T(2,128)}), f32[4,2,512]{2,1,0:T(2,128)S(1)}, u32[]{:S(2)}, u32[]{:S(2)}) %all-to-all-start.1) | async-done | bytes 16416 | tf_op jit(solution)/shard_map/all_to_all | solution.py:276
  60.5 8.2 %all-to-all-start.2 = ((bf16[8,112,512]{2,1,0:T(8,128)(2,1)}), bf16[8,112,512]{2,1,0:T(8,128)(2,1)S(1)}, u32[]{:S(2)}, u32[]{:S(2)}) async-start(bf16[8,112,512]{2,1,0:T(8,128)(2,1)} %copy-done), calls=%async_computation.2 | async-start | bytes 1835008 | tf_op jit(solution)/shard_map/all_to_all | solution.py:288
  69.8 5.8 %collective-permute-start.1 = (bf16[7,16,512]{2,1,0:T(8,128)(2,1)S(1)}, bf16[7,16,512]{2,1,0:T(8,128)(2,1)S(1)}, u32[]{:S(2)}, u32[]{:S(2)}) collective-permute-start(bf16[7,16,512]{2,1,0:T(8,128)(2,1)S(1)} %get-tuple-element.52), channel_id=1, source_target_pairs={{0,8},{4,12},{8,16},{12,20},{16,24},{20,28},{24,0},{28,4},{1,9},{5... | collective-permute-start | bytes 344072 | tf_op jit(solution)/shard_map/ppermute | solution.py:38
  75.6 7.9 %collective-permute-start.2 = (bf16[7,16,512]{2,1,0:T(8,128)(2,1)S(1)}, bf16[7,16,512]{2,1,0:T(8,128)(2,1)S(1)}, u32[]{:S(2)}, u32[]{:S(2)}) collective-permute-start(bf16[7,16,512]{2,1,0:T(8,128)(2,1)S(1)} %get-tuple-element.53), channel_id=1, source_target_pairs={{0,16},{4,20},{8,24},{12,28},{16,0},{20,4},{24,8},{28,12},{1,17},{... | collective-permute-start | bytes 344072 | tf_op jit(solution)/shard_map/ppermute | solution.py:38
  83.6 3.4 %collective-permute-start.3 = (bf16[7,16,512]{2,1,0:T(8,128)(2,1)S(1)}, bf16[7,16,512]{2,1,0:T(8,128)(2,1)S(1)}, u32[]{:S(2)}, u32[]{:S(2)}) collective-permute-start(bf16[7,16,512]{2,1,0:T(8,128)(2,1)S(1)} %get-tuple-element.54), channel_id=1, source_target_pairs={{0,24},{4,28},{8,0},{12,4},{16,8},{20,12},{24,16},{28,20},{1,25},{... | collective-permute-start | bytes 344072 | tf_op jit(solution)/shard_map/ppermute | solution.py:38
  87.0 6.9 %collective-permute-done.3.refs_3_ = bf16[7,16,512]{2,1,0:T(8,128)(2,1)S(1)} collective-permute-done((bf16[7,16,512]{2,1,0:T(8,128)(2,1)S(1)}, bf16[7,16,512]{2,1,0:T(8,128)(2,1)S(1)}, u32[]{:S(2)}, u32[]{:S(2)}) %collective-permute-start.3) | collective-permute-done | bytes 114720 | tf_op jit(solution)/shard_map/ppermute | solution.py:38
  94.3 4.2 %collective-permute-start.4 = (bf16[8,112,512]{2,1,0:T(8,128)(2,1)S(1)}, bf16[8,112,512]{2,1,0:T(8,128)(2,1)S(1)}, u32[]{:S(2)}, u32[]{:S(2)}) collective-permute-start(bf16[8,112,512]{2,1,0:T(8,128)(2,1)S(1)} %shard_map.109), channel_id=1, source_target_pairs={{0,32},{32,0},{1,33},{33,1},{2,34},{34,2},{3,35},{35,3},{4,36},{36... | collective-permute-start | bytes 2752520 | tf_op jit(solution)/shard_map/ppermute | solution.py:42
  98.5 2.4 %collective-permute-start.7 = (bf16[7,16,512]{2,1,0:T(8,128)(2,1)S(1)}, bf16[7,16,512]{2,1,0:T(8,128)(2,1)S(1)}, u32[]{:S(2)}, u32[]{:S(2)}) collective-permute-start(bf16[7,16,512]{2,1,0:T(8,128)(2,1)S(1)} %shard_map.108.refs_0_), channel_id=1, source_target_pairs={{0,3},{1,2},{2,1},{3,0},{4,7},{5,6},{6,5},{7,4},{8,11},{9,10},{10,... | collective-permute-start | bytes 344072 | tf_op jit(solution)/shard_map/ppermute | solution.py:46
  100.8 4.5 %collective-permute-start.6 = (bf16[7,16,512]{2,1,0:T(8,128)(2,1)S(1)}, bf16[7,16,512]{2,1,0:T(8,128)(2,1)S(1)}, u32[]{:S(2)}, u32[]{:S(2)}) collective-permute-start(bf16[7,16,512]{2,1,0:T(8,128)(2,1)S(1)} %shard_map.108.refs_0_), channel_id=1, source_target_pairs={{0,2},{1,3},{2,0},{3,1},{4,6},{5,7},{6,4},{7,5},{8,10},{9,11},{10,... | collective-permute-start | bytes 344072 | tf_op jit(solution)/shard_map/ppermute | solution.py:46
  105.3 2.5 %collective-permute-start.5 = (bf16[7,16,512]{2,1,0:T(8,128)(2,1)S(1)}, bf16[7,16,512]{2,1,0:T(8,128)(2,1)S(1)}, u32[]{:S(2)}, u32[]{:S(2)}) collective-permute-start(bf16[7,16,512]{2,1,0:T(8,128)(2,1)S(1)} %shard_map.108.refs_0_), channel_id=1, source_target_pairs={{0,1},{1,0},{2,3},{3,2},{4,5},{5,4},{6,7},{7,6},{8,9},{9,8},{10,11... | collective-permute-start | bytes 344072 | tf_op jit(solution)/shard_map/ppermute | solution.py:46
  109.0 5.2 %collective-permute-done.6.refs_2_ = bf16[7,16,512]{2,1,0:T(8,128)(2,1)S(1)} collective-permute-done((bf16[7,16,512]{2,1,0:T(8,128)(2,1)S(1)}, bf16[7,16,512]{2,1,0:T(8,128)(2,1)S(1)}, u32[]{:S(2)}, u32[]{:S(2)}) %collective-permute-start.6) | collective-permute-done | bytes 114720 | tf_op jit(solution)/shard_map/ppermute | solution.py:46
  114.2 8.7 %all-to-all-start.3 = ((bf16[32,112,128]{2,1,0:T(8,128)(2,1)}), bf16[32,112,128]{2,1,0:T(8,128)(2,1)S(1)}, u32[]{:S(2)}, u32[]{:S(2)}) async-start(bf16[32,112,128]{2,1,0:T(8,128)(2,1)} %shard_map.110), calls=%async_computation.3 | async-start | bytes 1835008 | tf_op jit(solution)/shard_map/all_to_all | solution.py:298
  126.0 6.4 %collective-permute-done.8.got = bf16[4,64,512]{2,1,0:T(8,128)(2,1)S(1)} collective-permute-done((bf16[4,64,512]{2,1,0:T(8,128)(2,1)S(1)}, bf16[4,64,512]{2,1,0:T(8,128)(2,1)S(1)}, u32[]{:S(2)}, u32[]{:S(2)}) %collective-permute-start.8) | collective-permute-done | bytes 262176 | tf_op jit(solution)/shard_map/ppermute | solution.py:308
  132.5 2.8 %collective-permute-start.9 = (bf16[2,64,512]{2,1,0:T(8,128)(2,1)S(1)}, bf16[2,64,512]{2,1,0:T(8,128)(2,1)S(1)}, u32[]{:S(2)}, u32[]{:S(2)}) collective-permute-start(bf16[2,64,512]{2,1,0:T(8,128)(2,1)S(1)} %get-tuple-element.65), channel_id=1, source_target_pairs={{0,8},{4,12},{8,16},{12,20},{16,24},{20,28},{24,0},{28,4},{1,9},{5... | collective-permute-start | bytes 393224 | tf_op jit(solution)/shard_map/ppermute | solution.py:38
  135.3 6.2 %collective-permute-start.10 = (bf16[2,64,512]{2,1,0:T(8,128)(2,1)S(1)}, bf16[2,64,512]{2,1,0:T(8,128)(2,1)S(1)}, u32[]{:S(2)}, u32[]{:S(2)}) collective-permute-start(bf16[2,64,512]{2,1,0:T(8,128)(2,1)S(1)} %get-tuple-element.66), channel_id=1, source_target_pairs={{0,16},{4,20},{8,24},{12,28},{16,0},{20,4},{24,8},{28,12},{1,17},{... | collective-permute-start | bytes 393224 | tf_op jit(solution)/shard_map/ppermute | solution.py:38
  141.5 3.0 %collective-permute-start.11 = (bf16[2,64,512]{2,1,0:T(8,128)(2,1)S(1)}, bf16[2,64,512]{2,1,0:T(8,128)(2,1)S(1)}, u32[]{:S(2)}, u32[]{:S(2)}) collective-permute-start(bf16[2,64,512]{2,1,0:T(8,128)(2,1)S(1)} %get-tuple-element.67), channel_id=1, source_target_pairs={{0,24},{4,28},{8,0},{12,4},{16,8},{20,12},{24,16},{28,20},{1,25},{... | collective-permute-start | bytes 393224 | tf_op jit(solution)/shard_map/ppermute | solution.py:38
  146.1 3.1 %collective-permute-done.10.refs_2_ = bf16[2,64,512]{2,1,0:T(8,128)(2,1)S(1)} collective-permute-done((bf16[2,64,512]{2,1,0:T(8,128)(2,1)S(1)}, bf16[2,64,512]{2,1,0:T(8,128)(2,1)S(1)}, u32[]{:S(2)}, u32[]{:S(2)}) %collective-permute-start.10) | collective-permute-done | bytes 131104 | tf_op jit(solution)/shard_map/ppermute | solution.py:38
  149.2 5.1 %collective-permute-done.11.refs_3_ = bf16[2,64,512]{2,1,0:T(8,128)(2,1)S(1)} collective-permute-done((bf16[2,64,512]{2,1,0:T(8,128)(2,1)S(1)}, bf16[2,64,512]{2,1,0:T(8,128)(2,1)S(1)}, u32[]{:S(2)}, u32[]{:S(2)}) %collective-permute-start.11) | collective-permute-done | bytes 131104 | tf_op jit(solution)/shard_map/ppermute | solution.py:38
  154.3 2.3 %shard_map.114 = (bf16[512,512]{1,0:T(8,128)(2,1)}, bf16[512,512]{1,0:T(8,128)(2,1)}, bf16[512,512]{1,0:T(8,128)(2,1)}) custom-call(bf16[2,64,512]{2,1,0:T(8,128)(2,1)S(1)} %get-tuple-element.69.refs_0_, bf16[2,64,512]{2,1,0:T(8,128)(2,1)S(1)} %collective-permute-done.9.refs_1_, bf16[2,64,512]{2,1,0:T(8,128)(2,1)S(1)} %collective-permute-done.10.refs_2_, ...), custom_call_target="tpu_custom_call" | custom-call | flops 1073741824 | bytes 3145728 | tf_op jit(solution)/shard_map/pallas_call | solution.py:22
  (44 shorter events, 17.6 us)
Async XLA Ops:
  0.6 1.2 copy-start.1
  1.8 0.9 copy-start.2
  4.5 5.6 %copy-start.7 = (f32[1,3584]{1,0:T(1,128)S(1)}, f32[1,3584]{1,0:T(1,128)}, u32[]{:S(2)}) copy-start(f32[1,3584]{1,0:T(1,128)} %param.8) | copy-start | bytes 43012
  4.5 5.8 %copy-start.6 = (bf16[1,112,512]{2,1,0:T(8,128)(2,1)S(1)}, bf16[1,112,512]{2,1,0:T(8,128)(2,1)}, u32[]{:S(2)}) copy-start(bf16[1,112,512]{2,1,0:T(8,128)(2,1)} %param.9) | copy-start | bytes 344068
  4.5 38.6 %all-to-all-start = ((bf16[4,1408,128]{2,1,0:T(8,128)(2,1)}), bf16[4,1408,128]{2,1,0:T(8,128)(2,1)S(1)}, u32[]{:S(2)}, u32[]{:S(2)}) async-start(bf16[4,1408,128]{2,1,0:T(8,128)(2,1)} %shard_map.102), calls=%async_computation | async-start | bytes 2883584 | tf_op jit(solution)/shard_map/all_to_all | solution.py:243
  45.0 15.5 %collective-permute-start = (bf16[4,7,16,512]{3,2,1,0:T(8,128)(2,1)}, bf16[4,7,16,512]{3,2,1,0:T(8,128)(2,1)}, u32[]{:S(2)}, u32[]{:S(2)}) collective-permute-start(bf16[4,7,16,512]{3,2,1,0:T(8,128)(2,1)} %shard_map.103), channel_id=1, source_target_pairs={{0,4},{4,0},{8,12},{12,8},{16,20},{20,16},{24,28},{28,24},{1,5},{5... | collective-permute-start | bytes 1376264 | tf_op jit(solution)/shard_map/ppermute | solution.py:266
  51.0 7.7 %all-to-all-start.1 = ((f32[4,2,512]{2,1,0:T(2,128)}), f32[4,2,512]{2,1,0:T(2,128)S(1)}, u32[]{:S(2)}, u32[]{:S(2)}) async-start(f32[4,2,512]{2,1,0:T(2,128)} %shard_map.104), calls=%async_computation.1 | async-start | bytes 32768 | tf_op jit(solution)/shard_map/all_to_all | solution.py:276
  59.5 0.9 copy-start
  60.5 33.5 %all-to-all-start.2 = ((bf16[8,112,512]{2,1,0:T(8,128)(2,1)}), bf16[8,112,512]{2,1,0:T(8,128)(2,1)S(1)}, u32[]{:S(2)}, u32[]{:S(2)}) async-start(bf16[8,112,512]{2,1,0:T(8,128)(2,1)} %copy-done), calls=%async_computation.2 | async-start | bytes 1835008 | tf_op jit(solution)/shard_map/all_to_all | solution.py:288
  69.8 17.2 %collective-permute-start.1 = (bf16[7,16,512]{2,1,0:T(8,128)(2,1)S(1)}, bf16[7,16,512]{2,1,0:T(8,128)(2,1)S(1)}, u32[]{:S(2)}, u32[]{:S(2)}) collective-permute-start(bf16[7,16,512]{2,1,0:T(8,128)(2,1)S(1)} %get-tuple-element.52), channel_id=1, source_target_pairs={{0,8},{4,12},{8,16},{12,20},{16,24},{20,28},{24,0},{28,4},{1,9},{5... | collective-permute-start | bytes 344072 | tf_op jit(solution)/shard_map/ppermute | solution.py:38
  75.6 11.4 %collective-permute-start.2 = (bf16[7,16,512]{2,1,0:T(8,128)(2,1)S(1)}, bf16[7,16,512]{2,1,0:T(8,128)(2,1)S(1)}, u32[]{:S(2)}, u32[]{:S(2)}) collective-permute-start(bf16[7,16,512]{2,1,0:T(8,128)(2,1)S(1)} %get-tuple-element.53), channel_id=1, source_target_pairs={{0,16},{4,20},{8,24},{12,28},{16,0},{20,4},{24,8},{28,12},{1,17},{... | collective-permute-start | bytes 344072 | tf_op jit(solution)/shard_map/ppermute | solution.py:38
  83.6 10.3 %collective-permute-start.3 = (bf16[7,16,512]{2,1,0:T(8,128)(2,1)S(1)}, bf16[7,16,512]{2,1,0:T(8,128)(2,1)S(1)}, u32[]{:S(2)}, u32[]{:S(2)}) collective-permute-start(bf16[7,16,512]{2,1,0:T(8,128)(2,1)S(1)} %get-tuple-element.54), channel_id=1, source_target_pairs={{0,24},{4,28},{8,0},{12,4},{16,8},{20,12},{24,16},{28,20},{1,25},{... | collective-permute-start | bytes 344072 | tf_op jit(solution)/shard_map/ppermute | solution.py:38
  94.3 13.5 %collective-permute-start.4 = (bf16[8,112,512]{2,1,0:T(8,128)(2,1)S(1)}, bf16[8,112,512]{2,1,0:T(8,128)(2,1)S(1)}, u32[]{:S(2)}, u32[]{:S(2)}) collective-permute-start(bf16[8,112,512]{2,1,0:T(8,128)(2,1)S(1)} %shard_map.109), channel_id=1, source_target_pairs={{0,32},{32,0},{1,33},{33,1},{2,34},{34,2},{3,35},{35,3},{4,36},{36... | collective-permute-start | bytes 2752520 | tf_op jit(solution)/shard_map/ppermute | solution.py:42
  98.5 10.5 %collective-permute-start.7 = (bf16[7,16,512]{2,1,0:T(8,128)(2,1)S(1)}, bf16[7,16,512]{2,1,0:T(8,128)(2,1)S(1)}, u32[]{:S(2)}, u32[]{:S(2)}) collective-permute-start(bf16[7,16,512]{2,1,0:T(8,128)(2,1)S(1)} %shard_map.108.refs_0_), channel_id=1, source_target_pairs={{0,3},{1,2},{2,1},{3,0},{4,7},{5,6},{6,5},{7,4},{8,11},{9,10},{10,... | collective-permute-start | bytes 344072 | tf_op jit(solution)/shard_map/ppermute | solution.py:46
  100.8 13.4 %collective-permute-start.6 = (bf16[7,16,512]{2,1,0:T(8,128)(2,1)S(1)}, bf16[7,16,512]{2,1,0:T(8,128)(2,1)S(1)}, u32[]{:S(2)}, u32[]{:S(2)}) collective-permute-start(bf16[7,16,512]{2,1,0:T(8,128)(2,1)S(1)} %shard_map.108.refs_0_), channel_id=1, source_target_pairs={{0,2},{1,3},{2,0},{3,1},{4,6},{5,7},{6,4},{7,5},{8,10},{9,11},{10,... | collective-permute-start | bytes 344072 | tf_op jit(solution)/shard_map/ppermute | solution.py:46
  105.3 8.9 %collective-permute-start.5 = (bf16[7,16,512]{2,1,0:T(8,128)(2,1)S(1)}, bf16[7,16,512]{2,1,0:T(8,128)(2,1)S(1)}, u32[]{:S(2)}, u32[]{:S(2)}) collective-permute-start(bf16[7,16,512]{2,1,0:T(8,128)(2,1)S(1)} %shard_map.108.refs_0_), channel_id=1, source_target_pairs={{0,1},{1,0},{2,3},{3,2},{4,5},{5,4},{6,7},{7,6},{8,9},{9,8},{10,11... | collective-permute-start | bytes 344072 | tf_op jit(solution)/shard_map/ppermute | solution.py:46
  109.0 14.0 %copy-start.3 = (s32[1,7]{1,0:T(1,128)S(1)}, s32[1,7]{1,0:T(1,128)}, u32[]{:S(2)}) copy-start(s32[1,7]{1,0:T(1,128)} %owners.1) | copy-start | bytes 88
  114.2 30.7 %all-to-all-start.3 = ((bf16[32,112,128]{2,1,0:T(8,128)(2,1)}), bf16[32,112,128]{2,1,0:T(8,128)(2,1)S(1)}, u32[]{:S(2)}, u32[]{:S(2)}) async-start(bf16[32,112,128]{2,1,0:T(8,128)(2,1)} %shard_map.110), calls=%async_computation.3 | async-start | bytes 1835008 | tf_op jit(solution)/shard_map/all_to_all | solution.py:298
  122.9 31.4 %copy-start.4 = (bf16[1,1,512,512]{3,2,1,0:T(8,128)(2,1)S(1)}, bf16[1,1,512,512]{3,2,1,0:T(8,128)(2,1)}, u32[]{:S(2)}) copy-start(bf16[1,1,512,512]{3,2,1,0:T(8,128)(2,1)} %param.12) | copy-start | bytes 1572868
  122.9 31.4 %copy-start.5 = (bf16[1,1,512,512]{3,2,1,0:T(8,128)(2,1)S(1)}, bf16[1,1,512,512]{3,2,1,0:T(8,128)(2,1)}, u32[]{:S(2)}) copy-start(bf16[1,1,512,512]{3,2,1,0:T(8,128)(2,1)} %param.13) | copy-start | bytes 1572868
  124.1 8.3 %collective-permute-start.8 = (bf16[4,64,512]{2,1,0:T(8,128)(2,1)S(1)}, bf16[4,64,512]{2,1,0:T(8,128)(2,1)S(1)}, u32[]{:S(2)}, u32[]{:S(2)}) collective-permute-start(bf16[4,64,512]{2,1,0:T(8,128)(2,1)S(1)} %get-tuple-element.63), channel_id=1, source_target_pairs={{0,4},{4,0},{8,12},{12,8},{16,20},{20,16},{24,28},{28,24},{1,5},{5... | collective-permute-start | bytes 786440 | tf_op jit(solution)/shard_map/ppermute | solution.py:308
  132.5 13.6 %collective-permute-start.9 = (bf16[2,64,512]{2,1,0:T(8,128)(2,1)S(1)}, bf16[2,64,512]{2,1,0:T(8,128)(2,1)S(1)}, u32[]{:S(2)}, u32[]{:S(2)}) collective-permute-start(bf16[2,64,512]{2,1,0:T(8,128)(2,1)S(1)} %get-tuple-element.65), channel_id=1, source_target_pairs={{0,8},{4,12},{8,16},{12,20},{16,24},{20,28},{24,0},{28,4},{1,9},{5... | collective-permute-start | bytes 393224 | tf_op jit(solution)/shard_map/ppermute | solution.py:38
  135.3 13.9 %collective-permute-start.10 = (bf16[2,64,512]{2,1,0:T(8,128)(2,1)S(1)}, bf16[2,64,512]{2,1,0:T(8,128)(2,1)S(1)}, u32[]{:S(2)}, u32[]{:S(2)}) collective-permute-start(bf16[2,64,512]{2,1,0:T(8,128)(2,1)S(1)} %get-tuple-element.66), channel_id=1, source_target_pairs={{0,16},{4,20},{8,24},{12,28},{16,0},{20,4},{24,8},{28,12},{1,17},{... | collective-permute-start | bytes 393224 | tf_op jit(solution)/shard_map/ppermute | solution.py:38
  141.5 12.9 %collective-permute-start.11 = (bf16[2,64,512]{2,1,0:T(8,128)(2,1)S(1)}, bf16[2,64,512]{2,1,0:T(8,128)(2,1)S(1)}, u32[]{:S(2)}, u32[]{:S(2)}) collective-permute-start(bf16[2,64,512]{2,1,0:T(8,128)(2,1)S(1)} %get-tuple-element.67), channel_id=1, source_target_pairs={{0,24},{4,28},{8,0},{12,4},{16,8},{20,12},{24,16},{28,20},{1,25},{... | collective-permute-start | bytes 393224 | tf_op jit(solution)/shard_map/ppermute | solution.py:38
